TPU v7x, 128 devices: a whole 4x4x4 slice. The times are simulated.
128 devices in a mesh: section: 2 (over y_lo), rep: 8 (over y_hi, x), shard: 8 (over z, core).
Axes of the slice: x: 4, y: 4 (y_hi: 2, y_lo: 2; y = y_hi * 2 + y_lo), z: 4, core: 2. Of those that a mesh axis runs over, the one named last changes fastest.
Arguments:
- inputs: bfloat16 [2, 8, 1024, 768], P(None, 'rep', 'shard'), may hold values from -6 to 6
- cotangent: bfloat16 [2, 8, 1024, 768], P(None, 'rep', 'shard'), may hold values from -6 to 6
- w_qkv: bfloat16 [2, 768, 2304], P('section', 'shard'), may hold values from -0.21875 to 0.21875
- w_attn_out: bfloat16 [2, 768, 768], P('section', 'shard'), may hold values from -2.5 to 2.5
- gain_attn: bfloat16 [2, 768], P('section', 'shard'), may hold values from 0.5 to 1.5
- gain_ffn: bfloat16 [2, 768], P('section', 'shard'), may hold values from 0.5 to 1.5
- rel_bias: bfloat16 [2, 32, 12], P('section', 'shard'), may hold values from -4 to 4
- w_in: bfloat16 [2, 64, 768, 3072], P('section', ('rep', 'shard')), may hold values from -0.21875 to 0.21875
- w_out: bfloat16 [2, 64, 3072, 768], P('section', ('rep', 'shard')), may hold values from -0.109375 to 0.109375
- routes: int32 [2, 2, 8, 1024, 2], P('section', None, 'rep', 'shard'), may hold values from 0 to 63, all different within a row; in each aligned block of 128 rows (0 to 127, 128 to 255, ..., all dimensions but the last counted through in order) at most 5 rows name the same one
- gates: float32 [2, 2, 8, 1024, 2], P('section', None, 'rep', 'shard'), may hold values from 0.25 to 0.75
Outputs:
- section_out: bfloat16 [2, 2, 8, 1024, 768], P('section', None, 'rep', 'shard')
- section_in_grad: bfloat16 [2, 2, 8, 1024, 768], P('section', None, 'rep', 'shard')
- grad_w_qkv: float32 [2, 768, 2304], P('section', 'shard')
- grad_w_attn_out: float32 [2, 768, 768], P('section', 'shard')
- grad_gain_attn: float32 [2, 768], P('section', 'shard')
- grad_gain_ffn: float32 [2, 768], P('section', 'shard')
- grad_rel_bias: float32 [2, 32, 12], P('section', 'shard')
- grad_w_in: float32 [2, 64, 768, 3072], P('section', ('rep', 'shard'))
- grad_w_out: float32 [2, 64, 3072, 768], P('section', ('rep', 'shard'))
Inputs may be any that keep to these rules, and one draw needn't show every extreme that they name: `routes`: each token names two different experts. Within each aligned block of 128 tokens (one device's positions of one sequence) no expert is named more than 5 times, and in every draw some expert is named exactly 5 times in some block.
All inputs are finite; a program needn't handle non-finite values.
Results may differ from a plain program's by a relative error of at most 0.025.
Values may be sent and summed in bfloat16 or wider, within the bound.
No kernel may reach another device: no remote copies, remote signals or barrier semaphores. Data moves between devices by JAX's collectives and lax.ppermute only.
A program may use at most 320 MiB of HBM per device.

v0:
```python
from functools import partial

import jax
import jax.numpy as jnp
from jax import lax
from jax.sharding import PartitionSpec as P

H = 12
HD = 64
SEQ_LEN = 1024
BLOCK = 256
RELB = 32


NORM_EPSILON = 1e-05
MASKED = -1e30
HIGHEST_PREC = lax.Precision.HIGHEST


def from_behind(value, axis, steps):
    count = lax.axis_size(axis)
    initial, last = (max(0, -steps), min(count, count - steps))
    return lax.ppermute(value, axis, [(source, source + steps) for source in range(initial, last)])


def norm_forward(hidden, gain_vec):
    scaling = lax.rsqrt(jnp.mean(hidden * hidden, axis=-1, keepdims=True) + NORM_EPSILON)
    return (hidden * scaling * gain_vec, scaling)


def norm_backward(hidden, scaling, gain_vec, grad_in):
    gain_grad = jnp.sum(grad_in * hidden * scaling, axis=0)
    weighted = grad_in * gain_vec
    inner = jnp.mean(weighted * hidden, axis=-1, keepdims=True)
    return (weighted * scaling - hidden * scaling * scaling * scaling * inner, gain_grad)


def slot_tables(route_block, gate_block, experts, capacity):
    token_count = route_block.shape[0]
    flat_routes = route_block.reshape(-1)
    onehot = (flat_routes[:, None] == jnp.arange(experts, dtype=jnp.int32)[None, :]).astype(
        jnp.int32
    )
    slot_rank = jnp.sum((jnp.cumsum(onehot, axis=0) - onehot) * onehot, axis=1)
    slot_ids = flat_routes * capacity + slot_rank
    slot_owner = (
        jnp.full((experts * capacity,), token_count, jnp.int32)
        .at[slot_ids]
        .set(jnp.arange(2 * token_count, dtype=jnp.int32) // 2)
    )
    slot_gate = (
        jnp.zeros((experts * capacity,), jnp.float32).at[slot_ids].set(gate_block.reshape(-1))
    )
    return (slot_ids.reshape(token_count, 2), slot_owner, slot_gate)


def attention_weights(projected, keyval, bias_full, allowed):
    query_count = projected.shape[0]
    key_count = keyval.shape[0]
    queries = projected[:, : H * HD].reshape(query_count, H, HD)
    key_part = keyval[:, : H * HD].reshape(key_count, H, HD)
    logits = jnp.einsum(
        "qhd,khd->hqk", queries, key_part, preferred_element_type=jnp.float32
    ) * HD ** (-0.5)
    logits = jnp.where(allowed[None], logits + bias_full, MASKED)
    row_max = jnp.max(logits, axis=-1, keepdims=True)
    exp_terms = jnp.exp(logits - row_max)
    row_total = jnp.sum(exp_terms, axis=-1, keepdims=True)
    log_total = (row_max + jnp.log(row_total))[..., 0]
    return (exp_terms / row_total, log_total)


def context_of(soft_weights, keyval):
    key_count = keyval.shape[0]
    value_part = keyval[:, H * HD :].reshape(key_count, H, HD)
    mixed_values = jnp.einsum(
        "hqk,khd->qhd",
        soft_weights.astype(jnp.bfloat16),
        value_part,
        preferred_element_type=jnp.float32,
    )
    return mixed_values.reshape(soft_weights.shape[1], H * HD).astype(jnp.bfloat16)


def score_grads(soft_weights, projected, keyval, d_context):
    query_count = projected.shape[0]
    key_count = keyval.shape[0]
    key_part = keyval[:, : H * HD].reshape(key_count, H, HD)
    value_part = keyval[:, H * HD :].reshape(key_count, H, HD)
    d_heads = d_context.reshape(query_count, H, HD)
    d_weights = jnp.einsum("qhd,khd->hqk", d_heads, value_part, preferred_element_type=jnp.float32)
    row_delta = jnp.sum(soft_weights * d_weights, axis=-1, keepdims=True)
    d_scores = soft_weights * (d_weights - row_delta)
    d_query = jnp.einsum(
        "hqk,khd->qhd", d_scores.astype(jnp.bfloat16), key_part, preferred_element_type=jnp.float32
    ) * HD ** (-0.5)
    return (d_query.reshape(query_count, H * HD), d_scores, row_delta[..., 0])


def key_grads_from_scores(soft_weights, d_scores, projected, d_context):
    query_count = projected.shape[0]
    queries = projected[:, : H * HD].reshape(query_count, H, HD)
    d_heads = d_context.reshape(query_count, H, HD)
    d_key = jnp.einsum(
        "hqk,qhd->khd", d_scores.astype(jnp.bfloat16), queries, preferred_element_type=jnp.float32
    ) * HD ** (-0.5)
    d_value = jnp.einsum(
        "hqk,qhd->khd",
        soft_weights.astype(jnp.bfloat16),
        d_heads,
        preferred_element_type=jnp.float32,
    )
    key_count = d_key.shape[0]
    return jnp.concatenate(
        [d_key.reshape(key_count, H * HD), d_value.reshape(key_count, H * HD)], axis=1
    )


def per_device(
    inputs, cotangent, w_qkv, w_attn_out, gain_attn, gain_ffn, rel_bias, w_in, w_out, routes, gates
):
    section_index = lax.axis_index("section")
    shard_index = lax.axis_index("shard")
    micro_count = inputs.shape[0]
    token_count = inputs.shape[2]
    model_width = inputs.shape[3]
    experts = lax.axis_size("rep") * lax.axis_size("shard")
    capacity = max(2, 5 * token_count // (2 * experts))
    qkv_full, attn_full, gain_a_full, gain_f_full, bias_table = (
        lax.all_gather(w_qkv, "shard", axis=1, tiled=True),
        lax.all_gather(w_attn_out, "shard", axis=1, tiled=True),
        lax.all_gather(gain_attn, "shard", axis=1, tiled=True),
        lax.all_gather(gain_ffn, "shard", axis=1, tiled=True),
        lax.all_gather(rel_bias, "shard", axis=1, tiled=True),
    )
    qkv_weight = qkv_full[0]
    attn_weight = attn_full[0]
    gain_a = gain_a_full[0].astype(jnp.float32)
    gain_f = gain_f_full[0].astype(jnp.float32)
    bias_rows = bias_table[0].astype(jnp.float32)
    first_proj = w_in[0, 0]
    second_proj = w_out[0, 0]
    places = shard_index * token_count + jnp.arange(token_count, dtype=jnp.int32)
    key_places = jnp.arange(SEQ_LEN, dtype=jnp.int32)
    distance = places[:, None] - key_places[None, :]
    bucket = jnp.clip((distance + BLOCK) * RELB // (SEQ_LEN + BLOCK), 0, RELB - 1)
    allowed = key_places[None, :] // BLOCK <= places[:, None] // BLOCK
    bucket_onehot = (bucket[:, :, None] == jnp.arange(RELB, dtype=jnp.int32)[None, None, :]).astype(
        jnp.float32
    )
    bias_full = jnp.einsum("qkb,bh->hqk", bucket_onehot, bias_rows, precision=HIGHEST_PREC)

    def front_part(hidden):
        normed, scaling = norm_forward(hidden, gain_a)
        normed_low = normed.astype(jnp.bfloat16)
        projected = jnp.dot(normed_low, qkv_weight, preferred_element_type=jnp.float32).astype(
            jnp.bfloat16
        )
        return (normed_low, scaling, projected)

    def middle_part(hidden, context):
        middle = hidden + jnp.dot(context, attn_weight, preferred_element_type=jnp.float32)
        normed, scaling = norm_forward(middle, gain_f)
        return (middle, scaling, normed.astype(jnp.bfloat16))

    def route_tables(micro_index):
        route_block = lax.dynamic_index_in_dim(routes[0], micro_index, 0, keepdims=False)[0]
        gate_block = lax.dynamic_index_in_dim(gates[0], micro_index, 0, keepdims=False)[0]
        slot_ids, slot_owner, slot_gate = slot_tables(route_block, gate_block, experts, capacity)
        return (slot_ids, slot_owner, gate_block, slot_gate)

    def dispatch_rows(normed_low, slot_owner):
        padded = jnp.concatenate([normed_low, jnp.zeros((1, model_width), jnp.bfloat16)], axis=0)
        return padded[slot_owner].reshape(experts, capacity, model_width)

    passed = jnp.zeros((token_count, model_width), jnp.bfloat16)
    layer_in, layer_out, kept_keys, kept_rows = ([], [], [], [])
    for step_index in range(micro_count + 1):
        micro_index = jnp.clip(step_index - section_index, 0, micro_count - 1)
        hidden = jnp.where(
            section_index == 0, inputs[min(step_index, micro_count - 1), 0], passed
        ).astype(jnp.float32)
        normed_low, scale_a, projected = front_part(hidden)
        keyval = lax.all_gather(projected[:, model_width:], "shard", axis=0, tiled=True)
        soft_weights, log_total = attention_weights(projected, keyval, bias_full, allowed)
        context = context_of(soft_weights, keyval)
        middle, scale_f, normed_ffn = middle_part(hidden, context)
        slot_ids, slot_owner, gate_block, slot_gate = route_tables(micro_index)
        arrived = lax.all_to_all(
            dispatch_rows(normed_ffn, slot_owner),
            ("rep", "shard"),
            split_axis=0,
            concat_axis=0,
            tiled=True,
        )
        expert_flat_rows = arrived.reshape(-1, model_width)
        expert_up_proj = jnp.dot(expert_flat_rows, first_proj, preferred_element_type=jnp.float32)
        expert_activated = jax.nn.gelu(expert_up_proj, approximate=False).astype(jnp.bfloat16)
        made = (
            jnp.dot(expert_activated, second_proj, preferred_element_type=jnp.float32)
            .astype(jnp.bfloat16)
            .reshape(arrived.shape)
        )
        returned = lax.all_to_all(made, ("rep", "shard"), split_axis=0, concat_axis=0, tiled=True)
        returned, arrived = (returned, arrived)
        returned_flat = returned.reshape(-1, model_width)
        expert_sum = gate_block[:, 0:1] * returned_flat[slot_ids[:, 0]].astype(
            jnp.float32
        ) + gate_block[:, 1:2] * returned_flat[slot_ids[:, 1]].astype(jnp.float32)
        finished = (middle + expert_sum).astype(jnp.bfloat16)
        layer_in.append(hidden.astype(jnp.bfloat16))
        layer_out.append(finished)
        kept_keys.append(keyval)
        kept_rows.append(arrived)
        if step_index < micro_count:
            passed = from_behind(finished, "section", 1)

    def pick_forward(items, batch_index):
        return jnp.where(section_index == 0, items[batch_index], items[batch_index + 1])

    saved_inputs = jnp.stack(
        [pick_forward(layer_in, batch_index) for batch_index in range(micro_count)]
    )
    section_out = jnp.stack(
        [pick_forward(layer_out, batch_index) for batch_index in range(micro_count)]
    )
    d_qkv = jnp.zeros((model_width, 3 * model_width), jnp.float32)
    d_attn_out = jnp.zeros((model_width, model_width), jnp.float32)
    d_gain_a = jnp.zeros((model_width,), jnp.float32)
    d_gain_f = jnp.zeros((model_width,), jnp.float32)
    d_score_sum = jnp.zeros(bias_full.shape, jnp.float32)
    d_first = jnp.zeros(first_proj.shape, jnp.float32)
    d_second = jnp.zeros(second_proj.shape, jnp.float32)
    received_grad = jnp.zeros((token_count, model_width), jnp.bfloat16)
    grads_in = []
    for step_index in range(micro_count + 1):
        batch_number = step_index - 1 + section_index
        micro_index = jnp.clip(batch_number, 0, micro_count - 1)
        is_valid = (batch_number >= 0) & (batch_number < micro_count)
        incoming = jnp.where(
            section_index == 1, cotangent[min(step_index, micro_count - 1), 0], received_grad
        ).astype(jnp.float32)
        incoming = jnp.where(is_valid, incoming, 0.0)
        hidden = lax.dynamic_index_in_dim(saved_inputs, micro_index, 0, keepdims=False).astype(
            jnp.float32
        )
        normed_low, scale_a, projected = front_part(hidden)
        keyval = lax.all_gather(projected[:, model_width:], "shard", axis=0, tiled=True)
        soft_weights, log_total = attention_weights(projected, keyval, bias_full, allowed)
        context = context_of(soft_weights, keyval)
        middle, scale_f, normed_ffn = middle_part(hidden, context)
        slot_ids, slot_owner, gate_block, slot_gate = route_tables(micro_index)
        padded_grad = jnp.concatenate([incoming, jnp.zeros((1, model_width), jnp.float32)], axis=0)
        grad_rows = (
            (slot_gate[:, None] * padded_grad[slot_owner])
            .astype(jnp.bfloat16)
            .reshape(experts, capacity, model_width)
        )
        arrived, grad_arrived = (
            lax.all_to_all(
                dispatch_rows(normed_ffn, slot_owner),
                ("rep", "shard"),
                split_axis=0,
                concat_axis=0,
                tiled=True,
            ),
            lax.all_to_all(grad_rows, ("rep", "shard"), split_axis=0, concat_axis=0, tiled=True),
        )
        flat_rows = arrived.reshape(-1, model_width)
        grad_flat = grad_arrived.reshape(-1, model_width)
        up_proj = jnp.dot(flat_rows, first_proj, preferred_element_type=jnp.float32)
        activated, gelu_pull = jax.vjp(partial(jax.nn.gelu, approximate=False), up_proj)
        d_second = d_second + jnp.einsum(
            "rf,rd->fd",
            activated.astype(jnp.bfloat16),
            grad_flat,
            preferred_element_type=jnp.float32,
        )
        (d_up,) = gelu_pull(
            jnp.einsum("rd,fd->rf", grad_flat, second_proj, preferred_element_type=jnp.float32)
        )
        d_up_low = d_up.astype(jnp.bfloat16)
        d_first = d_first + jnp.einsum(
            "rd,rf->df", flat_rows, d_up_low, preferred_element_type=jnp.float32
        )
        d_sent = jnp.einsum(
            "rf,df->rd", d_up_low, first_proj, preferred_element_type=jnp.float32
        ).astype(jnp.bfloat16)
        d_back = lax.all_to_all(
            d_sent.reshape(experts, capacity, model_width),
            ("rep", "shard"),
            split_axis=0,
            concat_axis=0,
            tiled=True,
        ).reshape(-1, model_width)
        d_normed_ffn = d_back[slot_ids[:, 0]].astype(jnp.float32) + d_back[slot_ids[:, 1]].astype(
            jnp.float32
        )
        d_middle_norm, gain_f_part = norm_backward(middle, scale_f, gain_f, d_normed_ffn)
        d_gain_f = d_gain_f + gain_f_part
        d_middle = incoming + d_middle_norm
        d_branch = d_middle.astype(jnp.bfloat16)
        d_attn_out = d_attn_out + jnp.einsum(
            "sd,se->de", context, d_branch, preferred_element_type=jnp.float32
        )
        d_context = jnp.einsum(
            "se,de->sd", d_branch, attn_weight, preferred_element_type=jnp.float32
        ).astype(jnp.bfloat16)
        d_query, d_scores, row_delta = score_grads(soft_weights, projected, keyval, d_context)
        d_score_sum = d_score_sum + d_scores
        d_keyval_part = key_grads_from_scores(soft_weights, d_scores, projected, d_context)
        d_keyval = lax.psum_scatter(
            d_keyval_part.astype(jnp.bfloat16), "shard", scatter_dimension=0, tiled=True
        ).astype(jnp.float32)
        d_projected = jnp.concatenate([d_query, d_keyval], axis=1).astype(jnp.bfloat16)
        d_qkv = d_qkv + jnp.einsum(
            "sd,se->de", normed_low, d_projected, preferred_element_type=jnp.float32
        )
        d_normed_attn = jnp.einsum(
            "se,de->sd", d_projected, qkv_weight, preferred_element_type=jnp.float32
        )
        d_hidden_norm, gain_a_part = norm_backward(hidden, scale_a, gain_a, d_normed_attn)
        d_gain_a = d_gain_a + gain_a_part
        d_hidden = (d_middle + d_hidden_norm).astype(jnp.bfloat16)
        grads_in.append(d_hidden)
        if step_index < micro_count:
            received_grad = from_behind(d_hidden, "section", -1)

    def pick_backward(items, batch_index):
        return jnp.where(section_index == 0, items[batch_index + 1], items[batch_index])

    section_in_grad = jnp.stack(
        [pick_backward(grads_in, batch_index) for batch_index in range(micro_count)]
    )
    d_rel = jnp.einsum("qkb,hqk->bh", bucket_onehot, d_score_sum, precision=HIGHEST_PREC)
    summed = (
        lax.psum_scatter(
            d_qkv[None].astype(jnp.bfloat16), "shard", scatter_dimension=1, tiled=True
        ).astype(jnp.float32),
        lax.psum_scatter(
            d_attn_out[None].astype(jnp.bfloat16), "shard", scatter_dimension=1, tiled=True
        ).astype(jnp.float32),
        lax.psum_scatter(
            d_gain_a[None].astype(jnp.bfloat16), "shard", scatter_dimension=1, tiled=True
        ).astype(jnp.float32),
        lax.psum_scatter(
            d_gain_f[None].astype(jnp.bfloat16), "shard", scatter_dimension=1, tiled=True
        ).astype(jnp.float32),
        lax.psum_scatter(
            d_rel[None].astype(jnp.bfloat16), "shard", scatter_dimension=1, tiled=True
        ).astype(jnp.float32),
    )
    grad_qkv, grad_attn, grad_gain_a, grad_gain_f, grad_bias = (
        lax.psum(summed[0].astype(jnp.bfloat16), "rep").astype(jnp.float32),
        lax.psum(summed[1].astype(jnp.bfloat16), "rep").astype(jnp.float32),
        lax.psum(summed[2].astype(jnp.bfloat16), "rep").astype(jnp.float32),
        lax.psum(summed[3].astype(jnp.bfloat16), "rep").astype(jnp.float32),
        lax.psum(summed[4].astype(jnp.bfloat16), "rep").astype(jnp.float32),
    )
    out_shape = (1, micro_count, 1, token_count, model_width)
    return (
        section_out.reshape(out_shape),
        section_in_grad.reshape(out_shape),
        grad_qkv,
        grad_attn,
        grad_gain_a,
        grad_gain_f,
        grad_bias,
        d_first[None, None],
        d_second[None, None],
    )


def solution(mesh):
    placed = (
        P(None, "rep", "shard", None),
        P(None, "rep", "shard", None),
        P("section", "shard", None),
        P("section", "shard", None),
        P("section", "shard"),
        P("section", "shard"),
        P("section", "shard", None),
        P("section", ("rep", "shard"), None, None),
        P("section", ("rep", "shard"), None, None),
        P("section", None, "rep", "shard", None),
        P("section", None, "rep", "shard", None),
    )
    return jax.shard_map(
        per_device,
        mesh=mesh,
        in_specs=placed,
        out_specs=(
            P("section", None, "rep", "shard", None),
            P("section", None, "rep", "shard", None),
            P("section", "shard", None),
            P("section", "shard", None),
            P("section", "shard"),
            P("section", "shard"),
            P("section", "shard", None),
            P("section", ("rep", "shard"), None, None),
            P("section", ("rep", "shard"), None, None),
        ),
        check_vma=False,
    )
```

profile of v0, /device:TPU:0, one launch (start us, length us, event | category | flops | bytes accessed | tf_op | source)
XLA Modules:
  0.0 1212.0 jit_solution(17386365333488640599)
XLA Ops:
  11.7 16.0 %all-reduce.12 = (bf16[768]{0:T(1024)(128)(2,1)S(1)}, bf16[768]{0:T(1024)(128)(2,1)S(1)}) all-reduce(bf16[768]{0:T(1024)(128)(2,1)S(1)} %dynamic-update-slice, bf16[768]{0:T(1024)(128)(2,1)S(1)} %dynamic-update-slice.1), channel_id=1, replica_groups=mesh['section'=2,'rep'=8,'shard'=8] {'shard'}, use_global_device_ids=true, to_apply=%add.9 | all-reduce | flops 1536 | bytes 6144
  28.7 13.1 %all-gather.9.cloned.1.call-done = bf16[1,768,2304]{2,1,0:T(8,128)(2,1)} async-done(((bf16[1,96,2304]{2,1,0:T(8,128)(2,1)}), bf16[1,768,2304]{2,1,0:T(8,128)(2,1)}) %all-gather.9.cloned.1.call-update) | async-done | bytes 3538960 | tf_op jit(solution)/shard_map/all_gather | solution.py:130
  48.2 11.2 all_gather.36
  61.6 6.0 fusion.7
  70.0 8.3 copy.152
  92.2 7.7 fusion.304
  105.8 9.9 all-to-all-start
  116.6 14.8 %all-to-all-done = bf16[64,5,768]{2,1,0:T(8,128)(2,1)S(1)} async-done(((bf16[64,5,768]{2,1,0:T(8,128)(2,1)}), bf16[64,5,768]{2,1,0:T(8,128)(2,1)S(1)}, u32[]{:S(2)}, u32[]{:S(2)}) %all-to-all-start) | async-done | bytes 491552 | tf_op jit(solution)/shard_map/all_to_all | solution.py:189
  131.6 14.6 %fusion.248 = bf16[320,768]{1,0:T(8,128)(2,1)S(1)} fusion(bf16[1,1,3072,768]{3,2,1,0:T(8,128)(2,1)} %param.19, bf16[320,768]{1,0:T(8,128)(2,1)S(1)} %reshape.997, bf16[1,1,768,3072]{3,2,1,0:T(8,128)(2,1)} %param.18), kind=kOutput, calls=%fused_computation.359 | convolution fusion | flops 3084042240 | bytes 10420224 | tf_op jit(solution)/shard_map/dot_general | solution.py:200
  147.3 5.6 all-to-all-start.1
  156.1 12.2 %all-to-all-done.1 = bf16[64,5,768]{2,1,0:T(8,128)(2,1)} async-done(((bf16[64,5,768]{2,1,0:T(8,128)(2,1)}), bf16[64,5,768]{2,1,0:T(8,128)(2,1)}, u32[]{:S(2)}, u32[]{:S(2)}) %all-to-all-start.1) | async-done | bytes 491552 | tf_op jit(solution)/shard_map/all_to_all | solution.py:204
  194.4 20.6 %all-gather.15.cloned.1.call-done = bf16[1024,1536]{1,0:T(8,128)(2,1)} async-done(((bf16[128,1536]{1,0:T(8,128)(2,1)}), bf16[1024,1536]{1,0:T(8,128)(2,1)}) %all-gather.15.cloned.1.call-update) | async-done | bytes 3145744 | tf_op jit(solution)/shard_map/all_gather | solution.py:184
  233.4 8.7 fusion.303
  251.5 9.1 all-to-all-start.2
  261.4 14.7 %all-to-all-done.2 = bf16[64,5,768]{2,1,0:T(8,128)(2,1)} async-done(((bf16[64,5,768]{2,1,0:T(8,128)(2,1)}), bf16[64,5,768]{2,1,0:T(8,128)(2,1)}, u32[]{:S(2)}, u32[]{:S(2)}) %all-to-all-start.2) | async-done | bytes 491552 | tf_op jit(solution)/shard_map/all_to_all | solution.py:189
  278.2 15.5 %fusion.255 = bf16[320,768]{1,0:T(8,128)(2,1)} fusion(bf16[1,1,3072,768]{3,2,1,0:T(8,128)(2,1)} %param.19, bf16[320,768]{1,0:T(8,128)(2,1)} %reshape.1005, bf16[1,1,768,3072]{3,2,1,0:T(8,128)(2,1)} %param.18), kind=kOutput, calls=%fused_computation.360 | convolution fusion | flops 3084042240 | bytes 10420224 | tf_op jit(solution)/shard_map/dot_general | solution.py:200
  295.7 5.8 all-to-all-start.3
  304.1 13.0 %all-to-all-done.3 = bf16[64,5,768]{2,1,0:T(8,128)(2,1)} async-done(((bf16[64,5,768]{2,1,0:T(8,128)(2,1)}), bf16[64,5,768]{2,1,0:T(8,128)(2,1)}, u32[]{:S(2)}, u32[]{:S(2)}) %all-to-all-start.3) | async-done | bytes 491552 | tf_op jit(solution)/shard_map/all_to_all | solution.py:204
  382.8 5.6 all-to-all-start.7
  394.8 8.5 all-gather.23.cloned.1.call-done
  419.3 8.3 fusion.296
  438.1 7.8 fusion.290
  463.2 8.1 fusion.293
  476.0 10.8 all-to-all-start.6
  488.1 14.2 %all-to-all-done.6 = bf16[64,5,768]{2,1,0:T(8,128)(2,1)S(1)} async-done(((bf16[64,5,768]{2,1,0:T(8,128)(2,1)}), bf16[64,5,768]{2,1,0:T(8,128)(2,1)S(1)}, u32[]{:S(2)}, u32[]{:S(2)}) %all-to-all-start.6) | async-done | bytes 491552 | tf_op jit(solution)/shard_map/all_to_all | solution.py:260
  503.3 11.4 fusion.56
  514.8 7.8 add_convert_fusion.3
  535.0 15.2 %all-to-all-done.8 = bf16[64,5,768]{2,1,0:T(8,128)(2,1)S(1)} async-done(((bf16[64,5,768]{2,1,0:T(8,128)(2,1)}), bf16[64,5,768]{2,1,0:T(8,128)(2,1)S(1)}, u32[]{:S(2)}, u32[]{:S(2)}) %all-to-all-start.8) | async-done | bytes 491552 | tf_op jit(solution)/shard_map/all_to_all | solution.py:289
  553.8 9.0 convolution_convert_fusion.8
  587.5 5.9 all-to-all-start.9
  597.8 16.6 %reduce-scatter.22.cloned.1.call-done = bf16[128,1536]{1,0:T(8,128)(2,1)} async-done(((bf16[1024,1536]{1,0:T(8,128)(2,1)}), bf16[128,1536]{1,0:T(8,128)(2,1)}) %reduce-scatter.22.cloned.1.call-update) | async-done | bytes 393232
  633.5 10.4 all-to-all-start.10
  643.9 12.8 %fusion.57 = (f32[320,3072]{1,0:T(8,128)}, f32[320,3072]{1,0:T(8,128)}) fusion(bf16[320,768]{1,0:T(8,128)(2,1)S(1)} %reshape.1035, bf16[1,1,768,3072]{3,2,1,0:T(8,128)(2,1)} %param.18), kind=kOutput, calls=%fused_computation.119 | convolution fusion | flops 1570897920 | bytes 13074432 | tf_op jit(solution)/shard_map/dot_general | solution.py:271
  659.7 7.4 add_convert_fusion.2
  673.7 7.9 all-to-all-start.11
  682.1 14.9 %all-to-all-done.11 = bf16[64,5,768]{2,1,0:T(8,128)(2,1)} async-done(((bf16[64,5,768]{2,1,0:T(8,128)(2,1)}), bf16[64,5,768]{2,1,0:T(8,128)(2,1)}, u32[]{:S(2)}, u32[]{:S(2)}) %all-to-all-start.11) | async-done | bytes 491552 | tf_op jit(solution)/shard_map/all_to_all | solution.py:289
  701.8 8.9 convolution_convert_fusion.7
  739.7 5.7 all-to-all-start.12
  745.5 7.0 fusion.12
  754.4 9.6 reduce-scatter.24.cloned.1.call-done
  782.2 8.3 all-to-all-start.13
  790.5 8.8 fusion.302
  800.6 6.2 fusion.30
  807.1 12.3 %add_convert_fusion.1 = bf16[320,3072]{1,0:T(8,128)(2,1)S(1)} fusion(f32[320,3072]{1,0:T(8,128)} %fusion.30, bf16[320,768]{1,0:T(8,128)(2,1)S(1)} %reshape.1049, bf16[1,1,3072,768]{3,2,1,0:T(8,128)(2,1)} %param.19), kind=kOutput, calls=%fused_computation.124 | convolution fusion | flops 1580728320 | bytes 11108352 | tf_op jit(solution)/shard_map/rd,fd->rf/dot_general | solution.py:280
  825.9 10.9 all-to-all-start.14
  838.5 13.8 %all-to-all-done.14 = bf16[64,5,768]{2,1,0:T(8,128)(2,1)} async-done(((bf16[64,5,768]{2,1,0:T(8,128)(2,1)}), bf16[64,5,768]{2,1,0:T(8,128)(2,1)}, u32[]{:S(2)}, u32[]{:S(2)}) %all-to-all-start.14) | async-done | bytes 491552 | tf_op jit(solution)/shard_map/all_to_all | solution.py:289
  858.9 8.9 convolution_convert_fusion.6
  867.9 5.9 multiply_reduce_fusion
  878.4 11.1 add_add_fusion
  903.2 8.2 fusion.605
  929.6 8.1 fusion.606
  937.8 5.6 fusion.135
  950.1 8.2 fusion.46
  958.3 17.1 %add_bitcast_fusion = f32[1,1,3072,768]{3,2,1,0:T(8,128)} fusion(f32[3072,768]{1,0:T(8,128)} %fusion.134, f32[3072,768]{1,0:T(8,128)} %fusion.135, bf16[320,768]{1,0:T(8,128)(2,1)S(1)} %copy-done.117, f32[320,3072]{1,0:T(8,128)} %fusion.30), kind=kOutput, calls=%fused_computation.39 | convolution fusion | flops 1578565632 | bytes 32735232 | tf_op jit(solution)/shard_map/rf,rd->fd/dot_general | solution.py:273
  978.6 5.7 all-to-all-start.4
  984.3 10.8 add_bitcast_fusion.1
  995.1 9.0 copy.186
  1004.3 14.6 %fusion.262 = bf16[320,768]{1,0:T(8,128)(2,1)S(1)} fusion(bf16[1,1,3072,768]{3,2,1,0:T(8,128)(2,1)} %param.19, bf16[320,768]{1,0:T(8,128)(2,1)S(1)} %reshape.1013, bf16[1,1,768,3072]{3,2,1,0:T(8,128)(2,1)} %param.18), kind=kOutput, calls=%fused_computation.361 | convolution fusion | flops 3084042240 | bytes 10420224 | tf_op jit(solution)/shard_map/dot_general | solution.py:200
  1020.0 10.5 all-to-all-start.5
  1030.6 11.0 fusion.307
  1042.3 26.5 %all-reduce.11 = bf16[1,32,12]{2,0,1:T(2,128)(2,1)} all-reduce(bf16[1,32,12]{2,0,1:T(2,128)(2,1)} %copy.187), channel_id=9, replica_groups=mesh['section'=2,'rep'=8,'shard'=8] {'shard'}, use_global_device_ids=true, to_apply=%region_77.78.clone | all-reduce | flops 384 | bytes 1536
  1090.6 24.0 %reduce-scatter.28.cloned.1.call-done = bf16[96,1]{1,0:T(8,128)(2,1)} async-done(((bf16[768,1]{1,0:T(8,128)(2,1)}), bf16[96,1]{1,0:T(8,128)(2,1)}) %reduce-scatter.28.cloned.1.call-update) | async-done | bytes 208
  1115.4 24.1 %all-reduce.13 = (bf16[1,96]{1,0:T(2,128)(2,1)S(1)}, bf16[1,96]{1,0:T(2,128)(2,1)S(1)}, bf16[1,4,12]{2,0,1:T(2,128)(2,1)S(1)}) all-reduce(bf16[1,96]{1,0:T(2,128)(2,1)S(1)} %copy.201, bf16[1,96]{1,0:T(2,128)(2,1)S(1)} %copy-done.166, ...), channel_id=1, replica_groups=mesh['section'=2,'rep'=8,'shard'=8] {'rep'}, use_global_device_ids=true, to_apply=%region_71.72 | all-reduce | flops 240 | bytes 960 | tf_op jit(solution)/shard_map/psum | solution.py:356
  1141.1 60.5 %all-reduce.17.cloned.1.call-done = (bf16[1,96,2304]{2,1,0:T(8,128)(2,1)}, bf16[1,96,768]{2,1,0:T(8,128)(2,1)}) async-done(((bf16[1,96,2304]{2,1,0:T(8,128)(2,1)}, bf16[1,96,768]{2,1,0:T(8,128)(2,1)}), (bf16[1,96,2304]{2,1,0:T(8,128)(2,1)}, bf16[1,96,768]{2,1,0:T(8,128)(2,1)})) %all-reduce.17.cloned.1.call-update) | async-done | bytes 589840 | tf_op jit(solution)/shard_map/psum | solution.py:354
  (782 shorter events, 442.9 us)
Async XLA Ops:
  7.2 39.1 %copy-start.131 = (s32[1,2,1,128,2]{3,4,2,1,0:T(2,128)S(1)}, s32[1,2,1,128,2]{3,4,2,1,0:T(2,128)}, u32[]{:S(2)}) copy-start(s32[1,2,1,128,2]{3,4,2,1,0:T(2,128)} %param.20) | copy-start | bytes 6148
  7.2 41.0 %copy-start.167 = (bf16[1,4,12]{2,1,0:T(4,128)(2,1)S(1)}, bf16[1,4,12]{2,1,0:T(4,128)(2,1)}, u32[]{:S(2)}) copy-start(bf16[1,4,12]{2,1,0:T(4,128)(2,1)} %param.17) | copy-start | bytes 292
  7.2 34.7 %all-gather.9.cloned.1.call-start = ((), (), s32[]{:S(2)}) async-start(), calls=%async_computation.22 | async-start | bytes 3981312 | tf_op jit(solution)/shard_map/all_gather | solution.py:130
  7.9 71.3 %all-gather.11.cloned.1.call-start = ((), (), s32[]{:S(2)}) async-start(), calls=%async_computation.23 | async-start | bytes 3538944 | tf_op jit(solution)/shard_map/all_gather | solution.py:184
  45.5 54.5 %all-gather.13.cloned.1.call-start = ((), (), s32[]{:S(2)}) async-start(), calls=%async_computation.24 | async-start | bytes 1327104 | tf_op jit(solution)/shard_map/all_gather | solution.py:131
  47.7 20.7 %copy-start.168 = (s32[256]{0:T(256)}, s32[256]{0:T(256)S(1)}, u32[]{:S(2)}) copy-start(s32[256]{0:T(256)S(1)} %and_select_fusion) | copy-start | bytes 3076
  48.2 19.3 %copy-start.51 = (s32[128,1024]{0,1:T(8,128)}, s32[128,1024]{0,1:T(8,128)S(1)}, u32[]{:S(2)}) copy-start(s32[128,1024]{0,1:T(8,128)S(1)} %fusion.308) | copy-start | bytes 1572868
  105.8 25.5 %all-to-all-start = ((bf16[64,5,768]{2,1,0:T(8,128)(2,1)}), bf16[64,5,768]{2,1,0:T(8,128)(2,1)S(1)}, u32[]{:S(2)}, u32[]{:S(2)}) async-start(bf16[64,5,768]{2,1,0:T(8,128)(2,1)} %reshape.996), calls=%async_computation | async-start | bytes 1572864 | tf_op jit(solution)/shard_map/all_to_all | solution.py:189
  131.6 21.4 %copy-start.132 = (f32[1,2,1,128,2]{3,4,2,1,0:T(2,128)S(1)}, f32[1,2,1,128,2]{3,4,2,1,0:T(2,128)}, u32[]{:S(2)}) copy-start(f32[1,2,1,128,2]{3,4,2,1,0:T(2,128)} %param.21) | copy-start | bytes 6148
  147.3 21.1 %all-to-all-start.1 = ((bf16[64,5,768]{2,1,0:T(8,128)(2,1)}), bf16[64,5,768]{2,1,0:T(8,128)(2,1)}, u32[]{:S(2)}, u32[]{:S(2)}) async-start(bf16[64,5,768]{2,1,0:T(8,128)(2,1)} %reshape.998), calls=%async_computation.1 | async-start | bytes 1572864 | tf_op jit(solution)/shard_map/all_to_all | solution.py:204
  152.9 34.2 %copy-start = (bf16[1,768,2304]{2,1,0:T(8,128)(2,1)S(1)}, bf16[1,768,2304]{2,1,0:T(8,128)(2,1)}, u32[]{:S(2)}) copy-start(bf16[1,768,2304]{2,1,0:T(8,128)(2,1)} %all-gather.9.cloned.1.call-done) | copy-start | bytes 10616836
  152.9 62.0 %all-gather.15.cloned.1.call-start = ((), (), s32[]{:S(2)}) async-start(), calls=%async_computation.25 | async-start | bytes 3538944 | tf_op jit(solution)/shard_map/all_gather | solution.py:184
  177.3 7.4 collective-permute-start
  251.5 24.6 %all-to-all-start.2 = ((bf16[64,5,768]{2,1,0:T(8,128)(2,1)}), bf16[64,5,768]{2,1,0:T(8,128)(2,1)}, u32[]{:S(2)}, u32[]{:S(2)}) async-start(bf16[64,5,768]{2,1,0:T(8,128)(2,1)} %reshape.1004), calls=%async_computation.2 | async-start | bytes 1572864 | tf_op jit(solution)/shard_map/all_to_all | solution.py:189
  295.7 21.3 %all-to-all-start.3 = ((bf16[64,5,768]{2,1,0:T(8,128)(2,1)}), bf16[64,5,768]{2,1,0:T(8,128)(2,1)}, u32[]{:S(2)}, u32[]{:S(2)}) async-start(bf16[64,5,768]{2,1,0:T(8,128)(2,1)} %reshape.1006), calls=%async_computation.3 | async-start | bytes 1572864 | tf_op jit(solution)/shard_map/all_to_all | solution.py:204
  301.6 88.6 %all-gather.19.cloned.1.call-start = ((), (), s32[]{:S(2)}) async-start(), calls=%async_computation.27 | async-start | bytes 3538944 | tf_op jit(solution)/shard_map/all_gather | solution.py:248
  326.6 7.3 collective-permute-start.1
  341.2 62.1 %all-gather.23.cloned.1.call-start = ((), (), s32[]{:S(2)}) async-start(), calls=%async_computation.29 | async-start | bytes 3538944 | tf_op jit(solution)/shard_map/all_gather | solution.py:248
  345.8 101.2 %all-gather.21.cloned.1.call-start = ((), (), s32[]{:S(2)}) async-start(), calls=%async_computation.28 | async-start | bytes 3538944 | tf_op jit(solution)/shard_map/all_gather | solution.py:248
  382.8 93.2 %all-to-all-start.7 = ((bf16[64,5,768]{2,1,0:T(8,128)(2,1)}), bf16[64,5,768]{2,1,0:T(8,128)(2,1)}, u32[]{:S(2)}, u32[]{:S(2)}) async-start(bf16[64,5,768]{2,1,0:T(8,128)(2,1)} %multiply_convert_fusion.11), calls=%async_computation.7 | async-start | bytes 1572864 | tf_op jit(solution)/shard_map/all_to_all | solution.py:267
  389.4 20.7 %copy-start.76 = (bf16[128,768]{0,1:T(8,128)(2,1)}, bf16[128,768]{0,1:T(8,128)(2,1)S(1)}, u32[]{:S(2)}) copy-start(bf16[128,768]{0,1:T(8,128)(2,1)S(1)} %copy.180) | copy-start | bytes 589828
  394.8 34.6 %copy-start.22 = (bf16[1024,768]{0,1:T(8,128)(2,1)}, bf16[1024,768]{0,1:T(8,128)(2,1)S(1)}, u32[]{:S(2)}) copy-start(bf16[1024,768]{0,1:T(8,128)(2,1)S(1)} %copy.167) | copy-start | bytes 4718596
  438.1 128.9 %copy-start.120 = (f32[12,128]{1,0:T(8,128)}, f32[12,128]{1,0:T(8,128)S(1)}, u32[]{:S(2)}) copy-start(f32[12,128]{1,0:T(8,128)S(1)} %get-tuple-element.137) | copy-start | bytes 18436
  476.0 26.3 %all-to-all-start.6 = ((bf16[64,5,768]{2,1,0:T(8,128)(2,1)}), bf16[64,5,768]{2,1,0:T(8,128)(2,1)S(1)}, u32[]{:S(2)}, u32[]{:S(2)}) async-start(bf16[64,5,768]{2,1,0:T(8,128)(2,1)} %reshape.1021), calls=%async_computation.6 | async-start | bytes 1572864 | tf_op jit(solution)/shard_map/all_to_all | solution.py:260
  488.1 26.6 %copy-start.71 = (bf16[320,768]{1,0:T(8,128)(2,1)}, bf16[320,768]{1,0:T(8,128)(2,1)S(1)}, u32[]{:S(2)}) copy-start(bf16[320,768]{1,0:T(8,128)(2,1)S(1)} %reshape.1023) | copy-start | bytes 1474564
  529.0 23.8 %copy-start.99 = (bf16[2,1,128,768]{3,2,1,0:T(8,128)(2,1)S(1)}, bf16[2,1,128,768]{3,2,1,0:T(8,128)(2,1)}, u32[]{:S(2)}) copy-start(bf16[2,1,128,768]{3,2,1,0:T(8,128)(2,1)} %param.12) | copy-start | bytes 1179652
  529.0 21.1 %all-to-all-start.8 = ((bf16[64,5,768]{2,1,0:T(8,128)(2,1)}), bf16[64,5,768]{2,1,0:T(8,128)(2,1)S(1)}, u32[]{:S(2)}, u32[]{:S(2)}) async-start(bf16[64,5,768]{2,1,0:T(8,128)(2,1)} %reshape.1024), calls=%async_computation.8 | async-start | bytes 1572864 | tf_op jit(solution)/shard_map/all_to_all | solution.py:289
  534.6 79.8 %reduce-scatter.22.cloned.1.call-start = ((), (), s32[]{:S(2)}) async-start(), calls=%async_computation.32 | async-start | bytes 3538944
  587.5 28.8 %copy-start.1 = (bf16[1,768,2304]{2,1,0:T(8,128)(2,1)S(1)}, bf16[1,768,2304]{2,1,0:T(8,128)(2,1)}, u32[]{:S(2)}) copy-start(bf16[1,768,2304]{2,1,0:T(8,128)(2,1)} %all-gather.9.cloned.1.call-done) | copy-start | bytes 10616836
  587.5 37.8 %all-to-all-start.9 = ((bf16[64,5,768]{2,1,0:T(8,128)(2,1)}), bf16[64,5,768]{2,1,0:T(8,128)(2,1)}, u32[]{:S(2)}, u32[]{:S(2)}) async-start(bf16[64,5,768]{2,1,0:T(8,128)(2,1)} %reshape.1034), calls=%async_computation.9 | async-start | bytes 1572864 | tf_op jit(solution)/shard_map/all_to_all | solution.py:260
  593.4 137.6 %all-gather.17.cloned.1.call-start = ((), (), s32[]{:S(2)}) async-start(), calls=%async_computation.26 | async-start | bytes 3538944 | tf_op jit(solution)/shard_map/all_gather | solution.py:184
  621.1 8.2 collective-permute-start.2
  627.1 16.7 %copy-start.73 = (bf16[320,768]{1,0:T(8,128)(2,1)}, bf16[320,768]{1,0:T(8,128)(2,1)S(1)}, u32[]{:S(2)}) copy-start(bf16[320,768]{1,0:T(8,128)(2,1)S(1)} %reshape.1035) | copy-start | bytes 1474564
  633.5 26.0 %all-to-all-start.10 = ((bf16[64,5,768]{2,1,0:T(8,128)(2,1)}), bf16[64,5,768]{2,1,0:T(8,128)(2,1)S(1)}, u32[]{:S(2)}, u32[]{:S(2)}) async-start(bf16[64,5,768]{2,1,0:T(8,128)(2,1)} %multiply_convert_fusion.10), calls=%async_computation.10 | async-start | bytes 1572864 | tf_op jit(solution)/shard_map/all_to_all | solution.py:267
  668.4 13.5 %copy-start.88 = (s32[1,1,1,128,2]{4,3,2,1,0:T(8,128)S(1)}, s32[1,1,1,128,2]{4,3,2,1,0:T(8,128)}, u32[]{:S(2)}) copy-start(s32[1,1,1,128,2]{4,3,2,1,0:T(8,128)} %copy-done.87) | copy-start | bytes 3076
  672.6 27.5 %copy-start.39 = (f32[128,768]{1,0:T(8,128)S(1)}, f32[128,768]{1,0:T(8,128)}, u32[]{:S(2)}) copy-start(f32[128,768]{1,0:T(8,128)} %copy-done.38) | copy-start | bytes 1179652
  672.6 27.5 %copy-start.154 = (f32[128]{0:T(128)S(1)}, f32[128]{0:T(128)}, u32[]{:S(2)}) copy-start(f32[128]{0:T(128)} %copy-done.153) | copy-start | bytes 1540
  673.7 23.3 %all-to-all-start.11 = ((bf16[64,5,768]{2,1,0:T(8,128)(2,1)}), bf16[64,5,768]{2,1,0:T(8,128)(2,1)}, u32[]{:S(2)}, u32[]{:S(2)}) async-start(bf16[64,5,768]{2,1,0:T(8,128)(2,1)} %reshape.1037), calls=%async_computation.11 | async-start | bytes 1572864 | tf_op jit(solution)/shard_map/all_to_all | solution.py:289
  681.5 19.5 %copy-start.5 = (bf16[1,768,768]{2,1,0:T(8,128)(2,1)S(1)}, bf16[1,768,768]{2,1,0:T(8,128)(2,1)}, u32[]{:S(2)}) copy-start(bf16[1,768,768]{2,1,0:T(8,128)(2,1)} %all-gather.13.cloned.1.call-done) | copy-start | bytes 3538948
  681.5 82.4 %reduce-scatter.24.cloned.1.call-start = ((), (), s32[]{:S(2)}) async-start(), calls=%async_computation.33 | async-start | bytes 3538944
  739.7 42.4 %all-to-all-start.12 = ((bf16[64,5,768]{2,1,0:T(8,128)(2,1)}), bf16[64,5,768]{2,1,0:T(8,128)(2,1)}, u32[]{:S(2)}, u32[]{:S(2)}) async-start(bf16[64,5,768]{2,1,0:T(8,128)(2,1)} %reshape.1047), calls=%async_computation.12 | async-start | bytes 1572864 | tf_op jit(solution)/shard_map/all_to_all | solution.py:260
  752.5 13.4 %copy-start.2 = (bf16[1,768,2304]{2,1,0:T(8,128)(2,1)S(1)}, bf16[1,768,2304]{2,1,0:T(8,128)(2,1)}, u32[]{:S(2)}) copy-start(bf16[1,768,2304]{2,1,0:T(8,128)(2,1)} %all-gather.9.cloned.1.call-done) | copy-start | bytes 10616836
  771.2 7.7 collective-permute-start.3
  782.2 24.7 %all-to-all-start.13 = ((bf16[64,5,768]{2,1,0:T(8,128)(2,1)}), bf16[64,5,768]{2,1,0:T(8,128)(2,1)S(1)}, u32[]{:S(2)}, u32[]{:S(2)}) async-start(bf16[64,5,768]{2,1,0:T(8,128)(2,1)} %multiply_convert_fusion.9), calls=%async_computation.13 | async-start | bytes 1572864 | tf_op jit(solution)/shard_map/all_to_all | solution.py:267
  807.1 12.3 %copy-start.116 = (bf16[320,768]{1,0:T(8,128)(2,1)}, bf16[320,768]{1,0:T(8,128)(2,1)S(1)}, u32[]{:S(2)}) copy-start(bf16[320,768]{1,0:T(8,128)(2,1)S(1)} %reshape.1049) | copy-start | bytes 1474564
  820.7 16.4 %copy-start.6 = (bf16[1,768,768]{2,1,0:T(8,128)(2,1)S(1)}, bf16[1,768,768]{2,1,0:T(8,128)(2,1)}, u32[]{:S(2)}) copy-start(bf16[1,768,768]{2,1,0:T(8,128)(2,1)} %all-gather.13.cloned.1.call-done) | copy-start | bytes 3538948
  820.7 16.4 %copy-start.59 = (bf16[128,768]{1,0:T(8,128)(2,1)S(1)}, bf16[128,768]{1,0:T(8,128)(2,1)}, u32[]{:S(2)}) copy-start(bf16[128,768]{1,0:T(8,128)(2,1)} %get-tuple-element.85) | copy-start | bytes 589828
  825.9 29.7 %copy-start.42 = (f32[128,768]{1,0:T(8,128)S(1)}, f32[128,768]{1,0:T(8,128)}, u32[]{:S(2)}) copy-start(f32[128,768]{1,0:T(8,128)} %get-tuple-element.142) | copy-start | bytes 1179652
  825.9 29.7 %copy-start.152 = (f32[128]{0:T(128)S(1)}, f32[128]{0:T(128)}, u32[]{:S(2)}) copy-start(f32[128]{0:T(128)} %add_rsqrt_fusion) | copy-start | bytes 1540
  825.9 26.3 %all-to-all-start.14 = ((bf16[64,5,768]{2,1,0:T(8,128)(2,1)}), bf16[64,5,768]{2,1,0:T(8,128)(2,1)}, u32[]{:S(2)}, u32[]{:S(2)}) async-start(bf16[64,5,768]{2,1,0:T(8,128)(2,1)} %reshape.1050), calls=%async_computation.14 | async-start | bytes 1572864 | tf_op jit(solution)/shard_map/all_to_all | solution.py:289
  836.8 111.9 %reduce-scatter.26.cloned.1.call-start = ((), (), s32[]{:S(2)}) async-start(), calls=%async_computation.34 | async-start | bytes 3538944
  838.4 20.2 %copy-start.55 = (f32[128,768]{1,0:T(8,128)}, f32[128,768]{1,0:T(8,128)S(1)}, u32[]{:S(2)}) copy-start(f32[128,768]{1,0:T(8,128)S(1)} %get-tuple-element.160) | copy-start | bytes 1179652
  858.1 67.5 %copy-start.40 = (f32[128,768]{1,0:T(8,128)}, f32[128,768]{1,0:T(8,128)S(1)}, u32[]{:S(2)}) copy-start(f32[128,768]{1,0:T(8,128)S(1)} %get-tuple-element.108) | copy-start | bytes 1179652
  897.6 171.8 %reduce-scatter.30.cloned.1.call-start = ((), (), s32[]{:S(2)}) async-start(), calls=%async_computation.36 | async-start | bytes 221184
  925.5 161.3 %reduce-scatter.20.cloned.1.call-start = ((), (), s32[]{:S(2)}) async-start(), calls=%async_computation.31 | async-start | bytes 1327104 | tf_op jit(solution)/shard_map/reduce_scatter | solution.py:340
  929.5 157.3 %reduce-scatter.18.cloned.1.call-start = ((), (), s32[]{:S(2)}) async-start(), calls=%async_computation.30 | async-start | bytes 3981312 | tf_op jit(solution)/shard_map/reduce_scatter | solution.py:337
  958.3 17.1 %copy-start.112 = (bf16[128,768]{1,0:T(8,128)(2,1)S(1)}, bf16[128,768]{1,0:T(8,128)(2,1)}, u32[]{:S(2)}) copy-start(bf16[128,768]{1,0:T(8,128)(2,1)} %get-tuple-element.109) | copy-start | bytes 589828
  978.6 25.4 %all-to-all-start.4 = ((bf16[64,5,768]{2,1,0:T(8,128)(2,1)}), bf16[64,5,768]{2,1,0:T(8,128)(2,1)S(1)}, u32[]{:S(2)}, u32[]{:S(2)}) async-start(bf16[64,5,768]{2,1,0:T(8,128)(2,1)} %reshape.1012), calls=%async_computation.4 | async-start | bytes 1572864 | tf_op jit(solution)/shard_map/all_to_all | solution.py:189
  1004.3 26.3 %copy-start.52 = (s32[128,1024]{0,1:T(8,128)S(1)}, s32[128,1024]{0,1:T(8,128)}, u32[]{:S(2)}) copy-start(s32[128,1024]{0,1:T(8,128)} %copy-done.51) | copy-start | bytes 1572868
  1020.0 50.7 %all-to-all-start.5 = ((bf16[64,5,768]{2,1,0:T(8,128)(2,1)}), bf16[64,5,768]{2,1,0:T(8,128)(2,1)}, u32[]{:S(2)}, u32[]{:S(2)}) async-start(bf16[64,5,768]{2,1,0:T(8,128)(2,1)} %reshape.1014), calls=%async_computation.5 | async-start | bytes 1572864 | tf_op jit(solution)/shard_map/all_to_all | solution.py:204
  1030.5 84.1 %reduce-scatter.28.cloned.1.call-start = ((), (), s32[]{:S(2)}) async-start(), calls=%async_computation.35 | async-start | bytes 221184
  1041.5 38.8 %copy-start.3 = (bf16[1,768,2304]{2,1,0:T(8,128)(2,1)S(1)}, bf16[1,768,2304]{2,1,0:T(8,128)(2,1)}, u32[]{:S(2)}) copy-start(bf16[1,768,2304]{2,1,0:T(8,128)(2,1)} %all-gather.9.cloned.1.call-done) | copy-start | bytes 10616836
  1084.1 31.3 %copy-start.166 = (bf16[1,96]{1,0:T(2,128)(2,1)S(1)}, bf16[1,96]{1,0:T(2,128)(2,1)}, u32[]{:S(2)}) copy-start(bf16[1,96]{1,0:T(2,128)(2,1)} %copy.203) | copy-start | bytes 580
  1085.0 116.7 %all-reduce.17.cloned.1.call-start = ((), (), s32[]{:S(2)}) async-start(), calls=%async_computation.37 | async-start | bytes 1179648 | tf_op jit(solution)/shard_map/psum | solution.py:354
  (154 other events, 890.3 us)
Sparse Core Ops, SparseCore 0:
  9.7 32.1 all-gather.8
  45.6 27.6 all-gather.10
  75.0 23.7 all-gather.12
  189.5 25.3 all-gather.14
  341.4 25.1 all-gather.18
  368.7 34.5 all-gather.22
  405.0 29.3 all-gather.20
  576.1 38.1 reduce-scatter.21
  625.5 39.4 all-gather.16
  724.0 39.9 reduce-scatter.23
  897.7 32.3 reduce-scatter.25
  932.3 29.2 reduce-scatter.29
  964.1 33.6 reduce-scatter.19
  1000.2 48.6 reduce-scatter.17
  1085.1 29.4 reduce-scatter.27
  1117.2 84.4 all-reduce.16
where the time goes:
time: 1220 us; the launch traced here: 1210 us
  matrix products  367 us (30%)
  waiting for transfers between devices  287 us (24%)
  local copies, waits for them, and re-layouts  237 us (19%)
  starting transfers between devices  126 us (10%)
  other arithmetic  98.4 us (8%)
  blocking collectives  77.8 us (6%)
  between operations  18.5 us (2%)
    psum x1, waiting for transfers between devices, per_device(): lax.psum(summed[0].astype(jnp.bfloat16), 'rep').astype(jnp.float32)  60.5 us
    unnamed x381, local copies, waits for them, and re-layouts  57.6 us
    unnamed x21, waiting for transfers between devices  51.7 us
    dot_general x6, matrix products, context_of(): jnp.einsum('hqk,khd->qhd', soft_weights.astype(jnp.bfloat16), value_part,...  49.5 us
    all_to_all x6, starting transfers between devices, per_device(): lax.all_to_all(dispatch_rows(normed_ffn, slot_owner), ('rep', 'shard'), s...  47.1 us
    dot_general x3, matrix products, per_device(): jnp.dot(expert_activated, second_proj, preferred_element_type=jnp.float32)  44.8 us
    all_to_all x3, waiting for transfers between devices, per_device(): lax.all_to_all(d_sent.reshape(experts, capacity, model_width), ('rep', 's...  43.8 us
    all_to_all x6, waiting for transfers between devices, per_device(): lax.all_to_all(dispatch_rows(normed_ffn, slot_owner), ('rep', 'shard'), s...  43.7 us
  transfers between devices with their start and end apart: 35, of which 20 were waited for; matrix products, arithmetic and copies ran while one was open for 38% of the time, Pallas kernels for 0%

commit v1 on v0

v1 whole, which is shorter than its diff:
```python
from functools import partial

import jax
import jax.numpy as jnp
from jax import lax
from jax.experimental import pallas as pl
from jax.experimental.pallas import tpu as pltpu
from jax.sharding import PartitionSpec as P

F32 = jnp.float32
BF = jnp.bfloat16
D = 768
H = 12
HD = 64
FF = 3072
SEQ = 1024
TOK = 128
BLOCK = 256
RELB = 32
EXPERTS = 64
CAP = 5
LANES = 128
COLS = D // LANES
CHUNK = 32
GROUP = 16
SLOTS = EXPERTS * CAP
GROUPS_ALL = 2 * EXPERTS // GROUP
ROWS = 2 * EXPERTS * CAP
PAIRS = H // 2
EPS = 1e-05
EVERYONE = ("section", "rep", "shard")
HIGHEST = lax.Precision.HIGHEST
MIB = 1 << 20


def mm(a, b):
    return lax.dot_general(a, b, (((1,), (0,)), ((), ())), preferred_element_type=F32)


def mm_nt(a, b):
    return lax.dot_general(a, b, (((1,), (1,)), ((), ())), preferred_element_type=F32)


def mm_tn(a, b):
    return lax.dot_general(a, b, (((0,), (0,)), ((), ())), preferred_element_type=F32)


def call(kernel, outs, name, flops, moved, vmem=32, **more):
    return pl.pallas_call(
        kernel,
        out_shape=outs,
        name=name,
        compiler_params=pltpu.CompilerParams(vmem_limit_bytes=vmem * MIB),
        cost_estimate=pl.CostEstimate(flops=flops, bytes_accessed=moved, transcendentals=0),
        **more,
    )


def shape(*dims, dtype=BF):
    return jax.ShapeDtypeStruct(dims, dtype)


def pack_tables():
    row = jnp.arange(GROUP * CAP * COLS, dtype=jnp.int32)[:, None]
    col = jnp.arange(GROUP * CHUNK, dtype=jnp.int32)[None, :]
    block, inside = row // (GROUP * CAP), row % (GROUP * CAP)
    place = (inside // CAP) * CHUNK + block * CAP + inside % CAP
    return (place == col).astype(BF)


def unpack(chunks, table, target):
    for g in range(chunks.shape[0] // GROUP):
        raw = chunks[g * GROUP : (g + 1) * GROUP].reshape(GROUP * CHUNK, LANES)
        rows = mm(table, raw).astype(BF)
        for c in range(COLS):
            target[g * GROUP * CAP : (g + 1) * GROUP * CAP, c * LANES : (c + 1) * LANES] = rows[
                c * GROUP * CAP : (c + 1) * GROUP * CAP
            ]


def pack(rows, table_t, target, first):
    for g in range(rows.shape[0] // (GROUP * CAP)):
        part = rows[g * GROUP * CAP : (g + 1) * GROUP * CAP]
        stacked = jnp.concatenate([part[:, c * LANES : (c + 1) * LANES] for c in range(COLS)], axis=0)
        chunk = mm(table_t, stacked).astype(BF).reshape(GROUP, CHUNK, LANES)
        target[first + g * GROUP : first + (g + 1) * GROUP] = chunk


def pack_for_layer(rows, table_t, target, layer):
    pack(rows, table_t, target, layer * EXPERTS)
    other = (1 - layer) * EXPERTS
    target[other : other + EXPERTS] = jnp.zeros((EXPERTS, CHUNK, LANES), BF)


def slots_by_token(slot_rows):
    places = lax.broadcasted_iota(jnp.int32, (SLOTS, TOK), 0)
    return [jnp.where(places == slot_rows[k : k + 1, :], 1.0, 0.0).astype(BF) for k in range(2)]


def tokens_by_slot(slot_cols):
    places = lax.broadcasted_iota(jnp.int32, (TOK, SLOTS), 1)
    return [jnp.where(places == slot_cols[:, k : k + 1], 1.0, 0.0).astype(BF) for k in range(2)]


def norm_of(hidden, gain):
    scaling = lax.rsqrt(jnp.mean(hidden * hidden, axis=-1, keepdims=True) + EPS)
    return hidden * scaling * gain, scaling


def norm_back(hidden, scaling, gain, grad):
    gain_grad = jnp.sum(grad * hidden * scaling, axis=0, keepdims=True)
    weighted = grad * gain
    inner = jnp.mean(weighted * hidden, axis=-1, keepdims=True)
    return weighted * scaling - hidden * (scaling * scaling * scaling * inner), gain_grad


def bias_tiles_kernel(line_ref, out_ref):
    for h in range(2):
        for delta in range(4):
            line = jnp.broadcast_to(line_ref[h * 4 + delta : h * 4 + delta + 1, :], (BLOCK, 2 * BLOCK))
            turned = pltpu.roll(line, 0, 1, stride=1, stride_axis=0)
            out_ref[h * 4 + delta] = turned[:, :BLOCK].astype(BF)


def bias_tiles(table):
    m = jnp.arange(2 * BLOCK, dtype=jnp.int32)
    ahead = jnp.where(m < BLOCK, m, m - 2 * BLOCK)
    distance = jnp.arange(4, dtype=jnp.int32)[:, None] * BLOCK - ahead[None, :]
    bucket = jnp.clip((distance + BLOCK) * RELB // (SEQ + BLOCK), 0, RELB - 1)
    onehot = (bucket[..., None] == jnp.arange(RELB, dtype=jnp.int32)).astype(F32)
    lines = jnp.einsum("dmb,bh->hdm", onehot, table, precision=HIGHEST).reshape(8, 2 * BLOCK)
    return call(bias_tiles_kernel, shape(8, BLOCK, BLOCK), "bias_tiles", 0, 1 << 20)(lines)


def head_mask(h, rows):
    lane = lax.broadcasted_iota(jnp.int32, (rows, LANES), 1)
    return (lane < HD) if h == 0 else (lane >= HD)


def attention_kernel(qkv_ref, bias_ref, ctx_ref, weights_ref):
    step = 128
    for i in range(4):
        keys = (i + 1) * BLOCK
        key = qkv_ref[0:keys, LANES : 2 * LANES]
        value = qkv_ref[0:keys, 2 * LANES : 3 * LANES]
        for part in range(BLOCK // step):
            first = i * BLOCK + part * step
            query = qkv_ref[first : first + step, 0:LANES] * jnp.asarray(HD**-0.5, BF)
            mixed = []
            for h in range(2):
                mask = head_mask(h, step)
                own = jnp.where(mask, query, jnp.zeros_like(query))
                scores = mm_nt(own, key)
                offset = jnp.concatenate(
                    [bias_ref[h * 4 + i - b, part * step : (part + 1) * step, :] for b in range(i + 1)], axis=1
                ).astype(F32)
                scores = scores + offset
                top = jnp.max(scores, axis=-1, keepdims=True)
                terms = jnp.exp(scores - top)
                total = jnp.sum(terms, axis=-1, keepdims=True)
                weights = (terms * (1.0 / total)).astype(BF)
                weights_ref[h, first : first + step, 0:keys] = weights
                mixed.append(mm(weights, value))
            ctx_ref[first : first + step, :] = jnp.where(head_mask(0, step), mixed[0], mixed[1]).astype(BF)


def attention(qkv, tiles):
    return call(
        attention_kernel,
        (shape(SEQ, LANES), shape(2, SEQ, SEQ)),
        "attention",
        2 * 2 * 2 * SEQ * SEQ * LANES,
        8 << 20,
    )(qkv, tiles)


def attention_back_kernel(qkv_ref, weights_ref, dout_ref, flip_ref, dproj_ref, diag_ref, dkey, dvalue, tiles):
    step = 128
    dkey[...] = jnp.zeros_like(dkey)
    dvalue[...] = jnp.zeros_like(dvalue)
    tiles[...] = jnp.zeros_like(tiles)
    for i in range(4):
        keys = (i + 1) * BLOCK
        key = qkv_ref[0:keys, LANES : 2 * LANES]
        value = qkv_ref[0:keys, 2 * LANES : 3 * LANES]
        for part in range(BLOCK // step):
            first = i * BLOCK + part * step
            query = qkv_ref[first : first + step, 0:LANES]
            dout = dout_ref[first : first + step, :]
            query_t = query.astype(F32).T.astype(BF)
            dout_t = dout.astype(F32).T.astype(BF)
            moved = []
            for h in range(2):
                own = jnp.where(head_mask(h, step), dout, jnp.zeros_like(dout))
                low = weights_ref[h, first : first + step, 0:keys]
                weights = low.astype(F32)
                dweights = mm_nt(own, value)
                delta = jnp.sum(weights * dweights, axis=-1, keepdims=True)
                dscores = weights * (dweights - delta)
                for b in range(i + 1):
                    rows = slice(part * step, (part + 1) * step)
                    tiles[h * 4 + i - b, rows, :] += dscores[:, b * BLOCK : (b + 1) * BLOCK]
                dlow = dscores.astype(BF)
                moved.append(mm(dlow, key))
                head = slice(h * HD, (h + 1) * HD)
                dkey[head, 0:keys] += mm(query_t[head], dlow)
                dvalue[head, 0:keys] += mm(dout_t[head], low)
            dquery = jnp.where(head_mask(0, step), moved[0], moved[1]) * HD**-0.5
            dproj_ref[first : first + step, 0:LANES] = dquery.astype(BF)
    dproj_ref[:, LANES : 2 * LANES] = (dkey[...] * HD**-0.5).T.astype(BF)
    dproj_ref[:, 2 * LANES : 3 * LANES] = dvalue[...].T.astype(BF)
    for n in range(8):
        tile = tiles[n]
        high = tile.astype(BF)
        rest = (tile - high.astype(F32)).astype(BF)
        flipped = mm(high, flip_ref[...]) + mm(rest, flip_ref[...])
        wide = jnp.concatenate([flipped, jnp.zeros_like(flipped)], axis=1)
        turned = pltpu.roll(wide, 0, 1, stride=1, stride_axis=0)
        diag_ref[n : n + 1, :] = jnp.sum(turned, axis=0, keepdims=True)


def attention_back(qkv, weights, dout):
    at = jnp.arange(BLOCK, dtype=jnp.int32)
    flip = (at[:, None] + at[None, :] == BLOCK - 1).astype(BF)
    dproj, diag = call(
        attention_back_kernel,
        (shape(SEQ, 3 * LANES), shape(8, 2 * BLOCK, dtype=F32)),
        "attention_back",
        2 * 4 * 2 * SEQ * SEQ * LANES,
        8 << 20,
        scratch_shapes=[
            pltpu.VMEM((LANES, SEQ), F32),
            pltpu.VMEM((LANES, SEQ), F32),
            pltpu.VMEM((8, BLOCK, BLOCK), F32),
        ],
    )(qkv, weights, dout, flip)
    m = jnp.arange(2 * BLOCK, dtype=jnp.int32)
    distance = jnp.arange(4, dtype=jnp.int32)[:, None] * BLOCK + m[None, :] - (BLOCK - 1)
    bucket = jnp.clip((distance + BLOCK) * RELB // (SEQ + BLOCK), 0, RELB - 1)
    onehot = (bucket[..., None] == jnp.arange(RELB, dtype=jnp.int32)).astype(F32)
    return dproj, jnp.einsum("hdm,dmb->bh", diag.reshape(2, 4, 2 * BLOCK), onehot, precision=HIGHEST)


def middle_kernel(layer, ctx_ref, wao_ref, hidden_ref, gain_ref, slots_ref, table_ref, middle_ref, out_ref):
    context = jnp.concatenate([ctx_ref[g] for g in range(PAIRS)], axis=1)
    middle = hidden_ref[...].astype(F32) + mm(context, wao_ref[...])
    middle_ref[...] = middle
    normed = norm_of(middle, gain_ref[...])[0].astype(BF)
    first, second = slots_by_token(slots_ref[...])
    rows = mm(first + second, normed).astype(BF)
    pack_for_layer(rows, table_ref[...], out_ref, layer)


def middle_part(layer, ctx, wao, hidden, gain, slot_rows, table_t):
    return call(
        partial(middle_kernel, layer),
        (shape(TOK, D, dtype=F32), shape(2 * EXPERTS, CHUNK, LANES)),
        "middle",
        2 * TOK * D * D + 2 * SLOTS * TOK * D * 5,
        4 << 20,
    )(ctx, wao, hidden, gain, slot_rows, table_t)


def combined(back_ref, middle_ref, slots_ref, gates_ref, table_ref, rows):
    unpack(back_ref, table_ref[...], rows)
    picks = tokens_by_slot(slots_ref[...])
    gates = gates_ref[...]
    total = middle_ref[...]
    for k in range(2):
        total = total + gates[:, k : k + 1] * mm(picks[k], rows[...])
    return total.astype(BF)


def combine_kernel(back_ref, middle_ref, slots_ref, gates_ref, table_ref, out_ref, rows):
    out_ref[...] = combined(back_ref, middle_ref, slots_ref, gates_ref, table_ref, rows)


def combine_project_kernel(
    back_ref, middle_ref, slots_ref, gates_ref, table_ref, gain_ref, wqkv_ref, out_ref, normed_ref, send_ref, rows
):
    out = combined(back_ref, middle_ref, slots_ref, gates_ref, table_ref, rows)
    out_ref[...] = out
    normed = norm_of(out.astype(F32), gain_ref[...])[0].astype(BF)
    normed_ref[...] = normed
    projected = mm(normed, wqkv_ref[...]).astype(BF)
    for g in range(PAIRS):
        for part in range(3):
            first = part * D + g * LANES
            send_ref[g, :, part * LANES : (part + 1) * LANES] = projected[:, first : first + LANES]
    send_ref[PAIRS:8] = jnp.zeros((8 - PAIRS, TOK, 3 * LANES), BF)


def combine(back, middle, slot_cols, gates, table):
    return call(
        combine_kernel,
        shape(TOK, D),
        "combine",
        2 * TOK * SLOTS * D * 6,
        4 << 20,
        scratch_shapes=[pltpu.VMEM((SLOTS, D), BF)],
    )(back, middle, slot_cols, gates, table)


def combine_project(back, middle, slot_cols, gates, table, gain, wqkv):
    return call(
        combine_project_kernel,
        (shape(TOK, D), shape(TOK, D), shape(8, TOK, 3 * LANES)),
        "combine_project",
        2 * TOK * D * 3 * D,
        8 << 20,
        scratch_shapes=[pltpu.VMEM((SLOTS, D), BF)],
    )(back, middle, slot_cols, gates, table, gain, wqkv)


def send_grads(layer, dout, slot_rows, gates, table_t, out_ref):
    first, second = slots_by_token(slot_rows)
    wide = dout.astype(F32)
    rows = mm(first, (wide * gates[:, 0:1]).astype(BF)) + mm(second, (wide * gates[:, 1:2]).astype(BF))
    pack_for_layer(rows.astype(BF), table_t, out_ref, layer)


def grad_rows_kernel(layer, dout_ref, slots_ref, gates_ref, table_ref, out_ref):
    send_grads(layer, dout_ref[...], slots_ref[...], gates_ref[...], table_ref[...], out_ref)


def grad_rows(layer, dout, slot_rows, gates, table_t):
    return call(
        partial(grad_rows_kernel, layer),
        shape(2 * EXPERTS, CHUNK, LANES),
        "grad_rows",
        2 * TOK * SLOTS * D * 6,
        2 << 20,
    )(dout, slot_rows, gates, table_t)


def middle_back_kernel(
    back_ref, slots_ref, table_ref, dout_ref, middle_ref, gain_ref, wao_ref, dmid_ref, branch_ref, send_ref, dgain_ref, rows
):
    unpack(back_ref, table_ref[...], rows)
    first, second = tokens_by_slot(slots_ref[...])
    dnormed = mm(first + second, rows[...])
    middle = middle_ref[...]
    gain = gain_ref[...]
    scaling = lax.rsqrt(jnp.mean(middle * middle, axis=-1, keepdims=True) + EPS)
    moved, dgain = norm_back(middle, scaling, gain, dnormed)
    dgain_ref[...] = dgain
    dmid = dout_ref[...].astype(F32) + moved
    dmid_ref[...] = dmid
    branch = dmid.astype(BF)
    branch_ref[...] = branch
    dcontext = mm_nt(branch, wao_ref[...]).astype(BF)
    for g in range(PAIRS):
        send_ref[g] = dcontext[:, g * LANES : (g + 1) * LANES]
    send_ref[PAIRS:8] = jnp.zeros((8 - PAIRS, TOK, LANES), BF)


def middle_back(back, slot_cols, table, dout, middle, gain, wao):
    return call(
        middle_back_kernel,
        (shape(TOK, D, dtype=F32), shape(TOK, D), shape(8, TOK, LANES), shape(1, D, dtype=F32)),
        "middle_back",
        2 * TOK * D * D + 2 * TOK * SLOTS * D * 5,
        4 << 20,
        scratch_shapes=[pltpu.VMEM((SLOTS, D), BF)],
    )(back, slot_cols, table, dout, middle, gain, wao)


def hidden_grad(back_ref, wqkv_ref, hidden_ref, gain_ref, dmid_ref, dgain_ref):
    parts = [
        back_ref[g, :, part * LANES : (part + 1) * LANES] for part in range(3) for g in range(PAIRS)
    ]
    dnormed = mm_nt(jnp.concatenate(parts, axis=1), wqkv_ref[...])
    hidden = hidden_ref[...].astype(F32)
    scaling = lax.rsqrt(jnp.mean(hidden * hidden, axis=-1, keepdims=True) + EPS)
    moved, dgain = norm_back(hidden, scaling, gain_ref[...], dnormed)
    dgain_ref[...] = dgain
    return (dmid_ref[...] + moved).astype(BF)


def hidden_back_kernel(back_ref, wqkv_ref, hidden_ref, gain_ref, dmid_ref, dh_ref, dgain_ref):
    dh_ref[...] = hidden_grad(back_ref, wqkv_ref, hidden_ref, gain_ref, dmid_ref, dgain_ref)


def hidden_back_send_kernel(
    layer, back_ref, wqkv_ref, hidden_ref, gain_ref, dmid_ref, slots_ref, gates_ref, table_ref, dh_ref, dgain_ref, out_ref
):
    dh = hidden_grad(back_ref, wqkv_ref, hidden_ref, gain_ref, dmid_ref, dgain_ref)
    dh_ref[...] = dh
    send_grads(layer, dh, slots_ref[...], gates_ref[...], table_ref[...], out_ref)


def hidden_back(back, wqkv, hidden, gain, dmid):
    return call(
        hidden_back_kernel,
        (shape(TOK, D), shape(1, D, dtype=F32)),
        "hidden_back",
        2 * TOK * D * 3 * D,
        5 << 20,
    )(back, wqkv, hidden, gain, dmid)


def hidden_back_send(layer, back, wqkv, hidden, gain, dmid, slot_rows, gates, table_t):
    return call(
        partial(hidden_back_send_kernel, layer),
        (shape(TOK, D), shape(1, D, dtype=F32), shape(2 * EXPERTS, CHUNK, LANES)),
        "hidden_back_send",
        2 * TOK * D * 3 * D,
        6 << 20,
    )(back, wqkv, hidden, gain, dmid, slot_rows, gates, table_t)


FF_STEP = 512
ROW_STEP = 160


def gelu_parts(up):
    size = jnp.abs(up) * (0.5**0.5)
    t = 1.0 / (1.0 + 0.3275911 * size)
    bell = jnp.exp(up * up * -0.5)
    series = t * (0.254829592 + t * (-0.284496736 + t * (1.421413741 + t * (-1.453152027 + t * 1.061405429))))
    tail = 0.5 * series * bell
    phi = jnp.where(up < 0.0, tail, 1.0 - tail)
    return up * phi, phi + up * bell * 0.3989422804014327


def expert_forward_kernel(in_ref, win_ref, wout_ref, table_ref, table_t_ref, x_ref, act_ref, slope_ref, out_ref, total):
    step = pl.program_id(0)

    @pl.when(step == 0)
    def _():
        unpack(in_ref, table_ref[...], x_ref)
        total[...] = jnp.zeros_like(total)

    for r in range(ROWS // ROW_STEP):
        rows = slice(r * ROW_STEP, (r + 1) * ROW_STEP)
        act, slope = gelu_parts(mm(x_ref[rows, :], win_ref[...]))
        act = act.astype(BF)
        act_ref[rows, :] = act
        slope_ref[rows, :] = slope.astype(BF)
        total[rows, :] += mm(act, wout_ref[...])

    @pl.when(step == pl.num_programs(0) - 1)
    def _():
        pack(total[...].astype(BF), table_t_ref[...], out_ref, 0)


def whole(*dims):
    return pl.BlockSpec(dims, lambda f: (0,) * len(dims))


def ff_columns(rows):
    return pl.BlockSpec((rows, FF_STEP), lambda f: (0, f))


def ff_rows(columns):
    return pl.BlockSpec((FF_STEP, columns), lambda f: (f, 0))


CHUNKS = (2 * EXPERTS, CHUNK, LANES)
TABLE = (GROUP * CAP * COLS, GROUP * CHUNK)
TABLE_T = TABLE[::-1]


def expert_forward(arrived, first, second, table, table_t):
    return call(
        expert_forward_kernel,
        (shape(ROWS, D), shape(ROWS, FF), shape(ROWS, FF), shape(*CHUNKS)),
        "expert_forward",
        4 * ROWS * D * FF,
        20 << 20,
        vmem=40,
        grid=(FF // FF_STEP,),
        in_specs=[whole(*CHUNKS), ff_columns(D), ff_rows(D), whole(*TABLE), whole(*TABLE_T)],
        out_specs=(whole(ROWS, D), ff_columns(ROWS), ff_columns(ROWS), whole(*CHUNKS)),
        scratch_shapes=[pltpu.VMEM((ROWS, D), F32)],
    )(arrived, first, second, table, table_t)


def expert_back_kernel(in_ref, win_ref, wout_ref, slope_ref, table_ref, table_t_ref, grad_ref, dup_ref, out_ref, total):
    step = pl.program_id(0)

    @pl.when(step == 0)
    def _():
        unpack(in_ref, table_ref[...], grad_ref)
        total[...] = jnp.zeros_like(total)

    for r in range(ROWS // ROW_STEP):
        rows = slice(r * ROW_STEP, (r + 1) * ROW_STEP)
        dact = mm_nt(grad_ref[rows, :], wout_ref[...])
        dup = (dact * slope_ref[rows, :].astype(F32)).astype(BF)
        dup_ref[rows, :] = dup
        total[rows, :] += mm_nt(dup, win_ref[...])

    @pl.when(step == pl.num_programs(0) - 1)
    def _():
        pack(total[...].astype(BF), table_t_ref[...], out_ref, 0)


def expert_back(arrived, first, second, slope, table, table_t):
    return call(
        expert_back_kernel,
        (shape(ROWS, D), shape(ROWS, FF), shape(*CHUNKS)),
        "expert_back",
        4 * ROWS * D * FF,
        20 << 20,
        vmem=40,
        grid=(FF // FF_STEP,),
        in_specs=[whole(*CHUNKS), ff_columns(D), ff_rows(D), ff_columns(ROWS), whole(*TABLE), whole(*TABLE_T)],
        out_specs=(whole(ROWS, D), ff_columns(ROWS), whole(*CHUNKS)),
        scratch_shapes=[pltpu.VMEM((ROWS, D), F32)],
    )(arrived, first, second, slope, table, table_t)


def expert_both_kernel(
    in_ref, gin_ref, win_ref, wout_ref, table_ref, table_t_ref, x_ref, grad_ref, act_ref, dup_ref, out_ref, back_ref, total, dtotal
):
    step = pl.program_id(0)

    @pl.when(step == 0)
    def _():
        unpack(in_ref, table_ref[...], x_ref)
        unpack(gin_ref, table_ref[...], grad_ref)
        total[...] = jnp.zeros_like(total)
        dtotal[...] = jnp.zeros_like(dtotal)

    for r in range(ROWS // ROW_STEP):
        rows = slice(r * ROW_STEP, (r + 1) * ROW_STEP)
        act, slope = gelu_parts(mm(x_ref[rows, :], win_ref[...]))
        dup = (mm_nt(grad_ref[rows, :], wout_ref[...]) * slope).astype(BF)
        act = act.astype(BF)
        act_ref[rows, :] = act
        dup_ref[rows, :] = dup
        total[rows, :] += mm(act, wout_ref[...])
        dtotal[rows, :] += mm_nt(dup, win_ref[...])

    @pl.when(step == pl.num_programs(0) - 1)
    def _():
        pack(total[...].astype(BF), table_t_ref[...], out_ref, 0)
        pack(dtotal[...].astype(BF), table_t_ref[...], back_ref, 0)


def expert_both(arrived, grads, first, second, table, table_t):
    return call(
        expert_both_kernel,
        (shape(ROWS, D), shape(ROWS, D), shape(ROWS, FF), shape(ROWS, FF), shape(*CHUNKS), shape(*CHUNKS)),
        "expert_both",
        8 * ROWS * D * FF,
        24 << 20,
        vmem=44,
        grid=(FF // FF_STEP,),
        in_specs=[whole(*CHUNKS), whole(*CHUNKS), ff_columns(D), ff_rows(D), whole(*TABLE), whole(*TABLE_T)],
        out_specs=(
            whole(ROWS, D),
            whole(ROWS, D),
            ff_columns(ROWS),
            ff_columns(ROWS),
            whole(*CHUNKS),
            whole(*CHUNKS),
        ),
        scratch_shapes=[pltpu.VMEM((ROWS, D), F32), pltpu.VMEM((ROWS, D), F32)],
    )(arrived, grads, first, second, table, table_t)


def spread(chunks):
    return lax.all_to_all(chunks, EVERYONE, split_axis=0, concat_axis=0, tiled=True)


def across(chunks):
    return lax.all_to_all(chunks, "shard", split_axis=0, concat_axis=0, tiled=True)


def swap(value):
    return lax.ppermute(value, "section", [(0, 1), (1, 0)])


def slot_tables(routes):
    flat = routes.reshape(2, 2 * TOK)
    onehot = (flat[..., None] == jnp.arange(EXPERTS, dtype=jnp.int32)).astype(BF)
    at = jnp.arange(2 * TOK, dtype=jnp.int32)
    earlier = (at[None, :] < at[:, None]).astype(BF)
    before = jnp.einsum("ab,lbe->lae", earlier, onehot, preferred_element_type=F32)
    rank = jnp.sum(before * onehot.astype(F32), axis=-1).astype(jnp.int32)
    return (flat * CAP + rank).reshape(routes.shape)


def per_device(
    inputs, cotangent, w_qkv, w_attn_out, gain_attn, gain_ffn, rel_bias, w_in, w_out, routes, gates
):
    section = lax.axis_index("section")
    shard = lax.axis_index("shard")
    first_proj, second_proj = w_in[0, 0], w_out[0, 0]
    hidden0 = lax.dynamic_index_in_dim(inputs[:, 0], section, 0, keepdims=False)
    cot = lax.dynamic_index_in_dim(cotangent[:, 0], section, 0, keepdims=False)
    table = pack_tables()
    table_t = table.T

    rows = w_qkv.shape[1]
    columns = w_qkv[0].reshape(rows, 3, PAIRS, LANES).transpose(2, 0, 1, 3).reshape(PAIRS, rows, 3 * LANES)
    columns = jnp.concatenate([columns, jnp.zeros((2, rows, 3 * LANES), BF)], axis=0)
    biases = rel_bias[0].reshape(4, PAIRS, 2).transpose(1, 0, 2).reshape(PAIRS, 8)
    biases = jnp.pad(biases, ((0, 2), (0, 3 * LANES - 8)))
    gains = jnp.pad(jnp.concatenate([gain_attn, gain_ffn], axis=0), ((0, 0), (0, 3 * LANES - rows)))
    extra = jnp.concatenate(
        [jnp.broadcast_to(gains[None], (8, 2, 3 * LANES)), biases[:, None], jnp.zeros((8, 5, 3 * LANES), BF)], axis=1
    )
    parcel = jnp.concatenate([columns, extra], axis=1)
    parcel = jnp.concatenate([parcel, parcel], axis=0)
    got = lax.all_to_all(parcel, ("section", "shard"), split_axis=0, concat_axis=0, tiled=True)
    got = got.reshape(2, 8, rows + 8, 3 * LANES)
    w_own = got[:, :, :rows].reshape(2, D, 3 * LANES)
    gain_a = got[:, :, rows, :rows].reshape(2, 1, D).astype(F32)
    gain_f = got[:, :, rows + 1, :rows].reshape(2, 1, D).astype(F32)
    bias = got[:, :, rows + 2, :8].reshape(2, RELB, 2).astype(F32)
    tiles = [bias_tiles(bias[l]) for l in range(2)]

    full0 = lax.all_gather(hidden0, "shard", axis=0, tiled=True)
    w_ao = lax.all_gather(w_attn_out[0], ("section", "shard"), axis=0, tiled=True).reshape(2, D, D)
    w_full = lax.all_gather(w_qkv[0], ("section", "shard"), axis=0, tiled=True).reshape(2, D, 3 * D)

    def both_layers(values):
        own = lax.dynamic_index_in_dim(values[0, :, 0], section, 0, keepdims=False)
        other = swap(lax.dynamic_index_in_dim(values[0, :, 0], 1 - section, 0, keepdims=False))
        return jnp.where(section == 0, jnp.stack([own, other]), jnp.stack([other, own]))

    slot_cols = slot_tables(both_layers(routes))
    slot_rows = slot_cols.transpose(0, 2, 1)
    gate_cols = both_layers(gates)

    grads1 = spread(grad_rows(1, cot, slot_rows[1], gate_cols[1], table_t))

    normed0 = norm_of(full0.astype(F32), gain_a[0])[0].astype(BF)
    qkv0 = mm(normed0, w_own[0]).astype(BF)
    ctx0, weights0 = attention(qkv0, tiles[0])
    ctx0_tok = across(ctx0.reshape(8, TOK, LANES))
    middle0, send = middle_part(0, ctx0_tok, w_ao[0], hidden0, gain_f[0], slot_rows[0], table_t)
    x0, act0, slope0, made = expert_forward(spread(send), first_proj, second_proj, table, table_t)
    back = spread(made)[0:EXPERTS]
    out0, normed1, send = combine_project(back, middle0, slot_cols[0], gate_cols[0], table, gain_a[1], w_full[1])

    qkv1 = across(send).reshape(SEQ, 3 * LANES)
    normed1_full = lax.all_gather(normed1, "shard", axis=0, tiled=True)
    ctx1, weights1 = attention(qkv1, tiles[1])
    ctx1_tok = across(ctx1.reshape(8, TOK, LANES))
    middle1, send = middle_part(1, ctx1_tok, w_ao[1], out0, gain_f[1], slot_rows[1], table_t)
    x1, g1, act1, dup1, made1, dmade1 = expert_both(spread(send), grads1, first_proj, second_proj, table, table_t)

    back = spread(dmade1)[EXPERTS:]
    dmid1, branch1, send, dgain_f1 = middle_back(back, slot_cols[1], table, cot, middle1, gain_f[1], w_ao[1])
    branch1_full = lax.all_gather(branch1, "shard", axis=0, tiled=True)
    dproj1, drel1 = attention_back(qkv1, weights1, across(send).reshape(SEQ, LANES))
    dproj1_tok = across(dproj1.reshape(8, TOK, 3 * LANES))
    dh1, dgain_a1, send = hidden_back_send(
        0, dproj1_tok, w_full[1], out0, gain_a[1], dmid1, slot_rows[0], gate_cols[0], table_t
    )
    made1_back = spread(made1)[EXPERTS:]
    out1 = combine(made1_back, middle1, slot_cols[1], gate_cols[1], table)

    g0, dup0, dmade0 = expert_back(spread(send), first_proj, second_proj, slope0, table, table_t)
    back = spread(dmade0)[0:EXPERTS]
    dmid0, branch0, send, dgain_f0 = middle_back(back, slot_cols[0], table, dh1, middle0, gain_f[0], w_ao[0])
    branch0_full = lax.all_gather(branch0, "shard", axis=0, tiled=True)
    dproj0, drel0 = attention_back(qkv0, weights0, across(send).reshape(SEQ, LANES))
    dproj0_tok = across(dproj0.reshape(8, TOK, 3 * LANES))
    dh0, dgain_a0 = hidden_back(dproj0_tok, w_full[0], hidden0, gain_a[0], dmid0)

    def own(a, b):
        return jnp.where(section == 0, a, b)

    grad_in = mm_tn(own(x0, x1), own(dup0, dup1))
    grad_out = mm_tn(own(act0, act1), own(g0, g1))

    def parcel_of(normed, dproj, ctx, branch, dgain_a, dgain_f, drel):
        dqkv = mm_tn(normed, dproj).astype(BF).reshape(8, rows, 3 * LANES)
        dao = mm_tn(ctx, branch).astype(BF).reshape(8, 16, 2, 3 * LANES).transpose(0, 2, 1, 3)
        small = jnp.concatenate(
            [
                dgain_a.reshape(2, 3 * LANES),
                dgain_f.reshape(2, 3 * LANES),
                jnp.pad(drel.reshape(1, 2 * RELB), ((0, 3), (0, 3 * LANES - 2 * RELB))),
            ],
            axis=0,
        ).astype(BF)
        return jnp.concatenate(
            [dqkv, dao.reshape(8, 32, 3 * LANES), jnp.broadcast_to(small[None], (8, 8, 3 * LANES))], axis=1
        )

    parcels = jnp.concatenate(
        [
            parcel_of(normed0, dproj0, ctx0, branch0_full, dgain_a0, dgain_f0, drel0),
            parcel_of(normed1_full, dproj1, ctx1, branch1_full, dgain_a1, dgain_f1, drel1),
        ],
        axis=0,
    )
    got = lax.all_to_all(parcels, ("section", "rep"), split_axis=0, concat_axis=0, tiled=True)
    summed = jnp.sum(got.astype(F32), axis=0).astype(BF)

    turn = [(a * 8 + b, b * 8 + a) for a in range(8) for b in range(8)]
    block = lax.ppermute(summed[:rows], ("rep", "shard"), turn)
    blocks = lax.all_to_all(
        jnp.broadcast_to(block[None], (8, rows, 3 * LANES)), "rep", split_axis=0, concat_axis=0, tiled=True
    )
    grad_qkv = blocks[:PAIRS].reshape(PAIRS, rows, 3, LANES).transpose(1, 2, 0, 3).reshape(1, rows, 3 * D)
    rest = jnp.concatenate(
        [
            jnp.concatenate([summed[rows : rows + 16], summed[rows + 16 : rows + 32]], axis=1),
            summed[rows + 32 : rows + 40].reshape(4, D),
            jnp.zeros((4, D), BF),
        ],
        axis=0,
    )
    rests = lax.all_gather(rest, ("rep", "shard"), axis=0, tiled=False).reshape(8, 8, 24, D)
    dao = rests[:, :PAIRS, :16].transpose(1, 0, 2, 3).reshape(D, D)
    grad_ao = lax.dynamic_slice_in_dim(dao, shard * rows, rows, 0)[None]
    small = rests[0, :, 16:20].astype(F32)
    gains_sum = jnp.sum(small[:, 0:2], axis=0)
    grad_gain = lax.dynamic_slice_in_dim(gains_sum, shard * rows, rows, 1)
    drel = small[:PAIRS, 2, : 2 * RELB].reshape(PAIRS, RELB, 2).transpose(1, 0, 2).reshape(RELB, H)
    grad_bias = lax.dynamic_slice_in_dim(drel, shard * 4, 4, 0)[None]

    def by_layer(layer0, layer1):
        keep = jnp.where(section == 0, layer0, layer1)
        other = swap(jnp.where(section == 0, layer1, layer0))
        pair = jnp.where(section == 0, jnp.stack([keep, other]), jnp.stack([other, keep]))
        return pair.reshape(1, 2, 1, TOK, D)

    return (
        by_layer(out0, out1),
        by_layer(dh0, dh1),
        grad_qkv.astype(F32),
        grad_ao.astype(F32),
        grad_gain[0:1],
        grad_gain[1:2],
        grad_bias,
        grad_in[None, None],
        grad_out[None, None],
    )


def solution(mesh):
    placed = (
        P(None, "rep", "shard", None),
        P(None, "rep", "shard", None),
        P("section", "shard", None),
        P("section", "shard", None),
        P("section", "shard"),
        P("section", "shard"),
        P("section", "shard", None),
        P("section", ("rep", "shard"), None, None),
        P("section", ("rep", "shard"), None, None),
        P("section", None, "rep", "shard", None),
        P("section", None, "rep", "shard", None),
    )
    return jax.shard_map(
        per_device,
        mesh=mesh,
        in_specs=placed,
        out_specs=(
            P("section", None, "rep", "shard", None),
            P("section", None, "rep", "shard", None),
            P("section", "shard", None),
            P("section", "shard", None),
            P("section", "shard"),
            P("section", "shard"),
            P("section", "shard", None),
            P("section", ("rep", "shard"), None, None),
            P("section", ("rep", "shard"), None, None),
        ),
        check_vma=False,
    )
```

time: 1220 us -> 645 us (0.53)
  the two profiles are of different devices: /device:TPU:0 before, /device:TPU:25 now
where the time goes in v1:
time: 645 us; the launch traced here: 634 us
  waiting for transfers between devices  196 us (30%)
  Pallas kernels  115 us (18%)
  starting transfers between devices  101 us (16%)
  local copies, waits for them, and re-layouts  87.8 us (14%)
  blocking collectives  71.2 us (11%)
  matrix products  32.3 us (5%)
  between operations  15.8 us (2%)
  other arithmetic  13.6 us (2%)
    all_to_all x3, blocking collectives, spread(): lax.all_to_all(chunks, EVERYONE, split_axis=0, concat_axis=0, tiled=True)  71.2 us
    all_to_all x5, waiting for transfers between devices, spread(): lax.all_to_all(chunks, EVERYONE, split_axis=0, concat_axis=0, tiled=True)  69.6 us
    unnamed x215, local copies, waits for them, and re-layouts  52.9 us
    all_to_all x7, waiting for transfers between devices, across(): lax.all_to_all(chunks, 'shard', split_axis=0, concat_axis=0, tiled=True)  40.3 us
    all_to_all x5, starting transfers between devices, spread(): lax.all_to_all(chunks, EVERYONE, split_axis=0, concat_axis=0, tiled=True)  39.6 us
    all_to_all x7, starting transfers between devices, across(): lax.all_to_all(chunks, 'shard', split_axis=0, concat_axis=0, tiled=True)  33.8 us
    pallas_call x1, Pallas kernels, expert_both(): call(expert_both_kernel, (shape(ROWS, D), shape(ROWS, D), shape(ROWS, FF)...  29.4 us
    dot_general x6, matrix products, mm_tn(): lax.dot_general(a, b, (((0,), (0,)), ((), ())), preferred_element_type=F32)  28.2 us
  transfers between devices with their start and end apart: 27, of which 18 were waited for; matrix products, arithmetic and copies ran while one was open for 10% of the time, Pallas kernels for 17%

profile of v1, /device:TPU:25, one launch (start us, length us, event | category | flops | bytes accessed | tf_op | source)
XLA Modules:
  0.0 633.6 jit_solution(14601984479789387447)
XLA Ops:
  15.4 7.4 %all-to-all-start = ((bf16[16,104,384]{2,1,0:T(8,128)(2,1)}), bf16[16,104,384]{2,1,0:T(8,128)(2,1)}, u32[]{:S(2)}, u32[]{:S(2)}) async-start(bf16[16,104,384]{2,1,0:T(8,128)(2,1)} %maximum_maximum_fusion.1), calls=%async_computation | async-start | bytes 2555904 | tf_op jit(solution)/shard_map/all_to_all | solution.py:608
  25.7 20.2 %all-to-all-done = bf16[16,104,384]{2,1,0:T(8,128)(2,1)} async-done(((bf16[16,104,384]{2,1,0:T(8,128)(2,1)}), bf16[16,104,384]{2,1,0:T(8,128)(2,1)}, u32[]{:S(2)}, u32[]{:S(2)}) %all-to-all-start) | async-done | bytes 1277984 | tf_op jit(solution)/shard_map/all_to_all | solution.py:608
  50.7 1.8 fusion.4
  52.5 2.4 convolution_convert_fusion.qkv_ref
  55.0 6.4 %attention.2 = (bf16[1024,128]{1,0:T(8,128)(2,1)}, bf16[2,1024,1024]{2,1,0:T(8,128)(2,1)S(1)}) custom-call(bf16[1024,384]{1,0:T(8,128)(2,1)S(1)} %convolution_convert_fusion.qkv_ref, bf16[8,256,256]{2,1,0:T(8,128)(2,1)S(1)} %bias_tiles.2.bias_ref), custom_call_target="tpu_custom_call" | custom-call | flops 1073741824 | bytes 8388608 | tf_op jit(solution)/shard_map/attention/pallas_call | solution.py:168
  61.4 2.0 copy-done.81
  63.4 3.7 all-to-all-start.1
  67.1 19.9 %all-gather.20.cloned.1.call-done = bf16[1,1536,768]{2,1,0:T(8,128)(2,1)} async-done(((bf16[1,96,768]{2,1,0:T(8,128)(2,1)}), bf16[1,1536,768]{2,1,0:T(8,128)(2,1)}) %all-gather.20.cloned.1.call-update) | async-done | bytes 2359312 | tf_op jit(solution)/shard_map/all_gather | solution.py:617
  87.1 2.8 slice_bitcast_fusion.3
  93.0 8.5 %all-to-all-start.2 = ((bf16[128,32,128]{2,1,0:T(8,128)(2,1)}), bf16[128,32,128]{2,1,0:T(8,128)(2,1)S(1)}, u32[]{:S(2)}, u32[]{:S(2)}) async-start(bf16[128,32,128]{2,1,0:T(8,128)(2,1)} %copy-done.44), calls=%async_computation.2 | async-start | bytes 2097152 | tf_op jit(solution)/shard_map/all_to_all | solution.py:565
  101.7 17.8 %all-to-all-done.2.in_ref = bf16[128,32,128]{2,1,0:T(8,128)(2,1)S(1)} async-done(((bf16[128,32,128]{2,1,0:T(8,128)(2,1)}), bf16[128,32,128]{2,1,0:T(8,128)(2,1)S(1)}, u32[]{:S(2)}, u32[]{:S(2)}) %all-to-all-start.2) | async-done | bytes 1048608 | tf_op jit(solution)/shard_map/all_to_all | solution.py:565
  119.5 20.1 %expert_forward.1 = (bf16[640,768]{1,0:T(8,128)(2,1)S(1)}, bf16[640,3072]{1,0:T(8,128)(2,1)S(1)}, bf16[640,3072]{1,0:T(8,128)(2,1)S(1)}, bf16[128,32,128]{2,1,0:T(8,128)(2,1)}) custom-call(bf16[128,32,128]{2,1,0:T(8,128)(2,1)S(1)} %all-to-all-done.2.in_ref, bf16[768,3072]{1,0:T(8,128)(2,1)} %bitcast.149, bf16[3072,768]{1,0:T(8,128)(2,1)} %bitcast.152, ...), custom_call_target="tpu_custom_call" | custom-call | flops 6039797760 | bytes 20971520 | tf_op jit(solution)/shard_map/expert_forward/pallas_call | solution.py:465
  140.6 2.0 copy-done.85
  142.6 1.9 copy-done.88
  144.5 7.9 %all-to-all-start.3 = ((bf16[128,32,128]{2,1,0:T(8,128)(2,1)}), bf16[128,32,128]{2,1,0:T(8,128)(2,1)S(1)}, u32[]{:S(2)}, u32[]{:S(2)}) async-start(bf16[128,32,128]{2,1,0:T(8,128)(2,1)} %get-tuple-element.52), calls=%async_computation.3 | async-start | bytes 2097152 | tf_op jit(solution)/shard_map/all_to_all | solution.py:565
  154.4 3.4 collective-permute-done.1
  158.9 10.5 %all-to-all-done.3 = bf16[128,32,128]{2,1,0:T(8,128)(2,1)S(1)} async-done(((bf16[128,32,128]{2,1,0:T(8,128)(2,1)}), bf16[128,32,128]{2,1,0:T(8,128)(2,1)S(1)}, u32[]{:S(2)}, u32[]{:S(2)}) %all-to-all-start.3) | async-done | bytes 1048608 | tf_op jit(solution)/shard_map/all_to_all | solution.py:565
  170.3 5.4 slice_bitcast_fusion
  175.7 1.8 combine_project.1
  179.7 5.2 all-to-all-start.4
  189.2 8.2 %all-to-all-done.4 = bf16[8,128,384]{2,1,0:T(8,128)(2,1)} async-done(((bf16[8,128,384]{2,1,0:T(8,128)(2,1)}), bf16[8,128,384]{2,1,0:T(8,128)(2,1)}, u32[]{:S(2)}, u32[]{:S(2)}) %all-to-all-start.4) | async-done | bytes 786464 | tf_op jit(solution)/shard_map/all_to_all | solution.py:569
  198.6 6.9 %attention.3 = (bf16[1024,128]{1,0:T(8,128)(2,1)S(1)}, bf16[2,1024,1024]{2,1,0:T(8,128)(2,1)S(1)}) custom-call(bf16[1024,384]{1,0:T(8,128)(2,1)} %bitcast.26.qkv_ref, bf16[8,256,256]{2,1,0:T(8,128)(2,1)S(1)} %copy-done.46), custom_call_target="tpu_custom_call" | custom-call | flops 1073741824 | bytes 8388608 | tf_op jit(solution)/shard_map/attention/pallas_call | solution.py:168
  206.2 2.0 copy-done.83
  208.2 5.4 all-to-all-start.5
  221.1 8.3 %all-to-all-start.7 = ((bf16[128,32,128]{2,1,0:T(8,128)(2,1)}), bf16[128,32,128]{2,1,0:T(8,128)(2,1)}, u32[]{:S(2)}, u32[]{:S(2)}) async-start(bf16[128,32,128]{2,1,0:T(8,128)(2,1)} %copy-done.20), calls=%async_computation.7 | async-start | bytes 2097152 | tf_op jit(solution)/shard_map/all_to_all | solution.py:565
  232.7 2.3 middle.3
  236.7 9.3 %all-to-all-done.7.gin_ref = bf16[128,32,128]{2,1,0:T(8,128)(2,1)} async-done(((bf16[128,32,128]{2,1,0:T(8,128)(2,1)}), bf16[128,32,128]{2,1,0:T(8,128)(2,1)}, u32[]{:S(2)}, u32[]{:S(2)}) %all-to-all-start.7) | async-done | bytes 1048608 | tf_op jit(solution)/shard_map/all_to_all | solution.py:565
  246.0 7.4 %all-to-all-start.6 = ((bf16[128,32,128]{2,1,0:T(8,128)(2,1)}), bf16[128,32,128]{2,1,0:T(8,128)(2,1)}, u32[]{:S(2)}, u32[]{:S(2)}) async-start(bf16[128,32,128]{2,1,0:T(8,128)(2,1)} %copy-done.42), calls=%async_computation.6 | async-start | bytes 2097152 | tf_op jit(solution)/shard_map/all_to_all | solution.py:565
  254.0 16.1 %all-to-all-done.6.in_ref = bf16[128,32,128]{2,1,0:T(8,128)(2,1)} async-done(((bf16[128,32,128]{2,1,0:T(8,128)(2,1)}), bf16[128,32,128]{2,1,0:T(8,128)(2,1)}, u32[]{:S(2)}, u32[]{:S(2)}) %all-to-all-start.6) | async-done | bytes 1048608 | tf_op jit(solution)/shard_map/all_to_all | solution.py:565
  272.2 29.4 %expert_both.1 = (bf16[640,768]{1,0:T(8,128)(2,1)S(1)}, bf16[640,768]{1,0:T(8,128)(2,1)S(1)}, bf16[640,3072]{1,0:T(8,128)(2,1)}, bf16[640,3072]{1,0:T(8,128)(2,1...) custom-call(bf16[128,32,128]{2,1,0:T(8,128)(2,1)} %all-to-all-done.6.in_ref, ...), custom_call_target="tpu_custom_call" | custom-call | flops 12079595520 | bytes 25165824 | tf_op jit(solution)/shard_map/expert_both/pallas_call | solution.py:543
  305.6 7.5 %all-to-all-start.9 = ((bf16[128,32,128]{2,1,0:T(8,128)(2,1)}), bf16[128,32,128]{2,1,0:T(8,128)(2,1)}, u32[]{:S(2)}, u32[]{:S(2)}) async-start(bf16[128,32,128]{2,1,0:T(8,128)(2,1)} %copy-done.43), calls=%async_computation.9 | async-start | bytes 2097152 | tf_op jit(solution)/shard_map/all_to_all | solution.py:565
  313.9 15.9 %all-to-all-done.9 = bf16[128,32,128]{2,1,0:T(8,128)(2,1)} async-done(((bf16[128,32,128]{2,1,0:T(8,128)(2,1)}), bf16[128,32,128]{2,1,0:T(8,128)(2,1)}, u32[]{:S(2)}, u32[]{:S(2)}) %all-to-all-start.9) | async-done | bytes 1048608 | tf_op jit(solution)/shard_map/all_to_all | solution.py:565
  339.7 5.3 all-to-all-start.10
  345.7 5.9 all-to-all-done.10
  352.5 2.2 copy-done.84
  354.7 8.0 %attention_back.2 = (bf16[1024,384]{1,0:T(8,128)(2,1)S(1)}, f32[8,512]{1,0:T(8,128)S(1)}) custom-call(bf16[1024,384]{1,0:T(8,128)(2,1)} %bitcast.26.qkv_ref, bf16[2,1024,1024]{2,1,0:T(8,128)(2,1)S(1)} %copy-done.84, bf16[1024,128]{1,0:T(8,128)(2,1)} %bitcast.35.dout_ref, bf16[256,256]{1,0:T(8,128)(2,1)S(1)} %copy-done.71), custom_call_target="tpu_custom_call" | custom-call | flops 2147483648 | bytes 8388608 | tf_op jit(solution)/shard_map/attention_back/pallas_call | solution.py:225
  364.2 5.1 all-to-all-start.11
  369.9 11.8 %all-to-all-done.11.back_ref = bf16[8,128,384]{2,1,0:T(8,128)(2,1)} async-done(((bf16[8,128,384]{2,1,0:T(8,128)(2,1)}), bf16[8,128,384]{2,1,0:T(8,128)(2,1)}, u32[]{:S(2)}, u32[]{:S(2)}) %all-to-all-start.11) | async-done | bytes 786464 | tf_op jit(solution)/shard_map/all_to_all | solution.py:569
  385.6 4.1 hidden_back_send.1
  389.7 23.1 %all_to_all.90.in_ref = bf16[128,32,128]{2,1,0:T(8,128)(2,1)S(1)} all-to-all(bf16[128,32,128]{2,1,0:T(8,128)(2,1)S(1)} %get-tuple-element.66), channel_id=1, replica_groups=mesh['section'=2,'rep'=8,'shard'=8] {'section','rep','shard'}, dimensions={0} | all-to-all | bytes 2097152 | tf_op jit(solution)/shard_map/all_to_all | solution.py:565
  412.8 18.1 %expert_back.1 = (bf16[640,768]{1,0:T(8,128)(2,1)S(1)}, bf16[640,3072]{1,0:T(8,128)(2,1)S(1)}, bf16[128,32,128]{2,1,0:T(8,128)(2,1)S(1)}) custom-call(bf16[128,32,128]{2,1,0:T(8,128)(2,1)S(1)} %all_to_all.90.in_ref, bf16[768,3072]{1,0:T(8,128)(2,1)} %bitcast.151, bf16[3072,768]{1,0:T(8,128)(2,1)} %bitcast.154, bf16[640,3072]{1,0:T(8,128)(2,1)S(1)} %copy-done.89, ...), custom_call_target="tpu_custom_call" | custom-call | flops 6039797760 | bytes 20971520 | tf_op jit(solution)/shard_map/expert_back/pallas_call | solution.py:500
  431.0 23.8 %all_to_all.91 = bf16[128,32,128]{2,1,0:T(8,128)(2,1)S(1)} all-to-all(bf16[128,32,128]{2,1,0:T(8,128)(2,1)S(1)} %get-tuple-element.68), channel_id=1, replica_groups=mesh['section'=2,'rep'=8,'shard'=8] {'section','rep','shard'}, dimensions={0} | all-to-all | bytes 2097152 | tf_op jit(solution)/shard_map/all_to_all | solution.py:565
  454.9 2.3 middle_back.3
  458.2 3.4 convolution_convert_fusion.1
  461.6 4.5 all-to-all-start.14
  466.5 9.4 %all-to-all-done.14 = bf16[8,128,128]{2,1,0:T(8,128)(2,1)S(1)} async-done(((bf16[8,128,128]{2,1,0:T(8,128)(2,1)}), bf16[8,128,128]{2,1,0:T(8,128)(2,1)S(1)}, u32[]{:S(2)}, u32[]{:S(2)}) %all-to-all-start.14) | async-done | bytes 262176 | tf_op jit(solution)/shard_map/all_to_all | solution.py:569
  475.9 2.3 copy-done.82
  478.2 7.6 %attention_back.3 = (bf16[1024,384]{1,0:T(8,128)(2,1)}, f32[8,512]{1,0:T(8,128)S(1)}) custom-call(bf16[1024,384]{1,0:T(8,128)(2,1)S(1)} %copy-done.87, bf16[2,1024,1024]{2,1,0:T(8,128)(2,1)S(1)} %copy-done.82, bf16[1024,128]{1,0:T(8,128)(2,1)S(1)} %bitcast.126, bf16[256,256]{1,0:T(8,128)(2,1)S(1)} %copy-done.72), custom_call_target="tpu_custom_call" | custom-call | flops 2147483648 | bytes 8388608 | tf_op jit(solution)/shard_map/attention_back/pallas_call | solution.py:225
  485.8 4.6 all-to-all-start.15
  490.3 1.8 convolution_convert_fusion.3
  493.9 3.7 convolution_convert_fusion.2
  497.7 5.1 all-to-all-done.15.back_ref
  504.7 2.5 hidden_back.1
  508.7 1.9 convolution_convert_fusion.4
  512.1 6.2 all-to-all-start.16
  518.5 23.2 %all-to-all-done.16 = bf16[16,136,384]{2,1,0:T(8,128)(2,1)} async-done(((bf16[16,136,384]{2,1,0:T(8,128)(2,1)}), bf16[16,136,384]{2,1,0:T(8,128)(2,1)}, u32[]{:S(2)}, u32[]{:S(2)}) %all-to-all-start.16) | async-done | bytes 1671200 | tf_op jit(solution)/shard_map/all_to_all | solution.py:694
  544.1 24.4 %all_to_all.92 = bf16[128,32,128]{2,1,0:T(8,128)(2,1)S(1)} all-to-all(bf16[128,32,128]{2,1,0:T(8,128)(2,1)S(1)} %copy-done.41), channel_id=1, replica_groups=mesh['section'=2,'rep'=8,'shard'=8] {'section','rep','shard'}, dimensions={0} | all-to-all | bytes 2097152 | tf_op jit(solution)/shard_map/all_to_all | solution.py:565
  570.1 5.2 collective-permute-done.2
  576.1 8.8 %convolution_bitcast_fusion = f32[1,1,3072,768]{3,2,1,0:T(8,128)} fusion(bf16[640,3072]{1,0:T(8,128)(2,1)} %copy-done.85, bf16[640,3072]{1,0:T(8,128)(2,1)} %get-tuple-element.88, pred[]{:T(512)S(6)} %eq.180, bf16[640,768]{1,0:T(8,128)(2,1)S(1)} %copy-done.93, bf16[640,768]{1,0:T(8,128)(2,1)S(1)} %copy-done.91), kind=kOutput, calls=%fused_computation | convolution fusion | flops 3022356480 | bytes 19267584 | tf_op jit(solution)/shard_map/dot_general | solution.py:45
  584.9 6.7 %collective-permute-start.4 = (bf16[96,384]{1,0:T(8,128)(2,1)S(1)}, bf16[96,384]{1,0:T(8,128)(2,1)S(1)}, u32[]{:S(2)}, u32[]{:S(2)}) collective-permute-start(bf16[96,384]{1,0:T(8,128)(2,1)S(1)} %slice.194), channel_id=1, source_target_pairs={{0,0},{1,8},{2,16},{3,24},{4,32},{5,40},{6,48},{7,56},{8,1},{9,9},... | collective-permute-start | bytes 221192 | tf_op jit(solution)/shard_map/ppermute | solution.py:698
  592.2 4.0 collective-permute-done.4
  597.0 5.2 all-to-all-start.17
  602.2 8.6 %convolution_bitcast_fusion.1 = f32[1,1,768,3072]{3,2,1,0:T(8,128)} fusion(bf16[640,3072]{1,0:T(8,128)(2,1)} %copy-done.19, bf16[640,3072]{1,0:T(8,128)(2,1)} %get-tuple-element.86, pred[]{:T(512)S(6)} %eq.180, bf16[640,768]{1,0:T(8,128)(2,1)S(1)} %copy-done.22, bf16[640,768]{1,0:T(8,128)(2,1)S(1)} %copy-done.24), kind=kOutput, calls=%fused_computation.1 | convolution fusion | flops 3022356480 | bytes 19267584 | tf_op jit(solution)/shard_map/dot_general | solution.py:45
  614.6 6.9 %all-gather.24.cloned.1.call-done = bf16[1536,768]{1,0:T(8,128)(2,1)} async-done(((bf16[24,768]{1,0:T(8,128)(2,1)}), bf16[1536,768]{1,0:T(8,128)(2,1)}) %all-gather.24.cloned.1.call-update) | async-done | bytes 2359312 | tf_op jit(solution)/shard_map/all_gather | solution.py:711
  (368 shorter events, 92.4 us)
Async XLA Ops:
  7.2 43.5 %all-gather.18.cloned.1.call-start = ((), (), s32[]{:S(2)}) async-start(), calls=%async_computation.21 | async-start | bytes 1769472 | tf_op jit(solution)/shard_map/all_gather | solution.py:616
  8.9 78.1 %all-gather.20.cloned.1.call-start = ((), (), s32[]{:S(2)}) async-start(), calls=%async_computation.22 | async-start | bytes 2506752 | tf_op jit(solution)/shard_map/all_gather | solution.py:617
  9.7 160.6 %all-gather.22.cloned.1.call-start = ((), (), s32[]{:S(2)}) async-start(), calls=%async_computation.23 | async-start | bytes 7520256 | tf_op jit(solution)/shard_map/all_gather | solution.py:618
  11.1 12.9 %collective-permute-start = (s32[128,2]{0,1:T(2,128)S(1)}, s32[128,2]{0,1:T(2,128)S(1)}, u32[]{:S(2)}, u32[]{:S(2)}) collective-permute-start(s32[128,2]{0,1:T(2,128)S(1)} %get-tuple-element.123), channel_id=1, source_target_pairs={{0,64},{64,0},{1,65},{65,1},{2,66},{66,2},{3,67},{67,3},{4,68},{68... | collective-permute-start | bytes 3080 | tf_op jit(solution)/shard_map/ppermute | solution.py:573
  15.4 30.4 %all-to-all-start = ((bf16[16,104,384]{2,1,0:T(8,128)(2,1)}), bf16[16,104,384]{2,1,0:T(8,128)(2,1)}, u32[]{:S(2)}, u32[]{:S(2)}) async-start(bf16[16,104,384]{2,1,0:T(8,128)(2,1)} %maximum_maximum_fusion.1), calls=%async_computation | async-start | bytes 2555904 | tf_op jit(solution)/shard_map/all_to_all | solution.py:608
  23.7 95.8 %copy-start.3 = (bf16[512,480]{1,0:T(8,128)(2,1)}, bf16[512,480]{1,0:T(8,128)(2,1)S(1)}, u32[]{:S(2)}) copy-start(bf16[512,480]{1,0:T(8,128)(2,1)S(1)} %fusion.11.table_ref.table_t_ref) | copy-start | bytes 1474564
  23.7 66.1 %copy-start.26 = (bf16[128,768]{1,0:T(8,128)(2,1)}, bf16[128,768]{1,0:T(8,128)(2,1)S(1)}, u32[]{:S(2)}) copy-start(bf16[128,768]{1,0:T(8,128)(2,1)S(1)} %fusion.70.hidden_ref) | copy-start | bytes 589828
  25.7 64.2 %copy-start.79 = (s32[2,128]{1,0:T(2,128)}, s32[2,128]{1,0:T(2,128)S(1)}, u32[]{:S(2)}) copy-start(s32[2,128]{1,0:T(2,128)S(1)} %copy.109.slots_ref) | copy-start | bytes 3076
  50.7 39.2 %copy-start.73 = (f32[1,768]{1,0:T(1,128)}, f32[1,768]{1,0:T(1,128)S(1)}, u32[]{:S(2)}) copy-start(f32[1,768]{1,0:T(1,128)S(1)} %squeeze.96.gain_ref) | copy-start | bytes 9220
  52.5 8.9 %copy-start.102 = (f32[1024]{0:T(1024)}, f32[1024]{0:T(1024)S(1)}, u32[]{:S(2)}) copy-start(f32[1024]{0:T(1024)S(1)} %add_rsqrt_fusion) | copy-start | bytes 12292
  63.4 26.4 %all-to-all-start.1 = ((bf16[8,128,128]{2,1,0:T(8,128)(2,1)}), bf16[8,128,128]{2,1,0:T(8,128)(2,1)S(1)}, u32[]{:S(2)}, u32[]{:S(2)}) async-start(bf16[8,128,128]{2,1,0:T(8,128)(2,1)} %bitcast.9), calls=%async_computation.1 | async-start | bytes 524288 | tf_op jit(solution)/shard_map/all_to_all | solution.py:569
  93.0 26.5 %all-to-all-start.2 = ((bf16[128,32,128]{2,1,0:T(8,128)(2,1)}), bf16[128,32,128]{2,1,0:T(8,128)(2,1)S(1)}, u32[]{:S(2)}, u32[]{:S(2)}) async-start(bf16[128,32,128]{2,1,0:T(8,128)(2,1)} %copy-done.44), calls=%async_computation.2 | async-start | bytes 2097152 | tf_op jit(solution)/shard_map/all_to_all | solution.py:565
  101.7 38.0 %copy-start.9 = (bf16[480,512]{1,0:T(8,128)(2,1)}, bf16[480,512]{1,0:T(8,128)(2,1)S(1)}, u32[]{:S(2)}) copy-start(bf16[480,512]{1,0:T(8,128)(2,1)S(1)} %fusion.14.table_ref) | copy-start | bytes 1474564
  119.5 32.9 %copy-start.103 = (f32[1,2,1,128,2]{3,4,2,1,0:T(2,128)S(1)}, f32[1,2,1,128,2]{3,4,2,1,0:T(2,128)}, u32[]{:S(2)}) copy-start(f32[1,2,1,128,2]{3,4,2,1,0:T(2,128)} %param.21) | copy-start | bytes 6148
  144.5 24.9 %all-to-all-start.3 = ((bf16[128,32,128]{2,1,0:T(8,128)(2,1)}), bf16[128,32,128]{2,1,0:T(8,128)(2,1)S(1)}, u32[]{:S(2)}, u32[]{:S(2)}) async-start(bf16[128,32,128]{2,1,0:T(8,128)(2,1)} %get-tuple-element.52), calls=%async_computation.3 | async-start | bytes 2097152 | tf_op jit(solution)/shard_map/all_to_all | solution.py:565
  152.4 5.4 collective-permute-start.1
  158.9 16.8 %copy-start.75 = (f32[1,768]{1,0:T(1,128)}, f32[1,768]{1,0:T(1,128)S(1)}, u32[]{:S(2)}) copy-start(f32[1,768]{1,0:T(1,128)S(1)} %squeeze.104.gain_ref) | copy-start | bytes 9220
  179.7 17.7 %all-to-all-start.4 = ((bf16[8,128,384]{2,1,0:T(8,128)(2,1)}), bf16[8,128,384]{2,1,0:T(8,128)(2,1)}, u32[]{:S(2)}, u32[]{:S(2)}) async-start(bf16[8,128,384]{2,1,0:T(8,128)(2,1)} %copy-done.51), calls=%async_computation.4 | async-start | bytes 1572864 | tf_op jit(solution)/shard_map/all_to_all | solution.py:569
  208.2 21.1 %copy-start.98 = (f32[8,96]{1,0:T(8,128)S(1)}, f32[8,96]{1,0:T(8,128)}, u32[]{:S(2)}) copy-start(f32[8,96]{1,0:T(8,128)} %get-tuple-element.93) | copy-start | bytes 9220
  208.2 12.9 %all-to-all-start.5 = ((bf16[8,128,128]{2,1,0:T(8,128)(2,1)}), bf16[8,128,128]{2,1,0:T(8,128)(2,1)}, u32[]{:S(2)}, u32[]{:S(2)}) async-start(bf16[8,128,128]{2,1,0:T(8,128)(2,1)} %bitcast.124), calls=%async_computation.5 | async-start | bytes 524288 | tf_op jit(solution)/shard_map/all_to_all | solution.py:569
  221.1 24.9 %all-to-all-start.7 = ((bf16[128,32,128]{2,1,0:T(8,128)(2,1)}), bf16[128,32,128]{2,1,0:T(8,128)(2,1)}, u32[]{:S(2)}, u32[]{:S(2)}) async-start(bf16[128,32,128]{2,1,0:T(8,128)(2,1)} %copy-done.20), calls=%async_computation.7 | async-start | bytes 2097152 | tf_op jit(solution)/shard_map/all_to_all | solution.py:565
  246.0 24.1 %all-to-all-start.6 = ((bf16[128,32,128]{2,1,0:T(8,128)(2,1)}), bf16[128,32,128]{2,1,0:T(8,128)(2,1)}, u32[]{:S(2)}, u32[]{:S(2)}) async-start(bf16[128,32,128]{2,1,0:T(8,128)(2,1)} %copy-done.42), calls=%async_computation.6 | async-start | bytes 2097152 | tf_op jit(solution)/shard_map/all_to_all | solution.py:565
  253.5 204.7 %all-gather.14.cloned.1.call-start = ((), (), s32[]{:S(2)}) async-start(), calls=%async_computation.19 | async-start | bytes 1769472 | tf_op jit(solution)/shard_map/all_gather | solution.py:641
  272.2 40.9 %copy-start.100 = (s32[256]{0:T(256)S(1)}, s32[256]{0:T(256)}, u32[]{:S(2)}) copy-start(s32[256]{0:T(256)} %get-tuple-element.97) | copy-start | bytes 3076
  305.6 24.2 %all-to-all-start.9 = ((bf16[128,32,128]{2,1,0:T(8,128)(2,1)}), bf16[128,32,128]{2,1,0:T(8,128)(2,1)}, u32[]{:S(2)}, u32[]{:S(2)}) async-start(bf16[128,32,128]{2,1,0:T(8,128)(2,1)} %copy-done.43), calls=%async_computation.9 | async-start | bytes 2097152 | tf_op jit(solution)/shard_map/all_to_all | solution.py:565
  339.7 11.9 %all-to-all-start.10 = ((bf16[8,128,128]{2,1,0:T(8,128)(2,1)}), bf16[8,128,128]{2,1,0:T(8,128)(2,1)}, u32[]{:S(2)}, u32[]{:S(2)}) async-start(bf16[8,128,128]{2,1,0:T(8,128)(2,1)} %copy-done.66), calls=%async_computation.10 | async-start | bytes 524288 | tf_op jit(solution)/shard_map/all_to_all | solution.py:569
  354.7 27.0 %copy-start.76 = (f32[1,768]{1,0:T(1,128)S(1)}, f32[1,768]{1,0:T(1,128)}, u32[]{:S(2)}) copy-start(f32[1,768]{1,0:T(1,128)} %copy-done.75) | copy-start | bytes 9220
  354.7 27.0 %copy-start.80 = (s32[2,128]{1,0:T(2,128)S(1)}, s32[2,128]{1,0:T(2,128)}, u32[]{:S(2)}) copy-start(s32[2,128]{1,0:T(2,128)} %copy-done.79) | copy-start | bytes 3076
  364.2 17.6 %all-to-all-start.11 = ((bf16[8,128,384]{2,1,0:T(8,128)(2,1)}), bf16[8,128,384]{2,1,0:T(8,128)(2,1)}, u32[]{:S(2)}, u32[]{:S(2)}) async-start(bf16[8,128,384]{2,1,0:T(8,128)(2,1)} %bitcast.125), calls=%async_computation.11 | async-start | bytes 1572864 | tf_op jit(solution)/shard_map/all_to_all | solution.py:569
  369.3 121.0 %all-gather.16.cloned.1.call-start = ((), (), s32[]{:S(2)}) async-start(), calls=%async_computation.20 | async-start | bytes 1769472 | tf_op jit(solution)/shard_map/all_gather | solution.py:649
  369.9 138.8 %all-gather.12.cloned.1.call-start = ((), (), s32[]{:S(2)}) async-start(), calls=%async_computation.18 | async-start | bytes 1769472 | tf_op jit(solution)/shard_map/all_gather | solution.py:661
  385.5 27.3 %copy-start.8 = (bf16[512,480]{1,0:T(8,128)(2,1)S(1)}, bf16[512,480]{1,0:T(8,128)(2,1)}, u32[]{:S(2)}) copy-start(bf16[512,480]{1,0:T(8,128)(2,1)} %copy-done.3) | copy-start | bytes 1474564
  385.5 27.3 %copy-start.13 = (bf16[480,512]{1,0:T(8,128)(2,1)S(1)}, bf16[480,512]{1,0:T(8,128)(2,1)}, u32[]{:S(2)}) copy-start(bf16[480,512]{1,0:T(8,128)(2,1)} %copy-done.9) | copy-start | bytes 1474564
  385.5 27.3 %copy-start.89 = (bf16[640,3072]{1,0:T(8,128)(2,1)S(1)}, bf16[640,3072]{1,0:T(8,128)(2,1)}, u32[]{:S(2)}) copy-start(bf16[640,3072]{1,0:T(8,128)(2,1)} %copy-done.88) | copy-start | bytes 11796484
  389.7 65.1 %copy-start.52 = (bf16[128,768]{1,0:T(8,128)(2,1)}, bf16[128,768]{1,0:T(8,128)(2,1)S(1)}, u32[]{:S(2)}) copy-start(bf16[128,768]{1,0:T(8,128)(2,1)S(1)} %get-tuple-element.69.dout_ref) | copy-start | bytes 589828
  430.9 26.2 %copy-start.19 = (bf16[640,3072]{1,0:T(8,128)(2,1)}, bf16[640,3072]{1,0:T(8,128)(2,1)S(1)}, u32[]{:S(2)}) copy-start(bf16[640,3072]{1,0:T(8,128)(2,1)S(1)} %get-tuple-element.85) | copy-start | bytes 11796484
  431.0 26.2 %copy-start.92 = (bf16[640,768]{1,0:T(8,128)(2,1)}, bf16[640,768]{1,0:T(8,128)(2,1)S(1)}, u32[]{:S(2)}) copy-start(bf16[640,768]{1,0:T(8,128)(2,1)S(1)} %get-tuple-element.89) | copy-start | bytes 2949124
  431.0 23.9 %copy-start.16 = (bf16[768,768]{1,0:T(8,128)(2,1)S(1)}, bf16[768,768]{1,0:T(8,128)(2,1)}, u32[]{:S(2)}) copy-start(bf16[768,768]{1,0:T(8,128)(2,1)} %copy-done.15) | copy-start | bytes 3538948
  431.0 23.9 %copy-start.36 = (f32[128,768]{1,0:T(8,128)S(1)}, f32[128,768]{1,0:T(8,128)}, u32[]{:S(2)}) copy-start(f32[128,768]{1,0:T(8,128)} %copy-done.34) | copy-start | bytes 1179652
  431.0 23.9 %copy-start.57 = (s32[128,2]{1,0:T(8,128)S(1)}, s32[128,2]{1,0:T(8,128)}, u32[]{:S(2)}) copy-start(s32[128,2]{1,0:T(8,128)} %squeeze.101.slots_ref) | copy-start | bytes 3076
  431.0 23.9 %copy-start.74 = (f32[1,768]{1,0:T(1,128)S(1)}, f32[1,768]{1,0:T(1,128)}, u32[]{:S(2)}) copy-start(f32[1,768]{1,0:T(1,128)} %copy-done.73) | copy-start | bytes 9220
  458.1 7.9 %copy-start.99 = (s32[4,512]{1,0:T(4,128)S(1)}, s32[4,512]{1,0:T(4,128)}, u32[]{:S(2)}) copy-start(s32[4,512]{1,0:T(4,128)} %get-tuple-element.126) | copy-start | bytes 24580
  458.1 17.8 %copy-start.72 = (bf16[256,256]{1,0:T(8,128)(2,1)S(1)}, bf16[256,256]{1,0:T(8,128)(2,1)}, u32[]{:S(2)}) copy-start(bf16[256,256]{1,0:T(8,128)(2,1)} %fusion.23.flip_ref) | copy-start | bytes 393220
  458.1 17.8 %copy-start.87 = (bf16[1024,384]{1,0:T(8,128)(2,1)S(1)}, bf16[1024,384]{1,0:T(8,128)(2,1)}, u32[]{:S(2)}) copy-start(bf16[1024,384]{1,0:T(8,128)(2,1)} %copy-done.86) | copy-start | bytes 2359300
  461.6 14.4 %all-to-all-start.14 = ((bf16[8,128,128]{2,1,0:T(8,128)(2,1)}), bf16[8,128,128]{2,1,0:T(8,128)(2,1)S(1)}, u32[]{:S(2)}, u32[]{:S(2)}) async-start(bf16[8,128,128]{2,1,0:T(8,128)(2,1)} %get-tuple-element.70), calls=%async_computation.14 | async-start | bytes 524288 | tf_op jit(solution)/shard_map/all_to_all | solution.py:569
  478.2 12.1 %copy-start.48 = (bf16[1024,128]{1,0:T(8,128)(2,1)S(1)}, bf16[1024,128]{1,0:T(8,128)(2,1)}, u32[]{:S(2)}) copy-start(bf16[1024,128]{1,0:T(8,128)(2,1)} %copy-done.47) | copy-start | bytes 786436
  485.8 17.0 %all-to-all-start.15 = ((bf16[8,128,384]{2,1,0:T(8,128)(2,1)}), bf16[8,128,384]{2,1,0:T(8,128)(2,1)}, u32[]{:S(2)}, u32[]{:S(2)}) async-start(bf16[8,128,384]{2,1,0:T(8,128)(2,1)} %bitcast.38), calls=%async_computation.15 | async-start | bytes 1572864 | tf_op jit(solution)/shard_map/all_to_all | solution.py:569
  493.9 8.8 %copy-start.2 = (bf16[768,2304]{1,0:T(8,128)(2,1)S(1)}, bf16[768,2304]{1,0:T(8,128)(2,1)}, u32[]{:S(2)}) copy-start(bf16[768,2304]{1,0:T(8,128)(2,1)} %get-tuple-element.99.wqkv_ref) | copy-start | bytes 10616836
  512.1 32.0 %copy-start.41 = (bf16[128,32,128]{2,1,0:T(8,128)(2,1)S(1)}, bf16[128,32,128]{2,1,0:T(8,128)(2,1)}, u32[]{:S(2)}) copy-start(bf16[128,32,128]{2,1,0:T(8,128)(2,1)} %copy-done.40) | copy-start | bytes 3145732
  512.1 29.5 %all-to-all-start.16 = ((bf16[16,136,384]{2,1,0:T(8,128)(2,1)}), bf16[16,136,384]{2,1,0:T(8,128)(2,1)}, u32[]{:S(2)}, u32[]{:S(2)}) async-start(bf16[16,136,384]{2,1,0:T(8,128)(2,1)} %maximum_maximum_fusion), calls=%async_computation.16 | async-start | bytes 3342336 | tf_op jit(solution)/shard_map/all_to_all | solution.py:694
  518.3 103.3 %all-gather.24.cloned.1.call-start = ((), (), s32[]{:S(2)}) async-start(), calls=%async_computation.24 | async-start | bytes 2396160 | tf_op jit(solution)/shard_map/all_gather | solution.py:711
  518.4 50.2 %copy-start.14 = (bf16[480,512]{1,0:T(8,128)(2,1)S(1)}, bf16[480,512]{1,0:T(8,128)(2,1)}, u32[]{:S(2)}) copy-start(bf16[480,512]{1,0:T(8,128)(2,1)} %copy-done.9) | copy-start | bytes 1474564
  518.4 50.2 %copy-start.39 = (f32[128,768]{1,0:T(8,128)S(1)}, f32[128,768]{1,0:T(8,128)}, u32[]{:S(2)}) copy-start(f32[128,768]{1,0:T(8,128)} %copy-done.37) | copy-start | bytes 1179652
  518.4 50.2 %copy-start.59 = (s32[128,2]{1,0:T(8,128)S(1)}, s32[128,2]{1,0:T(8,128)}, u32[]{:S(2)}) copy-start(s32[128,2]{1,0:T(8,128)} %squeeze.111.slots_ref) | copy-start | bytes 3076
  518.4 50.2 %copy-start.61 = (f32[128,2]{1,0:T(8,128)S(1)}, f32[128,2]{1,0:T(8,128)}, u32[]{:S(2)}) copy-start(f32[128,2]{1,0:T(8,128)} %get-tuple-element.109.gates_ref) | copy-start | bytes 3076
  543.4 26.2 %copy-start.31 = (bf16[128,768]{1,0:T(8,128)(2,1)S(1)}, bf16[128,768]{1,0:T(8,128)(2,1)}, u32[]{:S(2)}) copy-start(bf16[128,768]{1,0:T(8,128)(2,1)} %copy-done.28) | copy-start | bytes 589828
  569.6 5.7 collective-permute-start.2
  576.1 15.5 %copy-start.53 = (bf16[128,768]{1,0:T(8,128)(2,1)S(1)}, bf16[128,768]{1,0:T(8,128)(2,1)}, u32[]{:S(2)}) copy-start(bf16[128,768]{1,0:T(8,128)(2,1)} %copy-done.52) | copy-start | bytes 589828
  576.1 15.5 %copy-start.70 = (bf16[128,768]{1,0:T(8,128)(2,1)S(1)}, bf16[128,768]{1,0:T(8,128)(2,1)}, u32[]{:S(2)}) copy-start(bf16[128,768]{1,0:T(8,128)(2,1)} %copy-done.69) | copy-start | bytes 589828
  584.9 17.4 %copy-start.22 = (bf16[640,768]{1,0:T(8,128)(2,1)S(1)}, bf16[640,768]{1,0:T(8,128)(2,1)}, u32[]{:S(2)}) copy-start(bf16[640,768]{1,0:T(8,128)(2,1)} %copy-done.21) | copy-start | bytes 2949124
  584.9 17.4 %copy-start.24 = (bf16[640,768]{1,0:T(8,128)(2,1)S(1)}, bf16[640,768]{1,0:T(8,128)(2,1)}, u32[]{:S(2)}) copy-start(bf16[640,768]{1,0:T(8,128)(2,1)} %copy-done.23) | copy-start | bytes 2949124
  584.9 11.3 %collective-permute-start.4 = (bf16[96,384]{1,0:T(8,128)(2,1)S(1)}, bf16[96,384]{1,0:T(8,128)(2,1)S(1)}, u32[]{:S(2)}, u32[]{:S(2)}) collective-permute-start(bf16[96,384]{1,0:T(8,128)(2,1)S(1)} %slice.194), channel_id=1, source_target_pairs={{0,0},{1,8},{2,16},{3,24},{4,32},{5,40},{6,48},{7,56},{8,1},{9,9},... | collective-permute-start | bytes 221192 | tf_op jit(solution)/shard_map/ppermute | solution.py:698
  591.6 19.2 %collective-permute-start.3 = (bf16[128,768]{1,0:T(8,128)(2,1)S(1)}, bf16[128,768]{1,0:T(8,128)(2,1)S(1)}, u32[]{:S(2)}, u32[]{:S(2)}) collective-permute-start(bf16[128,768]{1,0:T(8,128)(2,1)S(1)} %get-tuple-element.106), channel_id=1, source_target_pairs={{0,64},{64,0},{1,65},{65,1},{2,66},{66,2},{3,67},{67,3},{4,68},{68... | collective-permute-start | bytes 589832 | tf_op jit(solution)/shard_map/ppermute | solution.py:573
  597.0 15.5 %all-to-all-start.17 = ((bf16[8,96,384]{2,1,0:T(8,128)(2,1)}), bf16[8,96,384]{2,1,0:T(8,128)(2,1)S(1)}, u32[]{:S(2)}, u32[]{:S(2)}) async-start(bf16[8,96,384]{2,1,0:T(8,128)(2,1)} %broadcast_in_dim.25), calls=%async_computation.17 | async-start | bytes 1179648 | tf_op jit(solution)/shard_map/all_to_all | solution.py:699
  (70 other events, 151.0 us)
Sparse Core Ops, SparseCore 0:
  10.3 38.2 all-gather.17
  50.3 36.6 all-gather.19
  88.8 57.2 all-gather.21
  255.7 26.2 all-gather.13
  371.5 24.2 all-gather.15
  458.1 24.9 all-gather.11
  544.2 77.3 all-gather.23

commit v2 on v1

v2 whole, which is shorter than its diff:
```python
from functools import partial

import jax
import jax.numpy as jnp
from jax import lax
from jax.experimental import pallas as pl
from jax.experimental.pallas import tpu as pltpu
from jax.sharding import PartitionSpec as P

F32 = jnp.float32
BF = jnp.bfloat16
D = 768
H = 12
HD = 64
FF = 3072
SEQ = 1024
TOK = 128
BLOCK = 256
RELB = 32
EXPERTS = 64
CAP = 5
LANES = 128
COLS = D // LANES
CHUNK = 32
GROUP = 16
SLOTS = EXPERTS * CAP
GROUPS_ALL = 2 * EXPERTS // GROUP
ROWS = 2 * EXPERTS * CAP
PAIRS = H // 2
EPS = 1e-05
EVERYONE = ("section", "rep", "shard")
HIGHEST = lax.Precision.HIGHEST
MIB = 1 << 20


def mm(a, b):
    return lax.dot_general(a, b, (((1,), (0,)), ((), ())), preferred_element_type=F32)


def mm_nt(a, b):
    return lax.dot_general(a, b, (((1,), (1,)), ((), ())), preferred_element_type=F32)


def mm_tn(a, b):
    return lax.dot_general(a, b, (((0,), (0,)), ((), ())), preferred_element_type=F32)


def call(kernel, outs, name, flops, moved, vmem=32, **more):
    run = pl.pallas_call(
        kernel,
        out_shape=outs,
        name=name,
        compiler_params=pltpu.CompilerParams(vmem_limit_bytes=vmem * MIB),
        cost_estimate=pl.CostEstimate(flops=flops, bytes_accessed=moved, transcendentals=0),
        **more,
    )

    def placed(*operands):
        return run(*(pltpu.with_memory_space_constraint(x, pltpu.HBM) if x.ndim > 1 else x for x in operands))

    return placed


def shape(*dims, dtype=BF):
    return pltpu.HBM(dims, dtype)


VMEM = pl.BlockSpec(memory_space=pltpu.VMEM)
ANYWHERE = pl.BlockSpec(memory_space=pl.ANY)


def pack_tables():
    row = jnp.arange(GROUP * CAP * COLS, dtype=jnp.int32)[:, None]
    col = jnp.arange(GROUP * CHUNK, dtype=jnp.int32)[None, :]
    block, inside = row // (GROUP * CAP), row % (GROUP * CAP)
    place = (inside // CAP) * CHUNK + block * CAP + inside % CAP
    return (place == col).astype(BF)


def unpack(chunks, table, target):
    size = GROUP * CAP
    for g in range(0, chunks.shape[0] // GROUP, 2):
        raw = [chunks[k * GROUP : (k + 1) * GROUP].reshape(GROUP * CHUNK, LANES) for k in (g, g + 1)]
        rows = mm(table, jnp.concatenate(raw, axis=1)).astype(BF)
        for k in range(2):
            for c in range(COLS):
                target[(g + k) * size : (g + k + 1) * size, c * LANES : (c + 1) * LANES] = rows[
                    c * size : (c + 1) * size, k * LANES : (k + 1) * LANES
                ]


def pack(rows, table_t, target, first):
    size = GROUP * CAP
    for g in range(0, rows.shape[0] // size, 2):
        stacked = jnp.concatenate(
            [
                jnp.concatenate(
                    [rows[k * size : (k + 1) * size, c * LANES : (c + 1) * LANES] for k in (g, g + 1)], axis=1
                )
                for c in range(COLS)
            ],
            axis=0,
        )
        both = mm(table_t, stacked).astype(BF)
        for k in range(2):
            chunk = both[:, k * LANES : (k + 1) * LANES].reshape(GROUP, CHUNK, LANES)
            target[first + (g + k) * GROUP : first + (g + k + 1) * GROUP] = chunk


def pack_for_layer(rows, table_t, target, layer):
    pack(rows, table_t, target, layer * EXPERTS)
    other = (1 - layer) * EXPERTS
    target[other : other + EXPERTS] = jnp.zeros((EXPERTS, CHUNK, LANES), BF)


def slots_by_token(slot_rows):
    places = lax.broadcasted_iota(jnp.int32, (SLOTS, TOK), 0)
    return [jnp.where(places == slot_rows[k : k + 1, :], 1.0, 0.0).astype(BF) for k in range(2)]


def tokens_by_slot(slot_cols):
    places = lax.broadcasted_iota(jnp.int32, (TOK, SLOTS), 1)
    return [jnp.where(places == slot_cols[:, k : k + 1], 1.0, 0.0).astype(BF) for k in range(2)]


def norm_of(hidden, gain):
    scaling = lax.rsqrt(jnp.mean(hidden * hidden, axis=-1, keepdims=True) + EPS)
    return hidden * scaling * gain, scaling


def norm_back(hidden, scaling, gain, grad):
    gain_grad = jnp.sum(grad * hidden * scaling, axis=0, keepdims=True)
    weighted = grad * gain
    inner = jnp.mean(weighted * hidden, axis=-1, keepdims=True)
    return weighted * scaling - hidden * (scaling * scaling * scaling * inner), gain_grad


def bias_tiles_kernel(line_ref, out_ref):
    for h in range(2):
        for delta in range(4):
            line = jnp.broadcast_to(line_ref[h * 4 + delta : h * 4 + delta + 1, :], (BLOCK, 2 * BLOCK))
            turned = pltpu.roll(line, 0, 1, stride=1, stride_axis=0)
            out_ref[h * 4 + delta] = turned[:, :BLOCK].astype(BF)


def bias_tiles(table):
    m = jnp.arange(2 * BLOCK, dtype=jnp.int32)
    ahead = jnp.where(m < BLOCK, m, m - 2 * BLOCK)
    distance = jnp.arange(4, dtype=jnp.int32)[:, None] * BLOCK - ahead[None, :]
    bucket = jnp.clip((distance + BLOCK) * RELB // (SEQ + BLOCK), 0, RELB - 1)
    onehot = (bucket[..., None] == jnp.arange(RELB, dtype=jnp.int32)).astype(F32)
    lines = jnp.einsum("dmb,bh->hdm", onehot, table, precision=HIGHEST).reshape(8, 2 * BLOCK)
    return call(bias_tiles_kernel, shape(8, BLOCK, BLOCK), "bias_tiles", 0, 1 << 20)(lines)


def head_mask(h, rows):
    lane = lax.broadcasted_iota(jnp.int32, (rows, LANES), 1)
    return (lane < HD) if h == 0 else (lane >= HD)


ATT_STEP = 128


def weight_blocks():
    return [(i, h) for i in range(4) for h in range(2)]


def weight_copy(i, h, vmem, hbm, sems, into):
    rows, keys = pl.ds(i * BLOCK, BLOCK), pl.ds(0, (i + 1) * BLOCK)
    ends = vmem.at[h, rows, keys], hbm.at[h, rows, keys]
    return pltpu.make_async_copy(*(ends if into else ends[::-1]), sems.at[h, i])


def attention_kernel(qkv_ref, bias_ref, ctx_ref, weights_hbm, held, sems):
    step = ATT_STEP
    for i in range(4):
        keys = (i + 1) * BLOCK
        key = qkv_ref[0:keys, LANES : 2 * LANES]
        value = qkv_ref[0:keys, 2 * LANES : 3 * LANES]
        for part in range(BLOCK // step):
            first = i * BLOCK + part * step
            query = qkv_ref[first : first + step, 0:LANES] * jnp.asarray(HD**-0.5, BF)
            mixed = []
            for h in range(2):
                mask = head_mask(h, step)
                own = jnp.where(mask, query, jnp.zeros_like(query))
                scores = mm_nt(own, key)
                offset = jnp.concatenate(
                    [bias_ref[h * 4 + i - b, part * step : (part + 1) * step, :] for b in range(i + 1)], axis=1
                ).astype(F32)
                scores = scores + offset
                top = jnp.max(scores, axis=-1, keepdims=True)
                terms = jnp.exp(scores - top)
                total = jnp.sum(terms, axis=-1, keepdims=True)
                weights = (terms * (1.0 / total)).astype(BF)
                held[h, first : first + step, 0:keys] = weights
                mixed.append(mm(weights, value))
            ctx_ref[first : first + step, :] = jnp.where(head_mask(0, step), mixed[0], mixed[1]).astype(BF)
        for h in range(2):
            weight_copy(i, h, held, weights_hbm, sems, True).start()
    for i, h in weight_blocks():
        weight_copy(i, h, held, weights_hbm, sems, True).wait()


def attention(qkv, tiles):
    return call(
        attention_kernel,
        (shape(SEQ, LANES), shape(2, SEQ, SEQ)),
        "attention",
        2 * 2 * 2 * SEQ * SEQ * LANES,
        8 << 20,
        in_specs=[VMEM] * 2,
        out_specs=(VMEM, ANYWHERE),
        scratch_shapes=[pltpu.VMEM((2, SEQ, SEQ), BF), pltpu.SemaphoreType.DMA((2, 4))],
    )(qkv, tiles)


def attention_back_kernel(qkv_ref, weights_hbm, dout_ref, flip_ref, dproj_ref, diag_ref, dkey, dvalue, tiles, held, sems):
    step = ATT_STEP
    for i, h in weight_blocks():
        weight_copy(i, h, held, weights_hbm, sems, False).start()
    dkey[...] = jnp.zeros_like(dkey)
    dvalue[...] = jnp.zeros_like(dvalue)
    for i in range(4):
        keys = (i + 1) * BLOCK
        key = qkv_ref[0:keys, LANES : 2 * LANES]
        value = qkv_ref[0:keys, 2 * LANES : 3 * LANES]
        for h in range(2):
            weight_copy(i, h, held, weights_hbm, sems, False).wait()
        for part in range(BLOCK // step):
            first = i * BLOCK + part * step
            rows = slice(part * step, (part + 1) * step)
            query = qkv_ref[first : first + step, 0:LANES]
            dout = dout_ref[first : first + step, :]
            query_t = query.astype(F32).T.astype(BF)
            dout_t = dout.astype(F32).T.astype(BF)
            moved = []
            for h in range(2):
                own = jnp.where(head_mask(h, step), dout, jnp.zeros_like(dout))
                low = held[h, first : first + step, 0:keys]
                weights = low.astype(F32)
                dweights = mm_nt(own, value)
                delta = jnp.sum(weights * dweights, axis=-1, keepdims=True)
                dscores = weights * (dweights - delta)
                for b in range(i + 1):
                    tile = dscores[:, b * BLOCK : (b + 1) * BLOCK]
                    n = h * 4 + i - b
                    tiles[n, rows, :] = tile if b == 0 else tiles[n, rows, :] + tile
                dlow = dscores.astype(BF)
                moved.append(mm(dlow, key))
                head = slice(h * HD, (h + 1) * HD)
                dkey[head, 0:keys] += mm(query_t[head], dlow)
                dvalue[head, 0:keys] += mm(dout_t[head], low)
            dquery = jnp.where(head_mask(0, step), moved[0], moved[1]) * HD**-0.5
            dproj_ref[first : first + step, 0:LANES] = dquery.astype(BF)
    dproj_ref[:, LANES : 2 * LANES] = (dkey[...] * HD**-0.5).T.astype(BF)
    dproj_ref[:, 2 * LANES : 3 * LANES] = dvalue[...].T.astype(BF)
    for n in range(8):
        tile = tiles[n]
        high = tile.astype(BF)
        rest = (tile - high.astype(F32)).astype(BF)
        flipped = mm(high, flip_ref[...]) + mm(rest, flip_ref[...])
        wide = jnp.concatenate([flipped, jnp.zeros_like(flipped)], axis=1)
        turned = pltpu.roll(wide, 0, 1, stride=1, stride_axis=0)
        diag_ref[n : n + 1, :] = jnp.sum(turned, axis=0, keepdims=True)


def attention_back(qkv, weights, dout):
    at = jnp.arange(BLOCK, dtype=jnp.int32)
    flip = (at[:, None] + at[None, :] == BLOCK - 1).astype(BF)
    return call(
        attention_back_kernel,
        (shape(SEQ, 3 * LANES), shape(8, 2 * BLOCK, dtype=F32)),
        "attention_back",
        2 * 4 * 2 * SEQ * SEQ * LANES,
        8 << 20,
        in_specs=[VMEM, ANYWHERE, VMEM, VMEM],
        out_specs=(VMEM, VMEM),
        scratch_shapes=[
            pltpu.VMEM((LANES, SEQ), F32),
            pltpu.VMEM((LANES, SEQ), F32),
            pltpu.VMEM((8, BLOCK, BLOCK), F32),
            pltpu.VMEM((2, SEQ, SEQ), BF),
            pltpu.SemaphoreType.DMA((2, 4)),
        ],
    )(qkv, weights, dout, flip)


def bias_grad(diag):
    m = jnp.arange(2 * BLOCK, dtype=jnp.int32)
    distance = jnp.arange(4, dtype=jnp.int32)[:, None] * BLOCK + m[None, :] - (BLOCK - 1)
    bucket = jnp.clip((distance + BLOCK) * RELB // (SEQ + BLOCK), 0, RELB - 1)
    onehot = (bucket[..., None] == jnp.arange(RELB, dtype=jnp.int32)).astype(F32)
    return jnp.einsum("hdm,dmb->bh", diag.reshape(2, 4, 2 * BLOCK), onehot, precision=HIGHEST)


def middle_kernel(
    layer, ctx_ref, wao_hbm, hidden_ref, gain_ref, slots_ref, table_ref, middle_ref, out_ref, context_ref, wao_ref, sem
):
    load = pltpu.make_async_copy(wao_hbm.at[layer], wao_ref, sem)
    load.start()
    context = jnp.concatenate([ctx_ref[g] for g in range(PAIRS)], axis=1)
    context_ref[...] = context
    load.wait()
    middle = hidden_ref[...].astype(F32) + mm(context, wao_ref[...])
    middle_ref[...] = middle
    normed = norm_of(middle, gain_ref[layer])[0].astype(BF)
    first, second = slots_by_token(slots_ref[layer])
    rows = mm(first + second, normed).astype(BF)
    pack_for_layer(rows, table_ref[...], out_ref, layer)


def weight_space(columns):
    return [pltpu.VMEM((D, columns), BF), pltpu.SemaphoreType.DMA]


def middle_part(layer, ctx, wao, hidden, gain, slot_rows, table_t):
    return call(
        partial(middle_kernel, layer),
        (shape(TOK, D, dtype=F32), shape(2 * EXPERTS, CHUNK, LANES), shape(TOK, D)),
        "middle",
        2 * TOK * D * D + 2 * SLOTS * TOK * D * 5,
        4 << 20,
        in_specs=[VMEM, ANYWHERE, VMEM, VMEM, VMEM, VMEM],
        scratch_shapes=weight_space(D),
    )(ctx, wao, hidden, gain, slot_rows, table_t)


def combined(layer, back_ref, middle_ref, slots_ref, gates_ref, table_ref, rows):
    unpack(back_ref.at[layer * EXPERTS : (layer + 1) * EXPERTS], table_ref[...], rows)
    picks = tokens_by_slot(slots_ref[layer])
    gates = gates_ref[layer]
    total = middle_ref[...]
    for k in range(2):
        total = total + gates[:, k : k + 1] * mm(picks[k], rows[...])
    return total.astype(BF)


def combine_kernel(layer, back_ref, middle_ref, slots_ref, gates_ref, table_ref, out_ref, rows):
    out_ref[...] = combined(layer, back_ref, middle_ref, slots_ref, gates_ref, table_ref, rows)


def combine(layer, back, middle, slot_cols, gates, table):
    return call(
        partial(combine_kernel, layer),
        shape(TOK, D),
        "combine",
        2 * TOK * SLOTS * D * 6,
        4 << 20,
        in_specs=[VMEM, VMEM, VMEM, VMEM, VMEM],
        scratch_shapes=[pltpu.VMEM((SLOTS, D), BF)],
    )(back, middle, slot_cols, gates, table)


def send_grads(layer, dout, slot_rows, gates, table_t, out_ref):
    first, second = slots_by_token(slot_rows)
    wide = dout.astype(F32)
    rows = mm(first, (wide * gates[:, 0:1]).astype(BF)) + mm(second, (wide * gates[:, 1:2]).astype(BF))
    pack_for_layer(rows.astype(BF), table_t, out_ref, layer)


def grad_rows_kernel(dout_ref, slots_ref, gates_ref, table_ref, out_ref):
    for m in range(2):
        first, second = slots_by_token(slots_ref[m])
        gates = gates_ref[m]
        wide = dout_ref[m].astype(F32)
        rows = mm(first, (wide * gates[:, 0:1]).astype(BF)) + mm(second, (wide * gates[:, 1:2]).astype(BF))
        pack(rows.astype(BF), table_ref[...], out_ref.at[:, m], 0)


def grad_rows(dout, slot_rows, gates, table_t):
    return call(
        grad_rows_kernel,
        shape(EXPERTS, 2, CHUNK, LANES),
        "grad_rows",
        4 * TOK * SLOTS * D * 6,
        2 << 20,
    )(dout, slot_rows, gates, table_t)


def middle_back_kernel(
    layer, back_ref, slots_ref, table_ref, dout_ref, middle_ref, gain_ref, wao_hbm, dmid_ref, branch_ref, send_ref, dgain_ref,
    rows, wao_ref, sem,
):
    load = pltpu.make_async_copy(wao_hbm.at[layer], wao_ref, sem)
    load.start()
    unpack(back_ref.at[layer * EXPERTS : (layer + 1) * EXPERTS], table_ref[...], rows)
    first, second = tokens_by_slot(slots_ref[layer])
    dnormed = mm(first + second, rows[...])
    middle = middle_ref[...]
    gain = gain_ref[layer]
    scaling = lax.rsqrt(jnp.mean(middle * middle, axis=-1, keepdims=True) + EPS)
    moved, dgain = norm_back(middle, scaling, gain, dnormed)
    dgain_ref[...] = dgain
    dmid = dout_ref[...].astype(F32) + moved
    dmid_ref[...] = dmid
    branch = dmid.astype(BF)
    branch_ref[...] = branch
    load.wait()
    dcontext = mm_nt(branch, wao_ref[...]).astype(BF)
    for g in range(PAIRS):
        send_ref[g] = dcontext[:, g * LANES : (g + 1) * LANES]
    send_ref[PAIRS:8] = jnp.zeros((8 - PAIRS, TOK, LANES), BF)


def middle_back(layer, back, slot_cols, table, dout, middle, gain, wao):
    return call(
        partial(middle_back_kernel, layer),
        (shape(TOK, D, dtype=F32), shape(TOK, D), shape(8, TOK, LANES), shape(1, D, dtype=F32)),
        "middle_back",
        2 * TOK * D * D + 2 * TOK * SLOTS * D * 5,
        4 << 20,
        in_specs=[VMEM] * 6 + [ANYWHERE],
        scratch_shapes=[pltpu.VMEM((SLOTS, D), BF)] + weight_space(D),
    )(back, slot_cols, table, dout, middle, gain, wao)


def hidden_grad(layer, back_ref, wqkv_hbm, hidden_ref, gain_ref, dmid_ref, wqkv_ref, sem):
    load = pltpu.make_async_copy(wqkv_hbm.at[layer], wqkv_ref, sem)
    load.start()
    parts = [
        back_ref[g, :, part * LANES : (part + 1) * LANES] for part in range(3) for g in range(PAIRS)
    ]
    hidden = hidden_ref[...].astype(F32)
    scaling = lax.rsqrt(jnp.mean(hidden * hidden, axis=-1, keepdims=True) + EPS)
    load.wait()
    dnormed = mm_nt(jnp.concatenate(parts, axis=1), wqkv_ref[...])
    moved, _ = norm_back(hidden, scaling, gain_ref[layer], dnormed)
    return (dmid_ref[...] + moved).astype(BF)


def hidden_back_kernel(layer, back_ref, wqkv_hbm, hidden_ref, gain_ref, dmid_ref, dh_ref, wqkv_ref, sem):
    dh_ref[...] = hidden_grad(layer, back_ref, wqkv_hbm, hidden_ref, gain_ref, dmid_ref, wqkv_ref, sem)


def hidden_back_send_kernel(
    layer, back_ref, wqkv_hbm, hidden_ref, gain_ref, dmid_ref, slots_ref, gates_ref, table_ref, dh_ref, out_ref, wqkv_ref, sem
):
    dh = hidden_grad(layer, back_ref, wqkv_hbm, hidden_ref, gain_ref, dmid_ref, wqkv_ref, sem)
    dh_ref[...] = dh
    send_grads(layer - 1, dh, slots_ref[layer - 1], gates_ref[layer - 1], table_ref[...], out_ref)


def hidden_back(layer, back, wqkv, hidden, gain, dmid):
    return call(
        partial(hidden_back_kernel, layer),
        shape(TOK, D),
        "hidden_back",
        2 * TOK * D * 3 * D,
        5 << 20,
        in_specs=[VMEM, ANYWHERE, VMEM, VMEM, VMEM],
        scratch_shapes=weight_space(3 * D),
    )(back, wqkv, hidden, gain, dmid)


def hidden_back_send(layer, back, wqkv, hidden, gain, dmid, slot_rows, gates, table_t):
    return call(
        partial(hidden_back_send_kernel, layer),
        (shape(TOK, D), shape(2 * EXPERTS, CHUNK, LANES)),
        "hidden_back_send",
        2 * TOK * D * 3 * D,
        6 << 20,
        in_specs=[VMEM, ANYWHERE] + [VMEM] * 6,
        scratch_shapes=weight_space(3 * D),
    )(back, wqkv, hidden, gain, dmid, slot_rows, gates, table_t)


FF_STEP = 1024
ROW_STEP = 320
CHUNKS = (2 * EXPERTS, CHUNK, LANES)


def gelu_parts(up):
    phi = 0.5 + 0.5 * lax.erf(up * 0.5**0.5)
    return up * phi, phi + up * (jnp.exp(up * up * -0.5) * 0.3989422804014327)


def row_blocks():
    return [slice(r, r + ROW_STEP) for r in range(0, ROWS, ROW_STEP)]


def over_hidden_units(one, weights, buffers, targets, sems):
    def copy(f, slot, k):
        columns = pl.ds(pl.multiple_of(f * FF_STEP, FF_STEP), FF_STEP)
        return pltpu.make_async_copy(buffers[k].at[slot], targets[k].at[:, columns], sems.at[slot, k])

    def step(f, carry):
        slot = lax.rem(f, 2)

        @pl.when(f >= 2)
        def _():
            for k in range(len(buffers)):
                copy(f - 2, slot, k).wait()

        for load in weights(f):
            load.wait()
        one(pl.ds(pl.multiple_of(f * FF_STEP, FF_STEP), FF_STEP), [b.at[slot] for b in buffers])
        for k in range(len(buffers)):
            copy(f, slot, k).start()
        return carry

    last = FF // FF_STEP
    lax.fori_loop(0, last, step, 0)
    for f in range(last - 2, last):
        for k in range(len(buffers)):
            copy(f, f % 2, k).wait()


def start_weights(win_hbm, wout_hbm, win_ref, wout_ref, sems, slope_hbm=None, slope=None):
    def copies(f):
        units = pl.ds(pl.multiple_of(f * FF_STEP, FF_STEP), FF_STEP)
        loads = [
            pltpu.make_async_copy(win_hbm.at[:, units], win_ref.at[:, units], sems.at[f, 0]),
            pltpu.make_async_copy(wout_hbm.at[units, :], wout_ref.at[units, :], sems.at[f, 1]),
        ]
        if slope is not None:
            loads.append(pltpu.make_async_copy(slope_hbm.at[:, units], slope.at[:, units], sems.at[f, 2]))
        return loads

    for f in range(FF // FF_STEP):
        for load in copies(f):
            load.start()
    return copies


def expert_space():
    return [
        pltpu.VMEM((D, FF), BF),
        pltpu.VMEM((FF, D), BF),
        pltpu.SemaphoreType.DMA((FF // FF_STEP, 3)),
    ]


def held_blocks():
    return pltpu.VMEM((2, ROWS, FF_STEP), BF)


def expert_forward_kernel(
    in_ref, win_hbm, wout_hbm, table_ref, table_t_ref, x_ref, act_hbm, slope_hbm, out_ref,
    win_ref, wout_ref, weight_sems, total, act_held, slope_held, sems,
):
    weights = start_weights(win_hbm, wout_hbm, win_ref, wout_ref, weight_sems)
    unpack(in_ref, table_ref[...], x_ref)
    total[...] = jnp.zeros_like(total)

    def one(columns, held):
        blocks = row_blocks()
        ups = mm(x_ref[blocks[0], :], win_ref[:, columns])
        for n, rows in enumerate(blocks):
            up = ups
            if n + 1 < len(blocks):
                ups = mm(x_ref[blocks[n + 1], :], win_ref[:, columns])
            act, slope = gelu_parts(up)
            act = act.astype(BF)
            held[0][rows, :] = act
            held[1][rows, :] = slope.astype(BF)
            total[rows, :] += mm(act, wout_ref[columns, :])

    over_hidden_units(one, weights, [act_held, slope_held], [act_hbm, slope_hbm], sems)
    pack(total[...].astype(BF), table_t_ref[...], out_ref, 0)


def expert_forward(arrived, first, second, table, table_t):
    return call(
        expert_forward_kernel,
        (shape(ROWS, D), shape(ROWS, FF), shape(ROWS, FF), shape(*CHUNKS)),
        "expert_forward",
        4 * ROWS * D * FF,
        20 << 20,
        vmem=40,
        in_specs=[VMEM, ANYWHERE, ANYWHERE, VMEM, VMEM],
        out_specs=(VMEM, ANYWHERE, ANYWHERE, VMEM),
        scratch_shapes=expert_space()
        + [pltpu.VMEM((ROWS, D), F32), held_blocks(), held_blocks(), pltpu.SemaphoreType.DMA((2, 2))],
    )(arrived, first, second, table, table_t)


def expert_back_kernel(
    in_ref, win_hbm, wout_hbm, slope_hbm, table_ref, table_t_ref, grad_ref, dup_hbm, out_ref,
    win_ref, wout_ref, weight_sems, total, slope, dup_held, sems,
):
    weights = start_weights(win_hbm, wout_hbm, win_ref, wout_ref, weight_sems, slope_hbm, slope)
    unpack(in_ref, table_ref[...], grad_ref)
    total[...] = jnp.zeros_like(total)

    def one(columns, held):
        blocks = row_blocks()
        dacts = mm_nt(grad_ref[blocks[0], :], wout_ref[columns, :])
        for n, rows in enumerate(blocks):
            dact = dacts
            if n + 1 < len(blocks):
                dacts = mm_nt(grad_ref[blocks[n + 1], :], wout_ref[columns, :])
            dup = (dact * slope[rows, columns].astype(F32)).astype(BF)
            held[0][rows, :] = dup
            total[rows, :] += mm_nt(dup, win_ref[:, columns])

    over_hidden_units(one, weights, [dup_held], [dup_hbm], sems)
    pack(total[...].astype(BF), table_t_ref[...], out_ref, 0)


def expert_back(arrived, first, second, slope, table, table_t):
    return call(
        expert_back_kernel,
        (shape(ROWS, D), shape(ROWS, FF), shape(*CHUNKS)),
        "expert_back",
        4 * ROWS * D * FF,
        20 << 20,
        vmem=40,
        in_specs=[VMEM, ANYWHERE, ANYWHERE, ANYWHERE, VMEM, VMEM],
        out_specs=(VMEM, ANYWHERE, VMEM),
        scratch_shapes=expert_space()
        + [
            pltpu.VMEM((ROWS, D), F32),
            pltpu.VMEM((ROWS, FF), BF),
            held_blocks(),
            pltpu.SemaphoreType.DMA((2, 1)),
        ],
    )(arrived, first, second, slope, table, table_t)


def expert_both_kernel(
    in_ref, gin_ref, win_hbm, wout_hbm, table_ref, table_t_ref, x_ref, grad_ref, act_hbm, dup_hbm, out_ref, back_ref,
    win_ref, wout_ref, weight_sems, total, dtotal, act_held, dup_held, sems,
):
    weights = start_weights(win_hbm, wout_hbm, win_ref, wout_ref, weight_sems)
    unpack(in_ref, table_ref[...], x_ref)
    for m in range(2):
        unpack(gin_ref.at[:, m], table_ref[...], grad_ref.at[m * SLOTS : (m + 1) * SLOTS])
    total[...] = jnp.zeros_like(total)
    dtotal[...] = jnp.zeros_like(dtotal)

    def one(columns, held):
        blocks = row_blocks()

        def first_products(rows):
            return mm(x_ref[rows, :], win_ref[:, columns]), mm_nt(grad_ref[rows, :], wout_ref[columns, :])

        ahead = first_products(blocks[0])
        for n, rows in enumerate(blocks):
            up, dact = ahead
            if n + 1 < len(blocks):
                ahead = first_products(blocks[n + 1])
            act, slope = gelu_parts(up)
            dup = (dact * slope).astype(BF)
            act = act.astype(BF)
            held[0][rows, :] = act
            held[1][rows, :] = dup
            total[rows, :] += mm(act, wout_ref[columns, :])
            dtotal[rows, :] += mm_nt(dup, win_ref[:, columns])

    over_hidden_units(one, weights, [act_held, dup_held], [act_hbm, dup_hbm], sems)
    pack(dtotal[...].astype(BF), table_t_ref[...], back_ref, 0)
    pack(total[...].astype(BF), table_t_ref[...], out_ref, 0)


def expert_both(arrived, grads, first, second, table, table_t):
    return call(
        expert_both_kernel,
        (shape(ROWS, D), shape(ROWS, D), shape(ROWS, FF), shape(ROWS, FF), shape(*CHUNKS), shape(*CHUNKS)),
        "expert_both",
        8 * ROWS * D * FF,
        24 << 20,
        vmem=44,
        in_specs=[VMEM, VMEM, ANYWHERE, ANYWHERE, VMEM, VMEM],
        out_specs=(VMEM, VMEM, ANYWHERE, ANYWHERE, VMEM, VMEM),
        scratch_shapes=expert_space()
        + [
            pltpu.VMEM((ROWS, D), F32),
            pltpu.VMEM((ROWS, D), F32),
            held_blocks(),
            held_blocks(),
            pltpu.SemaphoreType.DMA((2, 2)),
        ],
    )(arrived, grads, first, second, table, table_t)


ROWS_OWN = 96
TAIL = 16


def parcel_kernel(w_ref, tail_ref, out_ref):
    for g in range(8):
        for part in range(3):
            lanes = slice(part * LANES, (part + 1) * LANES)
            if g < PAIRS:
                block = w_ref[:, part * D + g * LANES : part * D + (g + 1) * LANES]
            else:
                block = jnp.zeros((ROWS_OWN, LANES), BF)
            out_ref[g, 0:ROWS_OWN, lanes] = block
            out_ref[8 + g, 0:ROWS_OWN, lanes] = block
        out_ref[g, ROWS_OWN:, :] = tail_ref[...]
        out_ref[8 + g, ROWS_OWN:, :] = tail_ref[...]


def parcels_of(w_qkv, gain_attn, gain_ffn, rel_bias):
    row = jnp.concatenate([gain_attn.reshape(1, -1), gain_ffn.reshape(1, -1), rel_bias.reshape(1, -1)], axis=1)
    tail = jnp.pad(row, ((0, TAIL - 1), (0, 3 * LANES - row.shape[1])))
    return call(parcel_kernel, shape(16, ROWS_OWN + TAIL, 3 * LANES), "parcels", 0, 2 << 20)(w_qkv, tail)


def small_parts(parcels):
    rows = parcels[:, ROWS_OWN].astype(F32).reshape(2, 8, 3 * LANES)
    gain_a = rows[:, :, :ROWS_OWN].reshape(2, 1, D)
    gain_f = rows[:, :, ROWS_OWN : 2 * ROWS_OWN].reshape(2, 1, D)
    bias = rows[:, :, 2 * ROWS_OWN : 2 * ROWS_OWN + 4 * H].reshape(2, RELB, H)
    first = 2 * jnp.minimum(lax.axis_index("shard"), PAIRS - 1)
    return gain_a, gain_f, lax.dynamic_slice_in_dim(bias, first, 2, 2)


def project_kernel(layer, shard_ref, parcel_ref, gain_ref, *refs):
    blocks, normed_ref, qkv_ref = refs[:8], refs[8], refs[9]
    own = jnp.concatenate([parcel_ref[layer * 8 + j, 0:ROWS_OWN, :] for j in range(8)], axis=0)
    shard = shard_ref[0]
    for n in range(8):
        back, other = n % 4, n // 4
        source = lax.rem(shard + 8 - 2 * back, 8)
        if other:
            source = source + 1 - 2 * lax.rem(source, 2)
        rows = pl.ds(pl.multiple_of(source * TOK, TOK), TOK)
        normed = norm_of(blocks[n][...].astype(F32), gain_ref[layer])[0].astype(BF)
        normed_ref[rows, :] = normed
        qkv_ref[rows, :] = mm(normed, own).astype(BF)


def project(layer, shard, parcels, gain, blocks):
    return call(
        partial(project_kernel, layer),
        (shape(SEQ, D), shape(SEQ, 3 * LANES)),
        "project",
        2 * SEQ * D * 3 * LANES,
        5 << 20,
        in_specs=[pl.BlockSpec(memory_space=pltpu.SMEM)] + [VMEM] * 10,
    )(shard, parcels, gain, *blocks)


WIDE = 4 * LANES


def dense_grads_kernel(layer, shard_ref, normed_ref, dproj_ref, context_ref, branch_ref, tail_ref, *refs):
    out_hbm, held, sem = refs[-3:]
    dqkv = mm_tn(normed_ref[...], dproj_ref[...]).astype(BF)
    group = jnp.minimum(shard_ref[0], PAIRS - 1)
    columns = pl.ds(pl.multiple_of(group * LANES, LANES), LANES)
    dao = mm_tn(context_ref[...], branch_ref[:, columns]).astype(BF)
    for r in range(8):
        rows = slice(r * ROWS_OWN, (r + 1) * ROWS_OWN)
        held[r, 0:ROWS_OWN, 0 : 3 * LANES] = dqkv[rows]
        held[r, 0:ROWS_OWN, 3 * LANES :] = dao[rows]
        held[r, ROWS_OWN:, :] = tail_ref[r]
    store = pltpu.make_async_copy(held, out_hbm.at[layer * 8 : (layer + 1) * 8], sem)
    store.start()
    store.wait()


def dense_grads(layer, shard, normed, dproj, context, branch, dgain_f, diag, filled=None):
    gains = jnp.pad(dgain_f.reshape(8, ROWS_OWN), ((0, 0), (0, LANES - ROWS_OWN)))
    biases = jnp.pad(bias_grad(diag).reshape(8, 8), ((0, 0), (0, 3 * LANES - 8)))
    tail = jnp.pad(jnp.concatenate([gains, biases], axis=1)[:, None].astype(BF), ((0, 0), (0, TAIL - 1), (0, 0)))
    more = () if filled is None else (filled,)
    return call(
        partial(dense_grads_kernel, layer),
        shape(16, ROWS_OWN + TAIL, WIDE),
        "dense_grads",
        2 * SEQ * D * WIDE,
        6 << 20,
        in_specs=[pl.BlockSpec(memory_space=pltpu.SMEM)] + [VMEM] * 5 + [ANYWHERE] * len(more),
        out_specs=ANYWHERE,
        scratch_shapes=[pltpu.VMEM((8, ROWS_OWN + TAIL, WIDE), BF), pltpu.SemaphoreType.DMA],
        input_output_aliases={6: 0} if more else {},
    )(shard, normed, dproj, context, branch, tail, *more)


def finish_kernel(rep_ref, w_ref, gain_ref, *refs):
    blocks, (qkv_ref, ao_ref, gain_a_ref, gain_f_ref, bias_ref, products) = refs[:8], refs[8:]
    rep = rep_ref[0]
    gain_f_ref[...] = jnp.zeros_like(gain_f_ref)
    products[...] = jnp.zeros_like(products)
    for n in range(8):
        other, back = n // 4, n % 4
        group = lax.rem(rep + 4 - back, 4) + lax.rem(rep // 4 + other, 2) * 4
        block = blocks[n][0:ROWS_OWN, :].astype(F32)
        extra = blocks[n][ROWS_OWN:, 0 : 2 * LANES].astype(F32)
        gain_f_ref[...] += extra[0:1, 0:ROWS_OWN]
        bias_ref[pl.ds(group, 1), :] = extra[0:1, LANES:]

        @pl.when(group < PAIRS)
        def _(block=block, group=group):
            for part in range(3):
                columns = pl.ds(pl.multiple_of(part * D + group * LANES, LANES), LANES)
                grad = block[:, part * LANES : (part + 1) * LANES]
                qkv_ref[:, columns] = grad
                products[...] += grad * w_ref[:, columns].astype(F32)
            ao_ref[:, pl.ds(pl.multiple_of(group * LANES, LANES), LANES)] = block[:, 3 * LANES :]

    sums = lax.dot_general(
        jnp.ones((8, LANES), F32), products[...], (((1,), (1,)), ((), ())), precision=HIGHEST, preferred_element_type=F32
    )
    gain_a_ref[...] = sums[0:1, :] / gain_ref[...]


def finish(rep, w_qkv, gain, blocks):
    return call(
        finish_kernel,
        (
            shape(ROWS_OWN, 3 * D, dtype=F32),
            shape(ROWS_OWN, D, dtype=F32),
            shape(1, ROWS_OWN, dtype=F32),
            shape(1, ROWS_OWN, dtype=F32),
            shape(8, LANES, dtype=F32),
        ),
        "finish",
        0,
        2 << 20,
        in_specs=[pl.BlockSpec(memory_space=pltpu.SMEM)] + [VMEM] * 10,
        scratch_shapes=[pltpu.VMEM((ROWS_OWN, LANES), F32)],
    )(rep, w_qkv, gain, *blocks)


def spread(chunks):
    return lax.all_to_all(chunks, EVERYONE, split_axis=0, concat_axis=0, tiled=True)


def across(chunks):
    return lax.all_to_all(chunks, "shard", split_axis=0, concat_axis=0, tiled=True)


def swap(value):
    return lax.ppermute(value, "section", [(0, 1), (1, 0)])


def after(value, *others):
    return lax.optimization_barrier((value, *others))[0]


def tokens_of_all(own):
    n = 8

    def from_chip(back):
        return lax.ppermute(own, "shard", [(j, (j + 2 * back) % n) for j in range(n)])

    same_core = [own, from_chip(1), from_chip(2), from_chip(3)]
    return same_core + [lax.ppermute(block, "shard", [(j, j ^ 1) for j in range(n)]) for block in same_core]


def slot_tables(routes):
    flat = routes.reshape(2, 2 * TOK)
    onehot = (flat[..., None] == jnp.arange(EXPERTS, dtype=jnp.int32)).astype(BF)
    at = jnp.arange(2 * TOK, dtype=jnp.int32)
    earlier = (at[None, :] < at[:, None]).astype(BF)
    before = jnp.einsum("ab,lbe->lae", earlier, onehot, preferred_element_type=F32)
    rank = jnp.sum(before * onehot.astype(F32), axis=-1).astype(jnp.int32)
    return (flat * CAP + rank).reshape(routes.shape)


def per_device(
    inputs, cotangent, w_qkv, w_attn_out, gain_attn, gain_ffn, rel_bias, w_in, w_out, routes, gates
):
    section = lax.axis_index("section")
    shard = lax.axis_index("shard")
    first_proj, second_proj = w_in[0, 0], w_out[0, 0]
    hidden0 = lax.dynamic_index_in_dim(inputs[:, 0], section, 0, keepdims=False)
    cot = lax.dynamic_index_in_dim(cotangent[:, 0], section, 0, keepdims=False)
    table = pack_tables()
    table_t = table.T

    full0 = tokens_of_all(hidden0)
    got = lax.all_to_all(
        after(parcels_of(w_qkv[0], gain_attn, gain_ffn, rel_bias[0]), *full0[1:]),
        ("section", "shard"),
        split_axis=0,
        concat_axis=0,
        tiled=True,
    )
    gain_a, gain_f, bias = small_parts(got)
    tiles = [bias_tiles(bias[l]) for l in range(2)]
    w_ao = lax.all_gather(after(w_attn_out[0], got), ("section", "shard"), axis=0, tiled=True).reshape(2, D, D)

    def both_layers(values):
        own = lax.dynamic_index_in_dim(values[0, :, 0], section, 0, keepdims=False)
        other = swap(lax.dynamic_index_in_dim(values[0, :, 0], 1 - section, 0, keepdims=False))
        return jnp.where(section == 0, jnp.stack([own, other]), jnp.stack([other, own]))

    slot_cols = slot_tables(both_layers(routes))
    slot_rows = slot_cols.transpose(0, 2, 1)
    gate_cols = both_layers(gates)

    own_slots = slot_tables(routes[0, :, 0]).transpose(0, 2, 1)
    own_grads = grad_rows(cotangent[:, 0], own_slots, gates[0, :, 0], table_t)

    own_index = shard.reshape(1)
    normed0, qkv0 = project(0, own_index, got, gain_a, full0)
    ctx0, weights0 = attention(qkv0, tiles[0])
    ctx0_tok = across(ctx0.reshape(8, TOK, LANES))
    middle0, send, ctx0_own = middle_part(0, ctx0_tok, w_ao, hidden0, gain_f, slot_rows, table_t)
    arrived = spread(send)
    grads1 = lax.all_to_all(
        after(own_grads, arrived), ("rep", "shard"), split_axis=0, concat_axis=0, tiled=True
    )
    x0, act0, slope0, made = expert_forward(arrived, first_proj, second_proj, table, table_t)
    back = spread(after(made, grads1))
    ctx0_full = lax.all_gather(ctx0_own, "shard", axis=0, tiled=True)
    w_full = lax.all_gather(after(w_qkv[0], arrived), ("section", "shard"), axis=0, tiled=True).reshape(2, D, 3 * D)
    out0 = combine(0, back, middle0, slot_cols, gate_cols, table)

    normed1, qkv1 = project(1, own_index, got, gain_a, tokens_of_all(out0))
    ctx1, weights1 = attention(qkv1, tiles[1])
    ctx1_tok = across(ctx1.reshape(8, TOK, LANES))
    middle1, send, ctx1_own = middle_part(1, ctx1_tok, w_ao, out0, gain_f, slot_rows, table_t)
    ctx1_full = lax.all_gather(ctx1_own, "shard", axis=0, tiled=True)
    x1, g1, act1, dup1, made1, dmade1 = expert_both(spread(send), grads1, first_proj, second_proj, table, table_t)

    back = spread(dmade1)
    dmid1, branch1, send, dgain_f1 = middle_back(1, back, slot_cols, table, cot, middle1, gain_f, w_ao)
    branch1_full = lax.all_gather(branch1, "shard", axis=0, tiled=True)
    dproj1, diag1 = attention_back(qkv1, weights1, across(send).reshape(SEQ, LANES))
    dproj1_tok = across(dproj1.reshape(8, TOK, 3 * LANES))
    dh1, send = hidden_back_send(1, dproj1_tok, w_full, out0, gain_a, dmid1, slot_rows, gate_cols, table_t)

    arrived = spread(send)
    made1_back = spread(after(made1, arrived))
    out1 = combine(1, made1_back, middle1, slot_cols, gate_cols, table)
    g0, dup0, dmade0 = expert_back(arrived, first_proj, second_proj, slope0, table, table_t)
    back = spread(after(dmade0, made1_back))
    dmid0, branch0, send, dgain_f0 = middle_back(0, back, slot_cols, table, dh1, middle0, gain_f, w_ao)
    branch0_full = lax.all_gather(branch0, "shard", axis=0, tiled=True)
    dproj0, diag0 = attention_back(qkv0, weights0, across(send).reshape(SEQ, LANES))

    dproj0_tok = across(dproj0.reshape(8, TOK, 3 * LANES))
    parcels = dense_grads(1, own_index, normed1, dproj1, ctx1_full, branch1_full, dgain_f1, diag1)
    parcels = dense_grads(0, own_index, normed0, dproj0, ctx0_full, branch0_full, dgain_f0, diag0, parcels)
    parcels = after(parcels, dproj0_tok)
    got = lax.all_to_all(parcels, ("section", "rep"), split_axis=0, concat_axis=0, tiled=True)

    def own(a, b):
        return jnp.where(section == 0, a, b)

    grad_in = mm_tn(own(x0, x1), own(dup0, dup1))
    grad_out = mm_tn(own(act0, act1), own(g0, g1))
    dh0 = hidden_back(0, dproj0_tok, w_full, hidden0, gain_a, dmid0)
    got, grad_in, grad_out, dh0 = lax.optimization_barrier((got, grad_in, grad_out, dh0))
    summed = jnp.sum(got.astype(F32), axis=0).astype(BF)

    block = lax.ppermute(summed, ("rep", "shard"), [(a * 8 + b, b * 8 + a) for a in range(8) for b in range(8)])
    blocks = [block] + [
        lax.ppermute(block, "rep", [(r, r // 4 * 4 + (r + k) % 4) for r in range(8)]) for k in range(1, 4)
    ]
    blocks = blocks + [lax.ppermute(b, "rep", [(r, (r + 4) % 8) for r in range(8)]) for b in blocks]
    grad_qkv, grad_ao, dgain_a, dgain_f, drel = finish(
        lax.axis_index("rep").reshape(1), w_qkv[0], gain_attn.astype(F32), blocks
    )
    grad_bias = drel[:PAIRS, :8].reshape(PAIRS, 4, 2).transpose(1, 0, 2).reshape(1, 4, H)

    def by_layer(layer0, layer1):
        keep = jnp.where(section == 0, layer0, layer1)
        other = swap(jnp.where(section == 0, layer1, layer0))
        pair = jnp.where(section == 0, jnp.stack([keep, other]), jnp.stack([other, keep]))
        return pair.reshape(1, 2, 1, TOK, D)

    return (
        by_layer(out0, out1),
        by_layer(dh0, dh1),
        grad_qkv[None],
        grad_ao[None],
        dgain_a,
        dgain_f,
        grad_bias,
        grad_in[None, None],
        grad_out[None, None],
    )


def solution(mesh):
    placed = (
        P(None, "rep", "shard", None),
        P(None, "rep", "shard", None),
        P("section", "shard", None),
        P("section", "shard", None),
        P("section", "shard"),
        P("section", "shard"),
        P("section", "shard", None),
        P("section", ("rep", "shard"), None, None),
        P("section", ("rep", "shard"), None, None),
        P("section", None, "rep", "shard", None),
        P("section", None, "rep", "shard", None),
    )
    return jax.shard_map(
        per_device,
        mesh=mesh,
        in_specs=placed,
        out_specs=(
            P("section", None, "rep", "shard", None),
            P("section", None, "rep", "shard", None),
            P("section", "shard", None),
            P("section", "shard", None),
            P("section", "shard"),
            P("section", "shard"),
            P("section", "shard", None),
            P("section", ("rep", "shard"), None, None),
            P("section", ("rep", "shard"), None, None),
        ),
        check_vma=False,
    )
```

time: 645 us -> 555 us (0.86)
  the two profiles are of different devices: /device:TPU:25 before, /device:TPU:0 now
where the time goes in v2:
time: 555 us; the launch traced here: 545 us
  Pallas kernels  151 us (27%)
  waiting for transfers between devices  130 us (23%)
  blocking collectives  106 us (19%)
  starting transfers between devices  95.4 us (17%)
  matrix products  18.1 us (3%)
  local copies, waits for them, and re-layouts  18 us (3%)
  between operations  15.4 us (3%)
  other arithmetic  11 us (2%)
    pallas_call x24, Pallas kernels, placed(): run(*(pltpu.with_memory_space_constraint(x, pltpu.HBM) if x.ndim > 1 else...  151 us
    all_to_all x5, waiting for transfers between devices, spread(): lax.all_to_all(chunks, EVERYONE, split_axis=0, concat_axis=0, tiled=True)  63 us
    all_to_all x2, blocking collectives, spread(): lax.all_to_all(chunks, EVERYONE, split_axis=0, concat_axis=0, tiled=True)  52.6 us
    all_to_all x5, starting transfers between devices, spread(): lax.all_to_all(chunks, EVERYONE, split_axis=0, concat_axis=0, tiled=True)  29.2 us
    all_to_all x2, blocking collectives, across(): lax.all_to_all(chunks, 'shard', split_axis=0, concat_axis=0, tiled=True)  29 us
    all_to_all x1, blocking collectives, per_device(): lax.all_to_all(after(parcels_of(w_qkv[0], gain_attn, gain_ffn, rel_bias[0...  24.2 us
    all_to_all x4, waiting for transfers between devices, across(): lax.all_to_all(chunks, 'shard', split_axis=0, concat_axis=0, tiled=True)  23.8 us
    ppermute x6, waiting for transfers between devices, from_chip(): lax.ppermute(own, 'shard', [(j, (j + 2 * back) % n) for j in range(n)])  16.9 us
  transfers between devices with their start and end apart: 43, of which 20 were waited for; matrix products, arithmetic and copies ran while one was open for 7% of the time, Pallas kernels for 26%

profile of v2, /device:TPU:0, one launch (start us, length us, event | category | flops | bytes accessed | tf_op | source)
XLA Modules:
  0.0 544.5 jit_solution(11573277998644595077)
XLA Ops:
  8.2 2.1 collective-permute-start
  10.3 3.6 collective-permute-start.1
  14.9 2.4 collective-permute-done.refs_1_
  17.3 5.4 collective-permute-done.1.refs_2_
  25.3 2.3 parcels.1
  27.6 24.2 %all_to_all.80.parcel_ref = bf16[16,112,384]{2,1,0:T(8,128)(2,1)S(1)} all-to-all(bf16[16,112,384]{2,1,0:T(8,128)(2,1)} %parcels.1), channel_id=1, replica_groups=mesh['section'=2,'rep'=8,'shard'=8] {'section','shard'}, dimensions={0} | all-to-all | bytes 2752512 | tf_op jit(solution)/shard_map/all_to_all | solution.py:867
  60.5 4.2 project.2
  64.7 8.8 %attention.2 = (bf16[1024,128]{1,0:T(8,128)(2,1)}, bf16[2,1024,1024]{2,1,0:T(8,128)(2,1)}) custom-call(bf16[1024,384]{1,0:T(8,128)(2,1)} %get-tuple-element.68.qkv_ref, bf16[8,256,256]{2,1,0:T(8,128)(2,1)} %bias_tiles.2.bias_ref), custom_call_target="tpu_custom_call" | custom-call | flops 1073741824 | bytes 8388608 | tf_op jit(solution)/shard_map/attention/pallas_call | solution.py:59
  73.5 3.4 all-to-all-start.1
  78.4 6.4 %all-to-all-done.1.ctx_ref = bf16[8,128,128]{2,1,0:T(8,128)(2,1)S(1)} async-done(((bf16[8,128,128]{2,1,0:T(8,128)(2,1)}), bf16[8,128,128]{2,1,0:T(8,128)(2,1)S(1)}, u32[]{:S(2)}, u32[]{:S(2)}) %all-to-all-start.1) | async-done | bytes 262176 | tf_op jit(solution)/shard_map/all_to_all | solution.py:824
  86.5 4.8 middle.2
  91.3 28.1 %all_to_all.81.in_ref = bf16[128,32,128]{2,1,0:T(8,128)(2,1)} all-to-all(bf16[128,32,128]{2,1,0:T(8,128)(2,1)} %get-tuple-element.71), channel_id=1, replica_groups=mesh['section'=2,'rep'=8,'shard'=8] {'section','rep','shard'}, dimensions={0} | all-to-all | bytes 2097152 | tf_op jit(solution)/shard_map/all_to_all | solution.py:820
  121.6 3.8 grad_rows.1
  125.4 5.3 all-to-all-start.3
  131.6 13.2 %expert_forward.1 = (bf16[640,768]{1,0:T(8,128)(2,1)}, bf16[640,3072]{1,0:T(8,128)(2,1)}, bf16[640,3072]{1,0:T(8,128)(2,1)}, bf16[128,32,128]{2,1,0:T(8,128)(2,1)}) custom-call(bf16[128,32,128]{2,1,0:T(8,128)(2,1)} %all_to_all.81.in_ref, bf16[768,3072]{1,0:T(8,128)(2,1)} %bitcast.136, bf16[3072,768]{1,0:T(8,128)(2,1)} %bitcast.139, ...), custom_call_target="tpu_custom_call" | custom-call | flops 6039797760 | bytes 20971520 | tf_op jit(solution)/shard_map/expert_forward/pallas_call | solution.py:59
  144.8 4.3 all-to-all-done.3.gin_ref
  149.1 6.9 %all-to-all-start.4 = ((bf16[128,32,128]{2,1,0:T(8,128)(2,1)}), bf16[128,32,128]{2,1,0:T(8,128)(2,1)S(1)}, u32[]{:S(2)}, u32[]{:S(2)}) async-start(bf16[128,32,128]{2,1,0:T(8,128)(2,1)} %get-tuple-element.74), calls=%async_computation.4 | async-start | bytes 2097152 | tf_op jit(solution)/shard_map/all_to_all | solution.py:820
  157.1 14.6 %collective-permute-done.8 = f32[128,2]{0,1:T(2,128)S(1)} collective-permute-done((f32[128,2]{0,1:T(2,128)S(1)}, f32[128,2]{0,1:T(2,128)S(1)}, u32[]{:S(2)}, u32[]{:S(2)}) %collective-permute-start.8) | collective-permute-done | bytes 1056 | tf_op jit(solution)/shard_map/ppermute | solution.py:828
  172.7 2.3 all-to-all-done.4.back_ref
  176.0 3.1 combine.2.refs_0_.hidden_ref
  181.5 2.1 collective-permute-start.11
  183.6 4.3 collective-permute-done.9.refs_1_
  187.9 4.7 collective-permute-done.10.refs_2_
  194.3 2.0 bias_tiles.3.bias_ref
  197.8 4.2 project.3
  202.1 8.8 %attention.3 = (bf16[1024,128]{1,0:T(8,128)(2,1)}, bf16[2,1024,1024]{2,1,0:T(8,128)(2,1)}) custom-call(bf16[1024,384]{1,0:T(8,128)(2,1)} %get-tuple-element.76.qkv_ref, bf16[8,256,256]{2,1,0:T(8,128)(2,1)} %bias_tiles.3.bias_ref), custom_call_target="tpu_custom_call" | custom-call | flops 1073741824 | bytes 8388608 | tf_op jit(solution)/shard_map/attention/pallas_call | solution.py:59
  210.9 11.6 %all_to_all.82.ctx_ref = bf16[8,128,128]{2,1,0:T(8,128)(2,1)} all-to-all(bf16[8,128,128]{2,1,0:T(8,128)(2,1)} %bitcast.123), channel_id=1, replica_groups=mesh['section'=2,'rep'=8,'shard'=8] {'shard'}, dimensions={0} | all-to-all | bytes 524288 | tf_op jit(solution)/shard_map/all_to_all | solution.py:824
  222.4 4.8 middle.3
  227.2 8.0 %all-to-all-start.6 = ((bf16[128,32,128]{2,1,0:T(8,128)(2,1)}), bf16[128,32,128]{2,1,0:T(8,128)(2,1)S(1)}, u32[]{:S(2)}, u32[]{:S(2)}) async-start(bf16[128,32,128]{2,1,0:T(8,128)(2,1)} %get-tuple-element.78), calls=%async_computation.6 | async-start | bytes 2097152 | tf_op jit(solution)/shard_map/all_to_all | solution.py:820
  236.0 18.1 %all-to-all-done.6.in_ref = bf16[128,32,128]{2,1,0:T(8,128)(2,1)S(1)} async-done(((bf16[128,32,128]{2,1,0:T(8,128)(2,1)}), bf16[128,32,128]{2,1,0:T(8,128)(2,1)S(1)}, u32[]{:S(2)}, u32[]{:S(2)}) %all-to-all-start.6) | async-done | bytes 1048608 | tf_op jit(solution)/shard_map/all_to_all | solution.py:820
  255.1 19.2 %expert_both.1 = (bf16[640,768]{1,0:T(8,128)(2,1)}, bf16[640,768]{1,0:T(8,128)(2,1)}, bf16[640,3072]{1,0:T(8,128)(2,1)}, bf16[640,3072]{1,0:T(8,128)(2,1)}, bf16...) custom-call(bf16[128,32,128]{2,1,0:T(8,128)(2,1)} %copy-done.13, bf16[64,2,32,128]{3,2,1,0:T(8,128)(2,1)} %copy-done.11, ...), custom_call_target="tpu_custom_call" | custom-call | flops 12079595520 | bytes 25165824 | tf_op jit(solution)/shard_map/expert_both/pallas_call | solution.py:59
  274.3 4.8 all-to-all-start.7
  279.8 18.0 %all-to-all-done.7.back_ref = bf16[128,32,128]{2,1,0:T(8,128)(2,1)S(1)} async-done(((bf16[128,32,128]{2,1,0:T(8,128)(2,1)}), bf16[128,32,128]{2,1,0:T(8,128)(2,1)S(1)}, u32[]{:S(2)}, u32[]{:S(2)}) %all-to-all-start.7) | async-done | bytes 1048608 | tf_op jit(solution)/shard_map/all_to_all | solution.py:820
  298.8 4.2 middle_back.2
  303.1 3.6 all-to-all-start.8
  307.3 8.0 %all-to-all-done.8 = bf16[8,128,128]{2,1,0:T(8,128)(2,1)S(1)} async-done(((bf16[8,128,128]{2,1,0:T(8,128)(2,1)}), bf16[8,128,128]{2,1,0:T(8,128)(2,1)S(1)}, u32[]{:S(2)}, u32[]{:S(2)}) %all-to-all-start.8) | async-done | bytes 262176 | tf_op jit(solution)/shard_map/all_to_all | solution.py:824
  316.0 10.0 %attention_back.2 = (bf16[1024,384]{1,0:T(8,128)(2,1)}, f32[8,512]{1,0:T(8,128)}) custom-call(bf16[1024,384]{1,0:T(8,128)(2,1)} %get-tuple-element.76.qkv_ref, bf16[2,1024,1024]{2,1,0:T(8,128)(2,1)} %get-tuple-element.80.weights_hbm, bf16[1024,128]{1,0:T(8,128)(2,1)} %bitcast.122, bf16[256,256]{1,0:T(8,128)(2,1)} %fusion.27.flip_ref), custom_call_target="tpu_custom_call" | custom-call | flops 2147483648 | bytes 8388608 | tf_op jit(solution)/shard_map/attention_back/pallas_call | solution.py:59
  326.1 17.5 %all_to_all.83.back_ref = bf16[8,128,384]{2,1,0:T(8,128)(2,1)} all-to-all(bf16[8,128,384]{2,1,0:T(8,128)(2,1)} %bitcast.119), channel_id=1, replica_groups=mesh['section'=2,'rep'=8,'shard'=8] {'shard'}, dimensions={0} | all-to-all | bytes 1572864 | tf_op jit(solution)/shard_map/all_to_all | solution.py:824
  343.6 7.2 %hidden_back_send.1 = (bf16[128,768]{1,0:T(8,128)(2,1)}, bf16[128,32,128]{2,1,0:T(8,128)(2,1)}) custom-call(bf16[8,128,384]{2,1,0:T(8,128)(2,1)} %all_to_all.83.back_ref, bf16[2,768,2304]{2,1,0:T(8,128)(2,1)} %bitcast.111, bf16[128,768]{1,0:T(8,128)(2,1)} %combine.2.refs_0_.hidden_ref, f32[2,1,768]{2,1,0:T(1,128)} %reshape.499.gain_ref, ...), custom_call_target="tpu_custom_call" | custom-call | flops 452984832 | bytes 6291456 | tf_op jit(solution)/shard_map/hidden_back_send/pallas_call | solution.py:59
  350.8 4.6 all-to-all-start.10
  356.0 18.3 %all-to-all-done.10.in_ref = bf16[128,32,128]{2,1,0:T(8,128)(2,1)S(1)} async-done(((bf16[128,32,128]{2,1,0:T(8,128)(2,1)}), bf16[128,32,128]{2,1,0:T(8,128)(2,1)S(1)}, u32[]{:S(2)}, u32[]{:S(2)}) %all-to-all-start.10) | async-done | bytes 1048608 | tf_op jit(solution)/shard_map/all_to_all | solution.py:820
  374.3 4.8 all-to-all-start.11
  379.2 12.4 %expert_back.1 = (bf16[640,768]{1,0:T(8,128)(2,1)}, bf16[640,3072]{1,0:T(8,128)(2,1)}, bf16[128,32,128]{2,1,0:T(8,128)(2,1)}) custom-call(bf16[128,32,128]{2,1,0:T(8,128)(2,1)} %copy-done.12, bf16[768,3072]{1,0:T(8,128)(2,1)} %bitcast.138, bf16[3072,768]{1,0:T(8,128)(2,1)} %bitcast.141, bf16[640,3072]{1,0:T(8,128)(2,1)} %get-tuple-element.91.slope_hbm, ...), custom_call_target="tpu_custom_call" | custom-call | flops 6039797760 | bytes 20971520 | tf_op jit(solution)/shard_map/expert_back/pallas_call | solution.py:59
  391.7 6.3 %all-to-all-done.11.back_ref = bf16[128,32,128]{2,1,0:T(8,128)(2,1)S(1)} async-done(((bf16[128,32,128]{2,1,0:T(8,128)(2,1)}), bf16[128,32,128]{2,1,0:T(8,128)(2,1)S(1)}, u32[]{:S(2)}, u32[]{:S(2)}) %all-to-all-start.11) | async-done | bytes 1048608 | tf_op jit(solution)/shard_map/all_to_all | solution.py:820
  397.9 24.6 %all_to_all.84.back_ref = bf16[128,32,128]{2,1,0:T(8,128)(2,1)} all-to-all(bf16[128,32,128]{2,1,0:T(8,128)(2,1)} %get-tuple-element.93), channel_id=1, replica_groups=mesh['section'=2,'rep'=8,'shard'=8] {'section','rep','shard'}, dimensions={0} | all-to-all | bytes 2097152 | tf_op jit(solution)/shard_map/all_to_all | solution.py:820
  422.5 4.2 middle_back.3
  427.3 3.4 all-to-all-start.13
  431.5 5.2 dense_grads.2.refs_0_
  436.6 3.4 all-to-all-done.13
  440.7 10.0 %attention_back.3 = (bf16[1024,384]{1,0:T(8,128)(2,1)}, f32[8,512]{1,0:T(8,128)}) custom-call(bf16[1024,384]{1,0:T(8,128)(2,1)} %get-tuple-element.68.qkv_ref, bf16[2,1024,1024]{2,1,0:T(8,128)(2,1)} %get-tuple-element.90.weights_hbm, bf16[1024,128]{1,0:T(8,128)(2,1)} %bitcast.120, bf16[256,256]{1,0:T(8,128)(2,1)} %fusion.27.flip_ref), custom_call_target="tpu_custom_call" | custom-call | flops 2147483648 | bytes 8388608 | tf_op jit(solution)/shard_map/attention_back/pallas_call | solution.py:59
  450.7 3.6 all-to-all-start.14
  456.3 5.0 dense_grads.3
  461.3 6.0 %all-to-all-done.14.back_ref = bf16[8,128,384]{2,1,0:T(8,128)(2,1)S(1)} async-done(((bf16[8,128,384]{2,1,0:T(8,128)(2,1)}), bf16[8,128,384]{2,1,0:T(8,128)(2,1)S(1)}, u32[]{:S(2)}, u32[]{:S(2)}) %all-to-all-start.14) | async-done | bytes 786464 | tf_op jit(solution)/shard_map/all_to_all | solution.py:824
  467.4 4.0 all-to-all-start.15
  471.4 10.2 %fusion.2 = f32[768,3072]{1,0:T(8,128)} fusion(bf16[640,3072]{1,0:T(8,128)(2,1)} %get-tuple-element.109, bf16[640,3072]{1,0:T(8,128)(2,1)} %get-tuple-element.110, pred[]{:T(512)S(6)} %eq.195, bf16[640,768]{1,0:T(8,128)(2,1)} %get-tuple-element.107, bf16[640,768]{1,0:T(8,128)(2,1)} %get-tuple-element.108), kind=kOutput, calls=%fused_computation.2 | convolution fusion | flops 3022356480 | bytes 19267584 | tf_op jit(solution)/shard_map/dot_general | solution.py:45
  481.6 6.6 %fusion = f32[3072,768]{1,0:T(8,128)} fusion(bf16[640,3072]{1,0:T(8,128)(2,1)S(1)} %copy-done.46, bf16[640,3072]{1,0:T(8,128)(2,1)S(1)} %copy-done.47, pred[]{:T(512)S(6)} %eq.195, bf16[640,768]{1,0:T(8,128)(2,1)S(1)} %copy-done.49, bf16[640,768]{1,0:T(8,128)(2,1)S(1)} %copy-done.48), kind=kOutput, calls=%fused_computation | convolution fusion | flops 3022356480 | bytes 19267584 | tf_op jit(solution)/shard_map/dot_general | solution.py:45
  488.2 3.0 combine.3
  494.2 5.6 %hidden_back.1 = bf16[128,768]{1,0:T(8,128)(2,1)} custom-call(bf16[8,128,384]{2,1,0:T(8,128)(2,1)} %copy-done.8, bf16[2,768,2304]{2,1,0:T(8,128)(2,1)} %bitcast.112, bf16[128,768]{1,0:T(8,128)(2,1)} %copy-done.9, f32[2,1,768]{2,1,0:T(1,128)} %reshape.499.gain_ref, f32[128,768]{1,0:T(8,128)} %get-tuple-element.115.dmid_ref), custom_call_target="tpu_custom_call" | custom-call | flops 452984832 | bytes 5242880 | tf_op jit(solution)/shard_map/hidden_back/pallas_call | solution.py:59
  502.8 4.8 collective-permute-start.19
  507.6 6.3 %collective-permute-start.20 = (bf16[112,512]{1,0:T(8,128)(2,1)S(1)}, bf16[112,512]{1,0:T(8,128)(2,1)S(1)}, u32[]{:S(2)}, u32[]{:S(2)}) collective-permute-start(bf16[112,512]{1,0:T(8,128)(2,1)S(1)} %collective-permute-done.18.refs_0_), channel_id=1, source_target_pairs={{0,16},{8,24},{16,0},{24,8},{32,48},{40,56},{48,32},{56,40},{1,17}... | collective-permute-start | bytes 344072 | tf_op jit(solution)/shard_map/ppermute | solution.py:945
  516.4 5.4 collective-permute-start.22
  521.8 3.1 collective-permute-start.23
  525.4 3.1 collective-permute-start.25
  533.1 2.6 finish.1
  (242 shorter events, 52.5 us)
Async XLA Ops:
  7.2 44.7 %copy-start.40 = (s32[1,2,1,128,2]{3,4,2,1,0:T(2,128)S(1)}, s32[1,2,1,128,2]{3,4,2,1,0:T(2,128)}, u32[]{:S(2)}) copy-start(s32[1,2,1,128,2]{3,4,2,1,0:T(2,128)} %param.20) | copy-start | bytes 6148
  7.2 79.3 %all-gather.7.cloned.1.call-start = ((), (), s32[]{:S(2)}) async-start(), calls=%async_computation.16 | async-start | bytes 2506752 | tf_op jit(solution)/shard_map/all_gather | solution.py:876
  8.2 52.2 %copy-start.9 = (bf16[128,768]{1,0:T(8,128)(2,1)}, bf16[128,768]{1,0:T(8,128)(2,1)S(1)}, u32[]{:S(2)}) copy-start(bf16[128,768]{1,0:T(8,128)(2,1)S(1)} %dynamic-slice_bitcast_fusion.1.refs_0_.hidden_ref) | copy-start | bytes 589828
  8.2 9.1 %collective-permute-start = (bf16[128,768]{1,0:T(8,128)(2,1)S(1)}, bf16[128,768]{1,0:T(8,128)(2,1)S(1)}, u32[]{:S(2)}, u32[]{:S(2)}) collective-permute-start(bf16[128,768]{1,0:T(8,128)(2,1)S(1)} %dynamic-slice_bitcast_fusion.1.refs_0_.hidden_ref), channel_id=1, source_target_pairs={{0,2},{1,3},{2,4},{3,5},{4,6},{5,7},{6,0},{7,1},{8,10},{9,11},{10,... | collective-permute-start | bytes 589832 | tf_op jit(solution)/shard_map/ppermute | solution.py:839
  10.3 12.4 %collective-permute-start.1 = (bf16[128,768]{1,0:T(8,128)(2,1)S(1)}, bf16[128,768]{1,0:T(8,128)(2,1)S(1)}, u32[]{:S(2)}, u32[]{:S(2)}) collective-permute-start(bf16[128,768]{1,0:T(8,128)(2,1)S(1)} %dynamic-slice_bitcast_fusion.1.refs_0_.hidden_ref), channel_id=1, source_target_pairs={{0,4},{1,5},{2,6},{3,7},{4,0},{5,1},{6,2},{7,3},{8,12},{9,13},{10,... | collective-permute-start | bytes 589832 | tf_op jit(solution)/shard_map/ppermute | solution.py:839
  13.9 8.8 %collective-permute-start.2 = (bf16[128,768]{1,0:T(8,128)(2,1)S(1)}, bf16[128,768]{1,0:T(8,128)(2,1)S(1)}, u32[]{:S(2)}, u32[]{:S(2)}) collective-permute-start(bf16[128,768]{1,0:T(8,128)(2,1)S(1)} %dynamic-slice_bitcast_fusion.1.refs_0_.hidden_ref), channel_id=1, source_target_pairs={{0,6},{1,7},{2,0},{3,1},{4,2},{5,3},{6,4},{7,5},{8,14},{9,15},{10,... | collective-permute-start | bytes 589832 | tf_op jit(solution)/shard_map/ppermute | solution.py:839
  14.9 12.7 %collective-permute-start.3 = (bf16[128,768]{1,0:T(8,128)(2,1)S(1)}, bf16[128,768]{1,0:T(8,128)(2,1)S(1)}, u32[]{:S(2)}, u32[]{:S(2)}) collective-permute-start(bf16[128,768]{1,0:T(8,128)(2,1)S(1)} %dynamic-slice_bitcast_fusion.1.refs_0_.hidden_ref), channel_id=1, source_target_pairs={{0,1},{1,0},{2,3},{3,2},{4,5},{5,4},{6,7},{7,6},{8,9},{9,8},{10,11... | collective-permute-start | bytes 589832 | tf_op jit(solution)/shard_map/ppermute | solution.py:842
  17.3 43.1 %copy-start.17 = (bf16[128,768]{1,0:T(8,128)(2,1)}, bf16[128,768]{1,0:T(8,128)(2,1)S(1)}, u32[]{:S(2)}) copy-start(bf16[128,768]{1,0:T(8,128)(2,1)S(1)} %collective-permute-done.refs_1_) | copy-start | bytes 589828
  17.3 10.3 %collective-permute-start.4 = (bf16[128,768]{1,0:T(8,128)(2,1)S(1)}, bf16[128,768]{1,0:T(8,128)(2,1)S(1)}, u32[]{:S(2)}, u32[]{:S(2)}) collective-permute-start(bf16[128,768]{1,0:T(8,128)(2,1)S(1)} %collective-permute-done.refs_1_), channel_id=1, source_target_pairs={{0,1},{1,0},{2,3},{3,2},{4,5},{5,4},{6,7},{7,6},{8,9},{9,8},{10,11... | collective-permute-start | bytes 589832 | tf_op jit(solution)/shard_map/ppermute | solution.py:842
  22.7 37.7 %copy-start.18 = (bf16[128,768]{1,0:T(8,128)(2,1)}, bf16[128,768]{1,0:T(8,128)(2,1)S(1)}, u32[]{:S(2)}) copy-start(bf16[128,768]{1,0:T(8,128)(2,1)S(1)} %collective-permute-done.1.refs_2_) | copy-start | bytes 589828
  22.7 4.9 collective-permute-start.5
  22.7 37.7 %copy-start.19 = (bf16[128,768]{1,0:T(8,128)(2,1)}, bf16[128,768]{1,0:T(8,128)(2,1)S(1)}, u32[]{:S(2)}) copy-start(bf16[128,768]{1,0:T(8,128)(2,1)S(1)} %collective-permute-done.2.refs_3_) | copy-start | bytes 589828
  22.7 4.9 collective-permute-start.6
  27.6 32.9 %copy-start.20 = (bf16[128,768]{1,0:T(8,128)(2,1)}, bf16[128,768]{1,0:T(8,128)(2,1)S(1)}, u32[]{:S(2)}) copy-start(bf16[128,768]{1,0:T(8,128)(2,1)S(1)} %collective-permute-done.3.refs_4_) | copy-start | bytes 589828
  27.6 32.9 %copy-start.21 = (bf16[128,768]{1,0:T(8,128)(2,1)}, bf16[128,768]{1,0:T(8,128)(2,1)S(1)}, u32[]{:S(2)}) copy-start(bf16[128,768]{1,0:T(8,128)(2,1)S(1)} %collective-permute-done.4.refs_5_) | copy-start | bytes 589828
  27.6 32.9 %copy-start.22 = (bf16[128,768]{1,0:T(8,128)(2,1)}, bf16[128,768]{1,0:T(8,128)(2,1)S(1)}, u32[]{:S(2)}) copy-start(bf16[128,768]{1,0:T(8,128)(2,1)S(1)} %collective-permute-done.5.refs_6_) | copy-start | bytes 589828
  27.6 32.8 %copy-start.23 = (bf16[128,768]{1,0:T(8,128)(2,1)}, bf16[128,768]{1,0:T(8,128)(2,1)S(1)}, u32[]{:S(2)}) copy-start(bf16[128,768]{1,0:T(8,128)(2,1)S(1)} %collective-permute-done.6.refs_7_) | copy-start | bytes 589828
  51.9 3.6 collective-permute-start.7
  73.5 46.7 %copy-start.42 = (f32[1,2,1,128,2]{3,4,2,1,0:T(2,128)S(1)}, f32[1,2,1,128,2]{3,4,2,1,0:T(2,128)}, u32[]{:S(2)}) copy-start(f32[1,2,1,128,2]{3,4,2,1,0:T(2,128)} %param.21) | copy-start | bytes 6148
  73.5 11.2 %all-to-all-start.1 = ((bf16[8,128,128]{2,1,0:T(8,128)(2,1)}), bf16[8,128,128]{2,1,0:T(8,128)(2,1)S(1)}, u32[]{:S(2)}, u32[]{:S(2)}) async-start(bf16[8,128,128]{2,1,0:T(8,128)(2,1)} %bitcast.121), calls=%async_computation.1 | async-start | bytes 524288 | tf_op jit(solution)/shard_map/all_to_all | solution.py:824
  76.9 266.6 %all-gather.9.cloned.1.call-start = ((), (), s32[]{:S(2)}) async-start(), calls=%async_computation.17 | async-start | bytes 7520256 | tf_op jit(solution)/shard_map/all_gather | solution.py:902
  77.0 48.4 %copy-start.4 = (s32[2,128,2]{2,1,0:T(8,128)}, s32[2,128,2]{2,1,0:T(8,128)S(1)}, u32[]{:S(2)}) copy-start(s32[2,128,2]{2,1,0:T(8,128)S(1)} %multiply_add_fusion.slots_ref) | copy-start | bytes 6148
  125.4 23.7 %all-to-all-start.3 = ((bf16[64,2,32,128]{3,2,1,0:T(8,128)(2,1)}), bf16[64,2,32,128]{3,2,1,0:T(8,128)(2,1)S(1)}, u32[]{:S(2)}, u32[]{:S(2)}) async-start(bf16[64,2,32,128]{3,2,1,0:T(8,128)(2,1)} %grad_rows.1), calls=%async_computation.3 | async-start | bytes 2097152 | tf_op jit(solution)/shard_map/all_to_all | solution.py:896
  149.1 53.0 %copy-start.11 = (bf16[64,2,32,128]{3,2,1,0:T(8,128)(2,1)}, bf16[64,2,32,128]{3,2,1,0:T(8,128)(2,1)S(1)}, u32[]{:S(2)}) copy-start(bf16[64,2,32,128]{3,2,1,0:T(8,128)(2,1)S(1)} %all-to-all-done.3.gin_ref) | copy-start | bytes 3145732
  149.1 26.0 %all-to-all-start.4 = ((bf16[128,32,128]{2,1,0:T(8,128)(2,1)}), bf16[128,32,128]{2,1,0:T(8,128)(2,1)S(1)}, u32[]{:S(2)}, u32[]{:S(2)}) async-start(bf16[128,32,128]{2,1,0:T(8,128)(2,1)} %get-tuple-element.74), calls=%async_computation.4 | async-start | bytes 2097152 | tf_op jit(solution)/shard_map/all_to_all | solution.py:820
  156.0 15.7 %collective-permute-start.8 = (f32[128,2]{0,1:T(2,128)S(1)}, f32[128,2]{0,1:T(2,128)S(1)}, u32[]{:S(2)}, u32[]{:S(2)}) collective-permute-start(f32[128,2]{0,1:T(2,128)S(1)} %get-tuple-element.161), channel_id=1, source_target_pairs={{0,64},{64,0},{1,65},{65,1},{2,66},{66,2},{3,67},{67,3},{4,68},{68... | collective-permute-start | bytes 3080 | tf_op jit(solution)/shard_map/ppermute | solution.py:828
  179.1 8.8 %collective-permute-start.9 = (bf16[128,768]{1,0:T(8,128)(2,1)}, bf16[128,768]{1,0:T(8,128)(2,1)S(1)}, u32[]{:S(2)}, u32[]{:S(2)}) collective-permute-start(bf16[128,768]{1,0:T(8,128)(2,1)} %combine.2.refs_0_.hidden_ref), channel_id=1, source_target_pairs={{0,2},{1,3},{2,4},{3,5},{4,6},{5,7},{6,0},{7,1},{8,10},{9,11},{10,... | collective-permute-start | bytes 589832 | tf_op jit(solution)/shard_map/ppermute | solution.py:839
  181.0 11.7 %collective-permute-start.10 = (bf16[128,768]{1,0:T(8,128)(2,1)}, bf16[128,768]{1,0:T(8,128)(2,1)S(1)}, u32[]{:S(2)}, u32[]{:S(2)}) collective-permute-start(bf16[128,768]{1,0:T(8,128)(2,1)} %combine.2.refs_0_.hidden_ref), channel_id=1, source_target_pairs={{0,4},{1,5},{2,6},{3,7},{4,0},{5,1},{6,2},{7,3},{8,12},{9,13},{10,... | collective-permute-start | bytes 589832 | tf_op jit(solution)/shard_map/ppermute | solution.py:839
  181.5 11.2 %collective-permute-start.11 = (bf16[128,768]{1,0:T(8,128)(2,1)}, bf16[128,768]{1,0:T(8,128)(2,1)S(1)}, u32[]{:S(2)}, u32[]{:S(2)}) collective-permute-start(bf16[128,768]{1,0:T(8,128)(2,1)} %combine.2.refs_0_.hidden_ref), channel_id=1, source_target_pairs={{0,6},{1,7},{2,0},{3,1},{4,2},{5,3},{6,4},{7,5},{8,14},{9,15},{10,... | collective-permute-start | bytes 589832 | tf_op jit(solution)/shard_map/ppermute | solution.py:839
  183.6 12.7 %collective-permute-start.12 = (bf16[128,768]{1,0:T(8,128)(2,1)}, bf16[128,768]{1,0:T(8,128)(2,1)S(1)}, u32[]{:S(2)}, u32[]{:S(2)}) collective-permute-start(bf16[128,768]{1,0:T(8,128)(2,1)} %combine.2.refs_0_.hidden_ref), channel_id=1, source_target_pairs={{0,1},{1,0},{2,3},{3,2},{4,5},{5,4},{6,7},{7,6},{8,9},{9,8},{10,11... | collective-permute-start | bytes 589832 | tf_op jit(solution)/shard_map/ppermute | solution.py:842
  187.9 8.4 %collective-permute-start.13 = (bf16[128,768]{1,0:T(8,128)(2,1)S(1)}, bf16[128,768]{1,0:T(8,128)(2,1)S(1)}, u32[]{:S(2)}, u32[]{:S(2)}) collective-permute-start(bf16[128,768]{1,0:T(8,128)(2,1)S(1)} %collective-permute-done.9.refs_1_), channel_id=1, source_target_pairs={{0,1},{1,0},{2,3},{3,2},{4,5},{5,4},{6,7},{7,6},{8,9},{9,8},{10,11... | collective-permute-start | bytes 589832 | tf_op jit(solution)/shard_map/ppermute | solution.py:842
  192.6 3.7 collective-permute-start.14
  192.8 3.6 collective-permute-start.15
  227.2 26.8 %all-to-all-start.6 = ((bf16[128,32,128]{2,1,0:T(8,128)(2,1)}), bf16[128,32,128]{2,1,0:T(8,128)(2,1)S(1)}, u32[]{:S(2)}, u32[]{:S(2)}) async-start(bf16[128,32,128]{2,1,0:T(8,128)(2,1)} %get-tuple-element.78), calls=%async_computation.6 | async-start | bytes 2097152 | tf_op jit(solution)/shard_map/all_to_all | solution.py:820
  235.2 196.3 %all-gather.15.cloned.1.call-start = ((), (), s32[]{:S(2)}) async-start(), calls=%async_computation.20 | async-start | bytes 1769472 | tf_op jit(solution)/shard_map/all_gather | solution.py:909
  235.9 43.2 %copy-start.39 = (bf16[2,1,128,768]{3,2,1,0:T(8,128)(2,1)S(1)}, bf16[2,1,128,768]{3,2,1,0:T(8,128)(2,1)}, u32[]{:S(2)}) copy-start(bf16[2,1,128,768]{3,2,1,0:T(8,128)(2,1)} %param.12) | copy-start | bytes 1179652
  274.3 23.6 %all-to-all-start.7 = ((bf16[128,32,128]{2,1,0:T(8,128)(2,1)}), bf16[128,32,128]{2,1,0:T(8,128)(2,1)S(1)}, u32[]{:S(2)}, u32[]{:S(2)}) async-start(bf16[128,32,128]{2,1,0:T(8,128)(2,1)} %get-tuple-element.81), calls=%async_computation.7 | async-start | bytes 2097152 | tf_op jit(solution)/shard_map/all_to_all | solution.py:820
  279.1 152.4 %all-gather.17.cloned.1.call-start = ((), (), s32[]{:S(2)}) async-start(), calls=%async_computation.21 | async-start | bytes 1769472 | tf_op jit(solution)/shard_map/all_gather | solution.py:914
  303.1 12.3 %all-to-all-start.8 = ((bf16[8,128,128]{2,1,0:T(8,128)(2,1)}), bf16[8,128,128]{2,1,0:T(8,128)(2,1)S(1)}, u32[]{:S(2)}, u32[]{:S(2)}) async-start(bf16[8,128,128]{2,1,0:T(8,128)(2,1)} %get-tuple-element.83), calls=%async_computation.8 | async-start | bytes 524288 | tf_op jit(solution)/shard_map/all_to_all | solution.py:824
  350.8 23.5 %all-to-all-start.10 = ((bf16[128,32,128]{2,1,0:T(8,128)(2,1)}), bf16[128,32,128]{2,1,0:T(8,128)(2,1)S(1)}, u32[]{:S(2)}, u32[]{:S(2)}) async-start(bf16[128,32,128]{2,1,0:T(8,128)(2,1)} %get-tuple-element.87), calls=%async_computation.10 | async-start | bytes 2097152 | tf_op jit(solution)/shard_map/all_to_all | solution.py:820
  355.4 100.9 %all-gather.11.cloned.1.call-start = ((), (), s32[]{:S(2)}) async-start(), calls=%async_computation.18 | async-start | bytes 1769472 | tf_op jit(solution)/shard_map/all_gather | solution.py:901
  374.3 23.6 %all-to-all-start.11 = ((bf16[128,32,128]{2,1,0:T(8,128)(2,1)}), bf16[128,32,128]{2,1,0:T(8,128)(2,1)S(1)}, u32[]{:S(2)}, u32[]{:S(2)}) async-start(bf16[128,32,128]{2,1,0:T(8,128)(2,1)} %get-tuple-element.88), calls=%async_computation.11 | async-start | bytes 2097152 | tf_op jit(solution)/shard_map/all_to_all | solution.py:820
  379.1 77.2 %all-gather.13.cloned.1.call-start = ((), (), s32[]{:S(2)}) async-start(), calls=%async_computation.19 | async-start | bytes 1769472 | tf_op jit(solution)/shard_map/all_gather | solution.py:925
  391.6 35.1 %copy-start.43 = (f32[1,768]{1,0:T(1,128)S(1)}, f32[1,768]{1,0:T(1,128)}, u32[]{:S(2)}) copy-start(f32[1,768]{1,0:T(1,128)} %get-tuple-element.104) | copy-start | bytes 9220
  391.7 35.2 %copy-start.41 = (f32[8,512]{1,0:T(8,128)S(1)}, f32[8,512]{1,0:T(8,128)}, u32[]{:S(2)}) copy-start(f32[8,512]{1,0:T(8,128)} %get-tuple-element.105) | copy-start | bytes 49156
  397.9 38.7 %copy-start.6 = (bf16[128,32,128]{2,1,0:T(8,128)(2,1)}, bf16[128,32,128]{2,1,0:T(8,128)(2,1)S(1)}, u32[]{:S(2)}) copy-start(bf16[128,32,128]{2,1,0:T(8,128)(2,1)S(1)} %all-to-all-done.11.back_ref) | copy-start | bytes 3145732
  427.3 12.7 %all-to-all-start.13 = ((bf16[8,128,128]{2,1,0:T(8,128)(2,1)}), bf16[8,128,128]{2,1,0:T(8,128)(2,1)S(1)}, u32[]{:S(2)}, u32[]{:S(2)}) async-start(bf16[8,128,128]{2,1,0:T(8,128)(2,1)} %get-tuple-element.95), calls=%async_computation.13 | async-start | bytes 524288 | tf_op jit(solution)/shard_map/all_to_all | solution.py:824
  440.7 13.6 %copy-start.44 = (f32[1,768]{1,0:T(1,128)S(1)}, f32[1,768]{1,0:T(1,128)}, u32[]{:S(2)}) copy-start(f32[1,768]{1,0:T(1,128)} %get-tuple-element.99) | copy-start | bytes 9220
  450.7 16.6 %all-to-all-start.14 = ((bf16[8,128,384]{2,1,0:T(8,128)(2,1)}), bf16[8,128,384]{2,1,0:T(8,128)(2,1)S(1)}, u32[]{:S(2)}, u32[]{:S(2)}) async-start(bf16[8,128,384]{2,1,0:T(8,128)(2,1)} %bitcast.118), calls=%async_computation.14 | async-start | bytes 1572864 | tf_op jit(solution)/shard_map/all_to_all | solution.py:824
  467.4 14.2 %copy-start.8 = (bf16[8,128,384]{2,1,0:T(8,128)(2,1)}, bf16[8,128,384]{2,1,0:T(8,128)(2,1)S(1)}, u32[]{:S(2)}) copy-start(bf16[8,128,384]{2,1,0:T(8,128)(2,1)S(1)} %all-to-all-done.14.back_ref) | copy-start | bytes 2359300
  467.4 32.4 %all-to-all-start.15 = ((bf16[16,112,512]{2,1,0:T(8,128)(2,1)}), bf16[16,112,512]{2,1,0:T(8,128)(2,1)S(1)}, u32[]{:S(2)}, u32[]{:S(2)}) async-start(bf16[16,112,512]{2,1,0:T(8,128)(2,1)} %dense_grads.3), calls=%async_computation.15 | async-start | bytes 3670016 | tf_op jit(solution)/shard_map/all_to_all | solution.py:932
  492.1 23.5 %collective-permute-start.16 = (bf16[128,768]{1,0:T(8,128)(2,1)S(1)}, bf16[128,768]{1,0:T(8,128)(2,1)S(1)}, u32[]{:S(2)}, u32[]{:S(2)}) collective-permute-start(bf16[128,768]{1,0:T(8,128)(2,1)S(1)} %get-tuple-element.155), channel_id=1, source_target_pairs={{0,64},{64,0},{1,65},{65,1},{2,66},{66,2},{3,67},{67,3},{4,68},{68... | collective-permute-start | bytes 589832 | tf_op jit(solution)/shard_map/ppermute | solution.py:828
  494.2 43.0 %copy-start.1 = (bf16[2,1,128,768]{3,2,1,0:T(8,128)(2,1)S(1)}, bf16[2,1,128,768]{3,2,1,0:T(8,128)(2,1)}, u32[]{:S(2)}) copy-start(bf16[2,1,128,768]{3,2,1,0:T(8,128)(2,1)} %param.11) | copy-start | bytes 1179652
  500.0 2.8 collective-permute-start.18
  501.7 26.8 %collective-permute-start.17 = (bf16[128,768]{1,0:T(8,128)(2,1)S(1)}, bf16[128,768]{1,0:T(8,128)(2,1)S(1)}, u32[]{:S(2)}, u32[]{:S(2)}) collective-permute-start(bf16[128,768]{1,0:T(8,128)(2,1)S(1)} %get-tuple-element.153), channel_id=1, source_target_pairs={{0,64},{64,0},{1,65},{65,1},{2,66},{66,2},{3,67},{67,3},{4,68},{68... | collective-permute-start | bytes 589832 | tf_op jit(solution)/shard_map/ppermute | solution.py:828
  502.8 29.7 %copy-start.31 = (bf16[112,512]{1,0:T(8,128)(2,1)}, bf16[112,512]{1,0:T(8,128)(2,1)S(1)}, u32[]{:S(2)}) copy-start(bf16[112,512]{1,0:T(8,128)(2,1)S(1)} %collective-permute-done.18.refs_0_) | copy-start | bytes 344068
  502.8 19.0 %collective-permute-start.19 = (bf16[112,512]{1,0:T(8,128)(2,1)S(1)}, bf16[112,512]{1,0:T(8,128)(2,1)S(1)}, u32[]{:S(2)}, u32[]{:S(2)}) collective-permute-start(bf16[112,512]{1,0:T(8,128)(2,1)S(1)} %collective-permute-done.18.refs_0_), channel_id=1, source_target_pairs={{0,8},{8,16},{16,24},{24,0},{32,40},{40,48},{48,56},{56,32},{1,9},... | collective-permute-start | bytes 344072 | tf_op jit(solution)/shard_map/ppermute | solution.py:945
  507.6 17.3 %collective-permute-start.20 = (bf16[112,512]{1,0:T(8,128)(2,1)S(1)}, bf16[112,512]{1,0:T(8,128)(2,1)S(1)}, u32[]{:S(2)}, u32[]{:S(2)}) collective-permute-start(bf16[112,512]{1,0:T(8,128)(2,1)S(1)} %collective-permute-done.18.refs_0_), channel_id=1, source_target_pairs={{0,16},{8,24},{16,0},{24,8},{32,48},{40,56},{48,32},{56,40},{1,17}... | collective-permute-start | bytes 344072 | tf_op jit(solution)/shard_map/ppermute | solution.py:945
  513.9 11.5 %collective-permute-start.21 = (bf16[112,512]{1,0:T(8,128)(2,1)S(1)}, bf16[112,512]{1,0:T(8,128)(2,1)S(1)}, u32[]{:S(2)}, u32[]{:S(2)}) collective-permute-start(bf16[112,512]{1,0:T(8,128)(2,1)S(1)} %collective-permute-done.18.refs_0_), channel_id=1, source_target_pairs={{0,24},{8,0},{16,8},{24,16},{32,56},{40,32},{48,40},{56,48},{1,25}... | collective-permute-start | bytes 344072 | tf_op jit(solution)/shard_map/ppermute | solution.py:945
  516.4 12.9 %collective-permute-start.22 = (bf16[112,512]{1,0:T(8,128)(2,1)S(1)}, bf16[112,512]{1,0:T(8,128)(2,1)S(1)}, u32[]{:S(2)}, u32[]{:S(2)}) collective-permute-start(bf16[112,512]{1,0:T(8,128)(2,1)S(1)} %collective-permute-done.18.refs_0_), channel_id=1, source_target_pairs={{0,32},{8,40},{16,48},{24,56},{32,0},{40,8},{48,16},{56,24},{1,33}... | collective-permute-start | bytes 344072 | tf_op jit(solution)/shard_map/ppermute | solution.py:947
  521.8 10.6 %copy-start.32 = (bf16[112,512]{1,0:T(8,128)(2,1)}, bf16[112,512]{1,0:T(8,128)(2,1)S(1)}, u32[]{:S(2)}) copy-start(bf16[112,512]{1,0:T(8,128)(2,1)S(1)} %collective-permute-done.19.refs_1_) | copy-start | bytes 344068
  521.8 7.5 %collective-permute-start.23 = (bf16[112,512]{1,0:T(8,128)(2,1)S(1)}, bf16[112,512]{1,0:T(8,128)(2,1)S(1)}, u32[]{:S(2)}, u32[]{:S(2)}) collective-permute-start(bf16[112,512]{1,0:T(8,128)(2,1)S(1)} %collective-permute-done.19.refs_1_), channel_id=1, source_target_pairs={{0,32},{8,40},{16,48},{24,56},{32,0},{40,8},{48,16},{56,24},{1,33}... | collective-permute-start | bytes 344072 | tf_op jit(solution)/shard_map/ppermute | solution.py:947
  525.0 6.3 %collective-permute-start.24 = (bf16[112,512]{1,0:T(8,128)(2,1)S(1)}, bf16[112,512]{1,0:T(8,128)(2,1)S(1)}, u32[]{:S(2)}, u32[]{:S(2)}) collective-permute-start(bf16[112,512]{1,0:T(8,128)(2,1)S(1)} %collective-permute-done.20.refs_2_), channel_id=1, source_target_pairs={{0,32},{8,40},{16,48},{24,56},{32,0},{40,8},{48,16},{56,24},{1,33}... | collective-permute-start | bytes 344072 | tf_op jit(solution)/shard_map/ppermute | solution.py:947
  525.4 7.1 %collective-permute-start.25 = (bf16[112,512]{1,0:T(8,128)(2,1)S(1)}, bf16[112,512]{1,0:T(8,128)(2,1)S(1)}, u32[]{:S(2)}, u32[]{:S(2)}) collective-permute-start(bf16[112,512]{1,0:T(8,128)(2,1)S(1)} %collective-permute-done.21.refs_3_), channel_id=1, source_target_pairs={{0,32},{8,40},{16,48},{24,56},{32,0},{40,8},{48,16},{56,24},{1,33}... | collective-permute-start | bytes 344072 | tf_op jit(solution)/shard_map/ppermute | solution.py:947
  (29 other events, 127.5 us)
Sparse Core Ops, SparseCore 0:
  52.0 34.4 all-gather.6
  119.6 64.6 all-gather.8
  237.7 26.1 all-gather.14
  303.2 21.7 all-gather.16
  357.6 26.7 all-gather.10
  426.8 21.7 all-gather.12
